TPU v7x, 32 devices: a whole 2x2x4 slice. The times are simulated.
32 devices in a mesh: dp: 8 (over y, x, core), mp: 4 (over z).
Axes of the slice: x: 2, y: 2, z: 4, core: 2. Of those that a mesh axis runs over, the one named last changes fastest.
Arguments:
- tokens: float32 [8192, 1536], P(('dp', 'mp')), may hold values from -62 to 62
- attn_gain: float32 [1536], replicated, may hold values from 0.1 to 1.9
- w_query: float32 [1536, 1536], P('dp', 'mp'), may hold values from -0.15625 to 0.15625
- w_key: float32 [1536, 512], P('dp', 'mp'), may hold values from -0.15625 to 0.15625
- w_value: float32 [1536, 512], P('dp', 'mp'), may hold values from -0.15625 to 0.15625
- w_out: float32 [1536, 1536], P('mp', 'dp'), may hold values from -1.75 to 1.75
- moe_gain: float32 [1536], replicated, may hold values from 0.1 to 1.9
- w_router: float32 [1536, 16], P('dp'), may hold values from -0.109375 to 0.109375
- w_gate: float32 [16, 1536, 1024], P(None, 'dp', 'mp'), may hold values from -0.15625 to 0.15625
- w_up: float32 [16, 1536, 1024], P(None, 'dp', 'mp'), may hold values from -0.15625 to 0.15625
- w_down: float32 [16, 1024, 1536], P('dp', 'mp'), may hold values from -0.1875 to 0.1875
- seq_lengths: int32 [8, 3], P('dp'), may hold values from 1 to 512, 1024 in all within a row
- deal_order: int32 [8192], replicated, may hold values from 0 to 8191, as said below
- expert_ids: int32 [8192, 2], P('dp'), may hold values from 0 to 15, all different within a row; in each aligned block of 1024 rows (0 to 1023, 1024 to 2047, ...) at most 256 rows name the same one
- out_grad: float32 [8192, 1536], P(('dp', 'mp')), may hold values from -6 to 6
Outputs:
- block_out: float32 [8192, 1536], P(('dp', 'mp'))
- tokens_grad: float32 [8192, 1536], P(('dp', 'mp'))
- attn_gain_grad: float32 [1536], replicated
- w_query_grad: float32 [1536, 1536], P('dp', 'mp')
- w_key_grad: float32 [1536, 512], P('dp', 'mp')
- w_value_grad: float32 [1536, 512], P('dp', 'mp')
- w_out_grad: float32 [1536, 1536], P('mp', 'dp')
- moe_gain_grad: float32 [1536], replicated
- w_router_grad: float32 [1536, 16], P('dp')
- w_gate_grad: float32 [16, 1536, 1024], P(None, 'dp', 'mp')
- w_up_grad: float32 [16, 1536, 1024], P(None, 'dp', 'mp')
- w_down_grad: float32 [16, 1024, 1536], P('dp', 'mp')
Inputs may be any that keep to these rules, and one draw needn't show every extreme that they name: `seq_lengths`: each row holds 3 lengths summing to 1024, the largest exactly 512. `deal_order`: a permutation of all rows; each block of 1024 dealt rows takes exactly 32 rows from every aligned span of 256 initial rows. `expert_ids`: the two experts of a row differ; within each aligned block of 1024 rows no expert is named by more than 256 rows, and one is named by exactly 256 in some blocks.
All inputs are finite; a program needn't handle non-finite values.
Results may differ from a plain program's by a relative error of at most 0.017.
Values may be sent and summed in bfloat16 or wider, within the bound.
A program may use at most 256 MiB of HBM per device.

v0:
```python
import jax
import jax.numpy as jnp
from jax import lax
from jax.sharding import PartitionSpec as P

D = 1536
HD = 64
E = 16
CAP = 256


EPS = 1e-05


def full_rows(values):
    return lax.all_gather(values, "mp", axis=0, tiled=True)


def row_share(partial_value):
    return lax.psum_scatter(partial_value, "mp", scatter_dimension=0, tiled=True)


def norm_apply(values, gain):
    energy = jnp.mean(values * values, axis=1)
    scale = lax.rsqrt(energy + EPS)
    normed = values * scale[:, None] * gain[None, :]
    return (scale, normed.astype(jnp.bfloat16))


def norm_back(values, gain, scale, grad_normed):
    weighted = grad_normed * gain[None, :]
    inner = jnp.mean(weighted * values, axis=1)
    grad_in = scale[:, None] * weighted - values * (scale * scale * scale * inner)[:, None]
    gain_grad = jnp.sum(grad_normed * values * scale[:, None], axis=0)
    return (grad_in, gain_grad)


def deal_tables(deal_order, block):
    groups = lax.axis_size("dp")
    parts = lax.axis_size("mp")
    me_index = lax.axis_index("dp")
    part_index = lax.axis_index("mp")
    shard = block // parts
    piece = shard // groups
    source = (deal_order // block).reshape(groups, block)
    local = (deal_order % block).reshape(groups, block)
    holder = local // shard
    match = ((source == me_index) & (holder == part_index)).astype(jnp.int32)
    place = jnp.where(match > 0, jnp.cumsum(match, axis=1) - 1, piece)
    target = jnp.broadcast_to(jnp.arange(groups, dtype=jnp.int32)[:, None], (groups, block))
    send_table = (
        jnp.zeros((groups, piece), jnp.int32)
        .at[target, place]
        .set(local - part_index * shard, mode="drop")
    )
    send_piece = send_table.reshape(-1)
    mine_source = lax.dynamic_index_in_dim(source, me_index, 0, keepdims=False)
    mine_holder = lax.dynamic_index_in_dim(holder, me_index, 0, keepdims=False)
    anchor = mine_holder * groups + mine_source
    hits = (anchor[:, None] == jnp.arange(groups * parts, dtype=jnp.int32)[None, :]).astype(
        jnp.int32
    )
    rank = jnp.sum((jnp.cumsum(hits, axis=0) - hits) * hits, axis=1)
    recv_gathered = anchor * piece + rank
    counter = jnp.arange(block, dtype=jnp.int32)
    arrange = jnp.zeros((block,), jnp.int32).at[recv_gathered].set(counter)
    home_index = (
        jnp.zeros((shard,), jnp.int32).at[send_piece].set(jnp.arange(shard, dtype=jnp.int32))
    )
    stretch_rows = lax.dynamic_slice_in_dim(arrange, part_index * shard, shard, 0)
    return (send_piece, recv_gathered, arrange, home_index, stretch_rows)


def to_dealt(values, tables):
    moved = lax.all_to_all(values[tables[0]], "dp", split_axis=0, concat_axis=0, tiled=True)
    return full_rows(moved)[tables[1]]


def to_home(stretch, tables):
    moved = lax.all_to_all(
        stretch.astype(jnp.bfloat16), "dp", split_axis=0, concat_axis=0, tiled=True
    ).astype(stretch.dtype)
    return moved[tables[3]]


def segment_of(lengths, rows):
    ends = jnp.cumsum(lengths)
    places = jnp.arange(rows, dtype=jnp.int32)
    return jnp.sum((places[:, None] >= ends[None, :]).astype(jnp.int32), axis=1)


def visible(segment, start, finish):
    query_pos = jnp.arange(start, finish, dtype=jnp.int32)
    key_pos = jnp.arange(finish, dtype=jnp.int32)
    same = segment[start:finish][:, None] == segment[:finish][None, :]
    return same & (key_pos[None, :] <= query_pos[:, None])


def slot_table(expert_ids):
    flat = expert_ids.reshape(-1)
    hits = (flat[:, None] == jnp.arange(E, dtype=jnp.int32)[None, :]).astype(jnp.int32)
    rank = jnp.sum((jnp.cumsum(hits, axis=0) - hits) * hits, axis=1)
    return flat * CAP + rank


def block_scores(query, key, segment, start, block, heads_kv, share):
    finish = start + block
    query_rows = query[start:finish].reshape(block, heads_kv, share, HD)
    key_rows = key[:finish].reshape(finish, heads_kv, HD)
    scores = jnp.einsum(
        "qgsd,tgd->gsqt", query_rows, key_rows, preferred_element_type=jnp.float32
    ) * HD ** (-0.5)
    return (query_rows, key_rows, jnp.where(visible(segment, start, finish), scores, -1e30))


def attend_forward(query, key, value, segment):
    rows = query.shape[0]
    heads_kv = key.shape[1] // HD
    share = query.shape[1] // key.shape[1]
    block = min(512, rows)
    outputs, totals = ([], [])
    for start in range(0, rows, block):
        finish = start + block
        query_rows, key_rows, masked = block_scores(
            query, key, segment, start, block, heads_kv, share
        )
        value_rows = value[:finish].reshape(finish, heads_kv, HD)
        highest = jnp.max(masked, axis=-1, keepdims=True)
        raised = jnp.exp(masked - highest)
        total = jnp.sum(raised, axis=-1, keepdims=True)
        probs = (raised / total).astype(jnp.bfloat16)
        mixed = jnp.einsum("gsqt,tgd->qgsd", probs, value_rows, preferred_element_type=jnp.float32)
        outputs.append(mixed.reshape(block, -1))
        totals.append(highest + jnp.log(total))
    return (jnp.concatenate(outputs, axis=0), totals)


def attend_back(query, key, value, segment, grad_mix, totals):
    rows = query.shape[0]
    heads_kv = key.shape[1] // HD
    share = query.shape[1] // key.shape[1]
    block = min(512, rows)
    scale = HD ** (-0.5)
    grad_query = []
    grad_key = jnp.zeros((rows, heads_kv, HD), jnp.float32)
    grad_value = jnp.zeros((rows, heads_kv, HD), jnp.float32)
    for number, start in enumerate(range(0, rows, block)):
        finish = start + block
        query_rows, key_rows, masked = block_scores(
            query, key, segment, start, block, heads_kv, share
        )
        value_rows = value[:finish].reshape(finish, heads_kv, HD)
        probs = jnp.exp(masked - totals[number])
        grad_rows = grad_mix[start:finish].reshape(block, heads_kv, share, HD)
        grad_probs = jnp.einsum(
            "qgsd,tgd->gsqt", grad_rows, value_rows, preferred_element_type=jnp.float32
        )
        inner = jnp.sum(probs * grad_probs, axis=-1, keepdims=True)
        grad_scores = (probs * (grad_probs - inner)).astype(jnp.bfloat16)
        piece = (
            jnp.einsum("gsqt,tgd->qgsd", grad_scores, key_rows, preferred_element_type=jnp.float32)
            * scale
        )
        grad_query.append(piece.reshape(block, -1))
        grad_key = grad_key.at[:finish].add(
            jnp.einsum(
                "gsqt,qgsd->tgd", grad_scores, query_rows, preferred_element_type=jnp.float32
            )
            * scale
        )
        grad_value = grad_value.at[:finish].add(
            jnp.einsum(
                "gsqt,qgsd->tgd",
                probs.astype(jnp.bfloat16),
                grad_rows,
                preferred_element_type=jnp.float32,
            )
        )
    grad_query = jnp.concatenate(grad_query, axis=0).astype(jnp.bfloat16)
    return (
        grad_query,
        grad_key.reshape(rows, -1).astype(jnp.bfloat16),
        grad_value.reshape(rows, -1).astype(jnp.bfloat16),
    )


def swiglu_both(rows_in, grad_in, gate_w, up_w, down_w):
    gate_part = jnp.einsum("ecd,edf->ecf", rows_in, gate_w, preferred_element_type=jnp.float32)
    up_part = jnp.einsum("ecd,edf->ecf", rows_in, up_w, preferred_element_type=jnp.float32)
    sigma = jax.nn.sigmoid(gate_part)
    hidden = (gate_part * sigma * up_part).astype(jnp.bfloat16)
    each = jnp.einsum("ecf,efd->ecd", hidden, down_w, preferred_element_type=jnp.float32)
    grad_hidden = jnp.einsum("ecd,efd->ecf", grad_in, down_w, preferred_element_type=jnp.float32)
    grad_gate = (grad_hidden * up_part * sigma * (1.0 + gate_part * (1.0 - sigma))).astype(
        jnp.bfloat16
    )
    grad_up = (grad_hidden * gate_part * sigma).astype(jnp.bfloat16)
    gate_grad = jnp.einsum("ecd,ecf->edf", rows_in, grad_gate, preferred_element_type=jnp.float32)
    up_grad = jnp.einsum("ecd,ecf->edf", rows_in, grad_up, preferred_element_type=jnp.float32)
    down_grad = jnp.einsum("ecf,ecd->efd", hidden, grad_in, preferred_element_type=jnp.float32)
    back_slots = jnp.einsum("ecf,edf->ecd", grad_gate, gate_w, preferred_element_type=jnp.float32)
    back_slots = back_slots + jnp.einsum(
        "ecf,edf->ecd", grad_up, up_w, preferred_element_type=jnp.float32
    )
    return (each, back_slots, gate_grad, up_grad, down_grad)


def experts_blocked(second_full, grad_full, owner, slot_gate, gate_w, up_w, down_w):
    rows = second_full.shape[0]
    stride = E // 4
    width = stride * CAP
    mixed = jnp.zeros((rows, D), jnp.float32)
    grad_mixed = jnp.zeros((rows, D), jnp.float32)
    dots, gate_grads, up_grads, down_grads = ([], [], [], [])
    for part in range(4):
        lead = part * stride
        owners = owner[part * width : (part + 1) * width]
        gates_here = slot_gate[part * width : (part + 1) * width]
        buffer = second_full[owners].reshape(stride, CAP, D)
        grad_slots = grad_full[owners].astype(jnp.float32)
        grad_each = (gates_here[:, None] * grad_slots).astype(jnp.bfloat16).reshape(stride, CAP, D)
        each, back_slots, gate_grad, up_grad, down_grad = swiglu_both(
            buffer,
            grad_each,
            gate_w[lead : lead + stride],
            up_w[lead : lead + stride],
            down_w[lead : lead + stride],
        )
        each = each.reshape(width, D)
        mixed = mixed.at[owners].add(each * gates_here[:, None])
        grad_mixed = grad_mixed.at[owners].add(back_slots.reshape(width, D))
        dots.append(jnp.sum(grad_slots * each, axis=1))
        gate_grads.append(gate_grad)
        up_grads.append(up_grad)
        down_grads.append(down_grad)
    return (
        mixed,
        grad_mixed,
        jnp.concatenate(dots, axis=0),
        jnp.concatenate(gate_grads, axis=0),
        jnp.concatenate(up_grads, axis=0),
        jnp.concatenate(down_grads, axis=0),
    )


def body(
    tokens,
    attn_gain,
    w_query,
    w_key,
    w_value,
    w_out,
    moe_gain,
    w_router,
    w_gate,
    w_up,
    w_down,
    seq_lengths,
    deal_order,
    expert_ids,
    out_grad,
):
    rows = tokens.shape[0] * lax.axis_size("mp")
    low_type = jnp.bfloat16
    query_w, key_w, value_w, out_w, router_w, gate_w, up_w, down_w = (
        lax.all_gather(w_query.astype(low_type), "dp", axis=0, tiled=True),
        lax.all_gather(w_key.astype(low_type), "dp", axis=0, tiled=True),
        lax.all_gather(w_value.astype(low_type), "dp", axis=0, tiled=True),
        lax.all_gather(w_out.astype(low_type), "dp", axis=1, tiled=True),
        lax.all_gather(w_router.astype(low_type), "dp", axis=0, tiled=True),
        lax.all_gather(w_gate.astype(low_type), "dp", axis=1, tiled=True),
        lax.all_gather(w_up.astype(low_type), "dp", axis=1, tiled=True),
        lax.all_gather(w_down.astype(low_type), "dp", axis=0, tiled=True),
    )
    tables = deal_tables(deal_order, rows)
    segment = segment_of(seq_lengths[0], rows)
    scale_one, normed_one = norm_apply(tokens, attn_gain)
    first_full = full_rows(normed_one)
    query = jnp.dot(first_full, query_w, preferred_element_type=jnp.float32).astype(low_type)
    key = jnp.dot(first_full, key_w, preferred_element_type=jnp.float32).astype(low_type)
    value = jnp.dot(first_full, value_w, preferred_element_type=jnp.float32).astype(low_type)
    mix, totals = attend_forward(query, key, value, segment)
    mix = mix.astype(low_type)
    middle = tokens + row_share(jnp.dot(mix, out_w, preferred_element_type=jnp.float32))
    scale_two, normed_two = norm_apply(middle, moe_gain)
    second_full = to_dealt(normed_two, tables)
    grad_full = to_dealt(out_grad.astype(low_type), tables)
    logits = jnp.dot(second_full, router_w, preferred_element_type=jnp.float32)
    picker = (expert_ids[:, :, None] == jnp.arange(E, dtype=jnp.int32)[None, None, :]).astype(
        jnp.float32
    )
    gates = jax.nn.softmax(jnp.sum(picker * logits[:, None, :], axis=2), axis=1)
    slots = slot_table(expert_ids)
    owner = (
        jnp.zeros((E * CAP,), jnp.int32).at[slots].set(jnp.arange(2 * rows, dtype=jnp.int32) // 2)
    )
    slot_gate = jnp.zeros((E * CAP,), jnp.float32).at[slots].set(gates.reshape(-1))
    mixed, grad_mixed, dots, grad_gate_all, grad_up_all, grad_down_all = experts_blocked(
        second_full, grad_full, owner, slot_gate, gate_w, up_w, down_w
    )
    block_out = middle + to_home(row_share(mixed[tables[2]]), tables)
    grad_gates = lax.psum(dots[slots].reshape(rows, 2), "mp")
    grad_chosen = gates * (grad_gates - jnp.sum(gates * grad_gates, axis=1, keepdims=True))
    grad_logits = jnp.sum(picker * grad_chosen[:, :, None], axis=1).astype(low_type)
    grad_router = jnp.einsum(
        "td,te->de", second_full, grad_logits, preferred_element_type=jnp.float32
    )
    grad_stretch = row_share(grad_mixed[tables[2]])
    grad_stretch = grad_stretch + jnp.einsum(
        "te,de->td", grad_logits[tables[4]], router_w, preferred_element_type=jnp.float32
    )
    grad_normed_two = to_home(grad_stretch, tables)
    grad_middle_norm, grad_moe_gain = norm_back(middle, moe_gain, scale_two, grad_normed_two)
    grad_middle = out_grad + grad_middle_norm
    grad_attn_full = full_rows(grad_middle.astype(low_type))
    grad_mix = jnp.einsum(
        "td,hd->th", grad_attn_full, out_w, preferred_element_type=jnp.float32
    ).astype(low_type)
    grad_out_w = jnp.einsum("th,td->hd", mix, grad_attn_full, preferred_element_type=jnp.float32)
    grad_query, grad_key, grad_value = attend_back(query, key, value, segment, grad_mix, totals)
    grad_first = jnp.einsum("th,dh->td", grad_query, query_w, preferred_element_type=jnp.float32)
    grad_first = grad_first + jnp.einsum(
        "th,dh->td", grad_key, key_w, preferred_element_type=jnp.float32
    )
    grad_first = grad_first + jnp.einsum(
        "th,dh->td", grad_value, value_w, preferred_element_type=jnp.float32
    )
    grad_query_w = jnp.einsum(
        "td,th->dh", first_full, grad_query, preferred_element_type=jnp.float32
    )
    grad_key_w = jnp.einsum("td,th->dh", first_full, grad_key, preferred_element_type=jnp.float32)
    grad_value_w = jnp.einsum(
        "td,th->dh", first_full, grad_value, preferred_element_type=jnp.float32
    )
    grad_tokens_norm, grad_attn_gain = norm_back(
        tokens, attn_gain, scale_one, row_share(grad_first)
    )
    tokens_grad = grad_middle + grad_tokens_norm
    attn_gain_sum, moe_gain_sum = lax.psum((grad_attn_gain, grad_moe_gain), ("dp", "mp"))
    query_sum, key_sum, value_sum, out_sum, router_sum, gate_sum, up_sum, down_sum = (
        lax.psum_scatter(
            grad_query_w.astype(jnp.bfloat16), "dp", scatter_dimension=0, tiled=True
        ).astype(jnp.float32),
        lax.psum_scatter(
            grad_key_w.astype(jnp.bfloat16), "dp", scatter_dimension=0, tiled=True
        ).astype(jnp.float32),
        lax.psum_scatter(
            grad_value_w.astype(jnp.bfloat16), "dp", scatter_dimension=0, tiled=True
        ).astype(jnp.float32),
        lax.psum_scatter(
            grad_out_w.astype(jnp.bfloat16), "dp", scatter_dimension=1, tiled=True
        ).astype(jnp.float32),
        lax.psum_scatter(
            grad_router.astype(jnp.bfloat16), "dp", scatter_dimension=0, tiled=True
        ).astype(jnp.float32),
        lax.psum_scatter(
            grad_gate_all.astype(jnp.bfloat16), "dp", scatter_dimension=1, tiled=True
        ).astype(jnp.float32),
        lax.psum_scatter(
            grad_up_all.astype(jnp.bfloat16), "dp", scatter_dimension=1, tiled=True
        ).astype(jnp.float32),
        lax.psum_scatter(
            grad_down_all.astype(jnp.bfloat16), "dp", scatter_dimension=0, tiled=True
        ).astype(jnp.float32),
    )
    return (
        block_out,
        tokens_grad,
        attn_gain_sum,
        query_sum,
        key_sum,
        value_sum,
        out_sum,
        moe_gain_sum,
        router_sum,
        gate_sum,
        up_sum,
        down_sum,
    )


def solution(mesh):
    return jax.shard_map(
        body,
        mesh=mesh,
        in_specs=(
            P(("dp", "mp"), None),
            P(),
            P("dp", "mp"),
            P("dp", "mp"),
            P("dp", "mp"),
            P("mp", "dp"),
            P(),
            P("dp", None),
            P(None, "dp", "mp"),
            P(None, "dp", "mp"),
            P("dp", "mp", None),
            P("dp", None),
            P(),
            P("dp", None),
            P(("dp", "mp"), None),
        ),
        out_specs=(
            P(("dp", "mp"), None),
            P(("dp", "mp"), None),
            P(),
            P("dp", "mp"),
            P("dp", "mp"),
            P("dp", "mp"),
            P("mp", "dp"),
            P(),
            P("dp", None),
            P(None, "dp", "mp"),
            P(None, "dp", "mp"),
            P("dp", "mp", None),
        ),
        check_vma=False,
    )
```

profile of v0, /device:TPU:0, one launch (start us, length us, event | category | flops | bytes accessed | tf_op | source)
XLA Modules:
  0.0 1739.2 jit_solution(6746271448315348290)
XLA Ops:
  15.3 12.1 all_gather.37
  27.4 9.5 all_gather.38
  38.1 40.7 %all-gather.11.cloned.1.call-done = bf16[1024,1536]{1,0:T(8,128)(2,1)} async-done(((bf16[256,1536]{1,0:T(8,128)(2,1)}), bf16[1024,1536]{1,0:T(8,128)(2,1)}) %all-gather.11.cloned.1.call-update) | async-done | bytes 3145744 | tf_op jit(solution)/shard_map/all_gather | solution.py:16
  85.3 18.7 %all-gather.13.cloned.1.call-done = bf16[1536,384]{1,0:T(8,128)(2,1)} async-done(((bf16[192,384]{1,0:T(8,128)(2,1)}), bf16[1536,384]{1,0:T(8,128)(2,1)}) %all-gather.13.cloned.1.call-update) | async-done | bytes 1179664 | tf_op jit(solution)/shard_map/all_gather | solution.py:266
  121.5 9.2 all-gather.15.cloned.1.call-done
  130.7 5.7 fusion.108
  140.5 30.4 %scatter_custom_fusion.12 = s32[256]{0:T(256)S(1)} fusion(s32[8192]{0:T(1024)S(1)} %get-tuple-element.145, s32[8192]{0:T(1024)S(1)} %get-tuple-element.144, s32[]{:T(128)} %constant.227.clone.1), kind=kCustom, calls=%fused_computation.334 | custom fusion | bytes 1028
  172.3 15.6 all_to_all.42
  188.0 59.3 %reduce-scatter.15.cloned.1.call-done = f32[256,1536]{1,0:T(8,128)} async-done(((f32[1024,1536]{1,0:T(8,128)}), f32[256,1536]{1,0:T(8,128)}) %reduce-scatter.15.cloned.1.call-update) | async-done | bytes 1572880 | tf_op jit(solution)/shard_map/reduce_scatter | solution.py:20
  251.6 16.1 all_to_all.43
  276.9 8.3 all-gather
  285.4 9.0 reduce-window.43
  305.2 8.5 scatter_custom_fusion
  314.9 9.0 gather_fusion.9
  323.9 5.6 gather_fusion.12
  329.5 5.6 gather_fusion.11
  335.1 5.5 gather_fusion.10
  340.7 5.5 gather_fusion.13
  346.2 30.2 %all-gather.17.cloned.1.call-done = bf16[1024,1536]{1,0:T(8,128)(2,1)} async-done(((bf16[256,1536]{1,0:T(8,128)(2,1)}), bf16[1024,1536]{1,0:T(8,128)(2,1)}) %all-gather.17.cloned.1.call-update) | async-done | bytes 3145744 | tf_op jit(solution)/shard_map/all_gather | solution.py:16
  376.4 9.0 gather_fusion.1
  385.4 5.7 gather_fusion.5
  391.1 5.6 gather_fusion.4
  396.7 5.6 gather_fusion.3
  402.3 5.7 gather_fusion.2
  409.1 40.6 %all-gather.19.cloned.1.call-done = bf16[16,1536,256]{2,1,0:T(8,128)(2,1)} async-done(((bf16[16,192,256]{2,1,0:T(8,128)(2,1)}), bf16[16,1536,256]{2,1,0:T(8,128)(2,1)}) %all-gather.19.cloned.1.call-update) | async-done | bytes 12582928 | tf_op jit(solution)/shard_map/all_gather | solution.py:271
  454.5 69.3 %all-gather.21.cloned.1.call-done = bf16[16,1536,256]{2,1,0:T(8,128)(2,1)} async-done(((bf16[16,192,256]{2,1,0:T(8,128)(2,1)}), bf16[16,1536,256]{2,1,0:T(8,128)(2,1)}) %all-gather.21.cloned.1.call-update) | async-done | bytes 12582928 | tf_op jit(solution)/shard_map/all_gather | solution.py:272
  523.7 5.4 multiply_convert_fusion.13
  529.2 68.6 %all-gather.23.cloned.1.call-done = bf16[16,256,1536]{2,1,0:T(8,128)(2,1)} async-done(((bf16[2,256,1536]{2,1,0:T(8,128)(2,1)}), bf16[16,256,1536]{2,1,0:T(8,128)(2,1)}) %all-gather.23.cloned.1.call-update) | async-done | bytes 12582928 | tf_op jit(solution)/shard_map/all_gather | solution.py:273
  597.8 5.9 fusion.6
  637.0 11.8 gather_fusion.15
  649.5 12.0 psum.21
  662.6 8.1 scatter_custom_fusion.1
  670.7 6.0 bitcast_multiply_fusion.2
  688.3 15.1 scatter_custom_fusion.2
  703.4 17.1 scatter_fusion
  720.5 17.2 scatter_fusion.1
  737.8 17.1 scatter_fusion.2
  754.9 10.5 gather_fusion.6
  775.6 5.7 convolution_add_fusion.3
  781.3 15.1 scatter_custom_fusion.8
  803.7 5.7 convolution_add_fusion.2
  809.5 17.7 %scatter_fusion.3 = f32[1024,1536]{1,0:T(8,128)} fusion(f32[1024,1536]{1,0:T(8,128)} %scatter_custom_fusion.8, s32[1024]{0:T(1024)S(1)} %copy-done.114, f32[1024,1536]{1,0:T(8,128)} %bitcast.362), kind=kCustom, calls=%fused_computation.27 | custom fusion | flops 1572864 | bytes 18878464 | tf_op jit(solution)/shard_map/scatter-add | solution.py:231
  834.4 5.7 convolution_add_fusion.1
  840.2 17.3 scatter_fusion.4
  864.7 5.7 convolution_add_fusion
  870.4 17.1 scatter_fusion.5
  887.5 10.5 gather_fusion.14
  908.1 97.7 %reduce-scatter.19.cloned.1.call-done = f32[256,1536]{1,0:T(8,128)} async-done(((f32[1024,1536]{1,0:T(8,128)}), f32[256,1536]{1,0:T(8,128)}) %reduce-scatter.19.cloned.1.call-update) | async-done | bytes 1572880 | tf_op jit(solution)/shard_map/reduce_scatter | solution.py:20
  1015.0 9.7 all-to-all-done.3
  1035.8 5.0 convolution_convert_fusion
  1049.6 46.9 %all-gather.27.cloned.1.call-done = bf16[1024,1536]{1,0:T(8,128)(2,1)} async-done(((bf16[256,1536]{1,0:T(8,128)(2,1)}), bf16[1024,1536]{1,0:T(8,128)(2,1)}) %all-gather.27.cloned.1.call-update) | async-done | bytes 3145744 | tf_op jit(solution)/shard_map/all_gather | solution.py:16
  1108.5 5.9 fusion
  1124.0 9.9 fusion.2
  1138.4 10.7 pad_maximum_fusion.2
  1158.1 5.5 pad_maximum_fusion
  1172.7 5.5 pad_maximum_fusion.1
  1178.3 5.1 convolution_convert_fusion.12
  1207.0 94.4 %reduce-scatter.35.cloned.1.call-done = bf16[2,256,1536]{2,1,0:T(8,128)(2,1)} async-done(((bf16[16,256,1536]{2,1,0:T(8,128)(2,1)}), bf16[2,256,1536]{2,1,0:T(8,128)(2,1)}) %reduce-scatter.35.cloned.1.call-update) | async-done | bytes 1572880 | tf_op jit(solution)/shard_map/reduce_scatter | solution.py:362
  1304.9 92.3 %reduce-scatter.31.cloned.1.call-done = bf16[16,192,256]{2,1,0:T(8,128)(2,1)} async-done(((bf16[16,1536,256]{2,1,0:T(8,128)(2,1)}), bf16[16,192,256]{2,1,0:T(8,128)(2,1)}) %reduce-scatter.31.cloned.1.call-update) | async-done | bytes 1572880 | tf_op jit(solution)/shard_map/reduce_scatter | solution.py:356
  1400.6 92.4 %reduce-scatter.33.cloned.1.call-done = bf16[16,192,256]{2,1,0:T(8,128)(2,1)} async-done(((bf16[16,1536,256]{2,1,0:T(8,128)(2,1)}), bf16[16,192,256]{2,1,0:T(8,128)(2,1)}) %reduce-scatter.33.cloned.1.call-update) | async-done | bytes 1572880 | tf_op jit(solution)/shard_map/reduce_scatter | solution.py:359
  1496.4 36.6 %reduce-scatter.29.cloned.1.call-done = bf16[384,192]{0,1:T(8,128)(2,1)} async-done(((bf16[384,1536]{0,1:T(8,128)(2,1)}), bf16[384,192]{0,1:T(8,128)(2,1)}) %reduce-scatter.29.cloned.1.call-update) | async-done | bytes 147472 | tf_op jit(solution)/shard_map/reduce_scatter | solution.py:350
  1534.7 38.6 %reduce-scatter.23.cloned.1.call-done = bf16[192,384]{1,0:T(8,128)(2,1)} async-done(((bf16[1536,384]{1,0:T(8,128)(2,1)}), bf16[192,384]{1,0:T(8,128)(2,1)}) %reduce-scatter.23.cloned.1.call-update) | async-done | bytes 147472 | tf_op jit(solution)/shard_map/reduce_scatter | solution.py:341
  1574.9 111.4 %reduce-scatter.21.cloned.1.call-done = f32[256,1536]{1,0:T(8,128)} async-done(((f32[1024,1536]{1,0:T(8,128)}), f32[256,1536]{1,0:T(8,128)}) %reduce-scatter.21.cloned.1.call-update) | async-done | bytes 1572880 | tf_op jit(solution)/shard_map/reduce_scatter | solution.py:20
  1688.2 40.9 %all-reduce.2 = (f32[1536]{0:T(1024)}, f32[1536]{0:T(1024)}) all-reduce(f32[1536]{0:T(1024)S(1)} %get-tuple-element.78, f32[1536]{0:T(1024)S(1)} %get-tuple-element.76), channel_id=1, replica_groups=mesh['dp'=8,'mp'=4] {'dp','mp'}, use_global_device_ids=true, to_apply=%region_48.49 | all-reduce | flops 3072 | bytes 24576 | tf_op jit(solution)/shard_map/psum | solution.py:339
  (555 shorter events, 272.0 us)
Async XLA Ops:
  7.2 71.6 %all-gather.11.cloned.1.call-start = ((), (), s32[]{:S(2)}) async-start(), calls=%async_computation.16 | async-start | bytes 3932160 | tf_op jit(solution)/shard_map/all_gather | solution.py:16
  12.5 91.6 %all-gather.13.cloned.1.call-start = ((), (), s32[]{:S(2)}) async-start(), calls=%async_computation.17 | async-start | bytes 1327104 | tf_op jit(solution)/shard_map/all_gather | solution.py:266
  13.3 117.4 %all-gather.15.cloned.1.call-start = ((), (), s32[]{:S(2)}) async-start(), calls=%async_computation.18 | async-start | bytes 1327104 | tf_op jit(solution)/shard_map/all_gather | solution.py:269
  14.0 233.3 %reduce-scatter.15.cloned.1.call-start = ((), (), s32[]{:S(2)}) async-start(), calls=%async_computation.19 | async-start | bytes 7864320 | tf_op jit(solution)/shard_map/reduce_scatter | solution.py:20
  36.9 47.1 %copy-start.39 = (bf16[1536,128]{1,0:T(8,128)(2,1)}, bf16[1536,128]{1,0:T(8,128)(2,1)S(1)}, u32[]{:S(2)}) copy-start(bf16[1536,128]{1,0:T(8,128)(2,1)S(1)} %all_gather.38) | copy-start | bytes 1179652
  85.3 21.5 %copy-start.56 = (pred[512,512]{0,1:T(8,128)(4,1)S(1)}, pred[512,512]{0,1:T(8,128)(4,1)}, u32[]{:S(2)}) copy-start(pred[512,512]{0,1:T(8,128)(4,1)} %fusion.106) | copy-start | bytes 786436
  85.3 21.5 %copy-start.78 = (bf16[512,128]{0,1:T(8,128)(2,1)S(1)}, bf16[512,128]{0,1:T(8,128)(2,1)}, u32[]{:S(2)}) copy-start(bf16[512,128]{0,1:T(8,128)(2,1)} %slice.297) | copy-start | bytes 393220
  111.9 18.8 %copy-start.87 = (bf16[2,64,3,512]{3,1,2,0:T(8,128)(2,1)}, bf16[2,64,3,512]{3,1,2,0:T(8,128)(2,1)S(1)}, u32[]{:S(2)}) copy-start(bf16[2,64,3,512]{3,1,2,0:T(8,128)(2,1)S(1)} %fusion.84) | copy-start | bytes 1179652
  121.5 14.9 copy-start.88
  136.4 178.5 %all-gather.25.cloned.1.call-start = ((), (), s32[]{:S(2)}) async-start(), calls=%async_computation.25 | async-start | bytes 3932160 | tf_op jit(solution)/shard_map/all_gather | solution.py:16
  171.0 76.3 %copy-start.7 = (f32[256,1536]{1,0:T(8,128)S(1)}, f32[256,1536]{1,0:T(8,128)}, u32[]{:S(2)}) copy-start(f32[256,1536]{1,0:T(8,128)} %param.27) | copy-start | bytes 4718596
  187.9 62.2 %copy-start.100 = (f32[1536]{0:T(1024)S(1)}, f32[1536]{0:T(1024)}, u32[]{:S(2)}) copy-start(f32[1536]{0:T(1024)} %param.33) | copy-start | bytes 18436
  187.9 188.5 %all-gather.17.cloned.1.call-start = ((), (), s32[]{:S(2)}) async-start(), calls=%async_computation.20 | async-start | bytes 3932160 | tf_op jit(solution)/shard_map/all_gather | solution.py:16
  267.8 181.9 %all-gather.19.cloned.1.call-start = ((), (), s32[]{:S(2)}) async-start(), calls=%async_computation.21 | async-start | bytes 14155776 | tf_op jit(solution)/shard_map/all_gather | solution.py:271
  271.2 252.5 %all-gather.21.cloned.1.call-start = ((), (), s32[]{:S(2)}) async-start(), calls=%async_computation.22 | async-start | bytes 14155776 | tf_op jit(solution)/shard_map/all_gather | solution.py:272
  272.7 325.1 %all-gather.23.cloned.1.call-start = ((), (), s32[]{:S(2)}) async-start(), calls=%async_computation.23 | async-start | bytes 14155776 | tf_op jit(solution)/shard_map/all_gather | solution.py:273
  276.0 624.5 %reduce-scatter.17.cloned.1.call-start = ((), (), s32[]{:S(2)}) async-start(), calls=%async_computation.24 | async-start | bytes 7864320 | tf_op jit(solution)/shard_map/reduce_scatter | solution.py:20
  285.3 122.7 %copy-start.85 = (bf16[1536,16]{0,1:T(8,128)(2,1)}, bf16[1536,16]{0,1:T(8,128)(2,1)S(1)}, u32[]{:S(2)}) copy-start(bf16[1536,16]{0,1:T(8,128)(2,1)S(1)} %reshape.1048) | copy-start | bytes 147460
  305.0 9.9 copy-start.115
  385.4 22.7 %copy-start = (bf16[1024,1536]{1,0:T(8,128)(2,1)}, bf16[1024,1536]{1,0:T(8,128)(2,1)S(1)}, u32[]{:S(2)}) copy-start(bf16[1024,1536]{1,0:T(8,128)(2,1)S(1)} %gather_fusion.1) | copy-start | bytes 9437188
  523.7 74.1 %copy-start.9 = (bf16[1024,1536]{1,0:T(8,128)(2,1)S(1)}, bf16[1024,1536]{1,0:T(8,128)(2,1)}, u32[]{:S(2)}) copy-start(bf16[1024,1536]{1,0:T(8,128)(2,1)} %gather_fusion.10) | copy-start | bytes 9437188
  603.7 7.8 slice-start.11
  603.7 7.8 slice-start.12
  606.8 9.1 slice-start.14
  606.8 9.7 slice-start.15
  662.1 14.6 copy-start.103
  688.3 15.1 copy-start.114
  703.4 17.1 copy-start.113
  720.5 17.3 copy-start.112
  737.8 17.1 copy-start.111
  765.4 240.4 %reduce-scatter.19.cloned.1.call-start = ((), (), s32[]{:S(2)}) async-start(), calls=%async_computation.26 | async-start | bytes 7864320 | tf_op jit(solution)/shard_map/reduce_scatter | solution.py:20
  765.7 30.7 %copy-start.122 = (f32[4,256]{1,0:T(4,128)}, f32[4,256]{1,0:T(4,128)S(1)}, u32[]{:S(2)}) copy-start(f32[4,256]{1,0:T(4,128)S(1)} %slice.255) | copy-start | bytes 12292
  781.3 15.1 copy-start.13
  809.5 17.7 %copy-start.16 = (bf16[1024,1536]{1,0:T(8,128)(2,1)S(1)}, bf16[1024,1536]{1,0:T(8,128)(2,1)}, u32[]{:S(2)}) copy-start(bf16[1024,1536]{1,0:T(8,128)(2,1)} %gather_fusion.12) | copy-start | bytes 9437188
  840.2 17.4 copy-start.19
  898.0 9.0 copy-start.104
  898.0 9.0 copy-start.106
  898.0 9.0 copy-start.124
  898.0 9.0 copy-start.96
  898.0 107.7 %copy-start.86 = (bf16[1536,16]{0,1:T(8,128)(2,1)S(1)}, bf16[1536,16]{0,1:T(8,128)(2,1)}, u32[]{:S(2)}) copy-start(bf16[1536,16]{0,1:T(8,128)(2,1)} %copy-done.85) | copy-start | bytes 147460
  903.4 105.0 %all-to-all-start.1 = ((bf16[8,32,1536]{2,1,0:T(8,128)(2,1)}), bf16[8,32,1536]{2,1,0:T(8,128)(2,1)S(1)}, u32[]{:S(2)}, u32[]{:S(2)}) async-start(bf16[8,32,1536]{2,1,0:T(8,128)(2,1)} %bitcast.47), calls=%async_computation.3 | async-start | bytes 1572864 | tf_op jit(solution)/shard_map/all_to_all | solution.py:80
  1008.4 16.2 all-to-all-start.3
  1012.1 84.5 %all-gather.27.cloned.1.call-start = ((), (), s32[]{:S(2)}) async-start(), calls=%async_computation.27 | async-start | bytes 3932160 | tf_op jit(solution)/shard_map/all_gather | solution.py:16
  1034.1 167.9 %reduce-scatter.37.cloned.1.call-start = ((), (), s32[]{:S(2)}) async-start(), calls=%async_computation.36 | async-start | bytes 442368
  1046.4 50.1 %copy-start.81 = (bf16[384,1536]{0,1:T(8,128)(2,1)S(1)}, bf16[384,1536]{0,1:T(8,128)(2,1)}, u32[]{:S(2)}) copy-start(bf16[384,1536]{0,1:T(8,128)(2,1)} %all-gather.15.cloned.1.call-done) | copy-start | bytes 3538948
  1049.2 154.4 %reduce-scatter.27.cloned.1.call-start = ((), (), s32[]{:S(2)}) async-start(), calls=%async_computation.31 | async-start | bytes 442368 | tf_op jit(solution)/shard_map/reduce_scatter | solution.py:347
  1096.5 11.9 slice-start
  1096.5 11.9 slice-start.1
  1104.0 12.5 slice-start.3
  1108.5 8.0 slice-start.4
  1123.8 81.8 %reduce-scatter.25.cloned.1.call-start = ((), (), s32[]{:S(2)}) async-start(), calls=%async_computation.30 | async-start | bytes 442368 | tf_op jit(solution)/shard_map/reduce_scatter | solution.py:344
  1124.0 9.9 copy-start.38
  1124.0 9.9 copy-start.82
  1138.3 163.1 %reduce-scatter.35.cloned.1.call-start = ((), (), s32[]{:S(2)}) async-start(), calls=%async_computation.35 | async-start | bytes 14155776 | tf_op jit(solution)/shard_map/reduce_scatter | solution.py:362
  1149.1 248.1 %reduce-scatter.31.cloned.1.call-start = ((), (), s32[]{:S(2)}) async-start(), calls=%async_computation.33 | async-start | bytes 14155776 | tf_op jit(solution)/shard_map/reduce_scatter | solution.py:356
  1163.6 329.4 %reduce-scatter.33.cloned.1.call-start = ((), (), s32[]{:S(2)}) async-start(), calls=%async_computation.34 | async-start | bytes 14155776 | tf_op jit(solution)/shard_map/reduce_scatter | solution.py:359
  1178.2 354.8 %reduce-scatter.29.cloned.1.call-start = ((), (), s32[]{:S(2)}) async-start(), calls=%async_computation.32 | async-start | bytes 1327104 | tf_op jit(solution)/shard_map/reduce_scatter | solution.py:350
  1183.4 389.8 %reduce-scatter.23.cloned.1.call-start = ((), (), s32[]{:S(2)}) async-start(), calls=%async_computation.29 | async-start | bytes 1327104 | tf_op jit(solution)/shard_map/reduce_scatter | solution.py:341
  1194.0 492.3 %reduce-scatter.21.cloned.1.call-start = ((), (), s32[]{:S(2)}) async-start(), calls=%async_computation.28 | async-start | bytes 7864320 | tf_op jit(solution)/shard_map/reduce_scatter | solution.py:20
  1400.6 285.7 %copy-start.8 = (f32[256,1536]{1,0:T(8,128)S(1)}, f32[256,1536]{1,0:T(8,128)}, u32[]{:S(2)}) copy-start(f32[256,1536]{1,0:T(8,128)} %param.27) | copy-start | bytes 4718596
  1400.6 285.7 %copy-start.102 = (f32[1536]{0:T(1024)S(1)}, f32[1536]{0:T(1024)}, u32[]{:S(2)}) copy-start(f32[1536]{0:T(1024)} %param.28) | copy-start | bytes 18436
  1400.6 285.7 %copy-start.117 = (f32[256]{0:T(256)S(1)}, f32[256]{0:T(256)}, u32[]{:S(2)}) copy-start(f32[256]{0:T(256)} %copy-done.116) | copy-start | bytes 3076
  1496.4 191.8 %copy-start.129 = (f32[256]{0:T(256)S(1)}, f32[256]{0:T(256)}, u32[]{:S(2)}) copy-start(f32[256]{0:T(256)} %copy-done.128) | copy-start | bytes 3076
  1496.4 232.7 %copy-start.35 = (f32[256,1536]{1,0:T(8,128)S(1)}, f32[256,1536]{1,0:T(8,128)}, u32[]{:S(2)}) copy-start(f32[256,1536]{1,0:T(8,128)} %get-tuple-element.83) | copy-start | bytes 4718596
  (113 other events, 386.1 us)
Sparse Core Ops, SparseCore 0:
  12.6 66.1 all-gather.10
  81.3 22.6 all-gather.12
  106.5 24.1 all-gather.14
  136.5 110.7 reduce-scatter.14
  248.7 64.0 all-gather.24
  314.2 62.1 all-gather.16
  378.9 70.7 all-gather.18
  451.6 72.1 all-gather.20
  525.6 72.1 all-gather.22
  765.6 107.9 reduce-scatter.16
  898.1 107.6 reduce-scatter.18
  1034.3 62.2 all-gather.26
  1099.6 32.4 reduce-scatter.36
  1135.0 33.7 reduce-scatter.26
  1171.7 33.8 reduce-scatter.24
  1209.0 92.4 reduce-scatter.34
  1304.8 92.3 reduce-scatter.30
  1400.5 92.3 reduce-scatter.32
  1496.2 36.7 reduce-scatter.28
  1536.4 36.7 reduce-scatter.22
  1575.5 110.7 reduce-scatter.20
where the time goes:
time: 1750 us; the launch traced here: 1740 us
  waiting for transfers between devices  958 us (55%)
  other arithmetic  255 us (15%)
  matrix products  200 us (11%)
  local copies, waits for them, and re-layouts  185 us (11%)
  blocking collectives  115 us (7%)
    reduce_scatter x4, waiting for transfers between devices, row_share(): lax.psum_scatter(partial_value, 'mp', scatter_dimension=0, tiled=True)  268 us
    all_gather x4, waiting for transfers between devices, full_rows(): return lax.all_gather(values, 'mp', axis=0, tiled=True)  118 us
    reduce_scatter x1, waiting for transfers between devices, body(): lax.psum_scatter(grad_down_all.astype(jnp.bfloat16), 'dp', scatter_dimens...  94.4 us
    reduce_scatter x1, waiting for transfers between devices, body(): lax.psum_scatter(grad_up_all.astype(jnp.bfloat16), 'dp', scatter_dimensio...  92.4 us
    reduce_scatter x1, waiting for transfers between devices, body(): lax.psum_scatter(grad_gate_all.astype(jnp.bfloat16), 'dp', scatter_dimens...  92.3 us
    all_gather x1, waiting for transfers between devices, body(): lax.all_gather(w_up.astype(low_type), 'dp', axis=1, tiled=True)  69.3 us
    all_gather x1, waiting for transfers between devices, body(): lax.all_gather(w_down.astype(low_type), 'dp', axis=0, tiled=True)  68.6 us
    scatter-add x4, other arithmetic, experts_blocked(): grad_mixed = grad_mixed.at[owners].add(back_slots.reshape(width, D))  67.2 us
  transfers between devices with their start and end apart: 23, of which 18 were waited for; matrix products, arithmetic and copies ran while one was open for 26% of the time, Pallas kernels for 0%

commit v1 on v0

--- a/solution.py
+++ b/solution.py
@@ -1,6 +1,10 @@
+import functools
+
 import jax
 import jax.numpy as jnp
 from jax import lax
+from jax.experimental import pallas as pl
+from jax.experimental.pallas import tpu as pltpu
 from jax.sharding import PartitionSpec as P
 
 D = 1536
@@ -35,52 +39,37 @@
     return (grad_in, gain_grad)
 
 
-def deal_tables(deal_order, block):
+def deal_tables(deal_order, expert_ids, block):
     groups = lax.axis_size("dp")
     parts = lax.axis_size("mp")
     me_index = lax.axis_index("dp")
     part_index = lax.axis_index("mp")
     shard = block // parts
-    piece = shard // groups
-    source = (deal_order // block).reshape(groups, block)
-    local = (deal_order % block).reshape(groups, block)
-    holder = local // shard
-    match = ((source == me_index) & (holder == part_index)).astype(jnp.int32)
-    place = jnp.where(match > 0, jnp.cumsum(match, axis=1) - 1, piece)
-    target = jnp.broadcast_to(jnp.arange(groups, dtype=jnp.int32)[:, None], (groups, block))
-    send_table = (
-        jnp.zeros((groups, piece), jnp.int32)
-        .at[target, place]
-        .set(local - part_index * shard, mode="drop")
-    )
-    send_piece = send_table.reshape(-1)
-    mine_source = lax.dynamic_index_in_dim(source, me_index, 0, keepdims=False)
-    mine_holder = lax.dynamic_index_in_dim(holder, me_index, 0, keepdims=False)
-    anchor = mine_holder * groups + mine_source
-    hits = (anchor[:, None] == jnp.arange(groups * parts, dtype=jnp.int32)[None, :]).astype(
-        jnp.int32
-    )
-    rank = jnp.sum((jnp.cumsum(hits, axis=0) - hits) * hits, axis=1)
-    recv_gathered = anchor * piece + rank
-    counter = jnp.arange(block, dtype=jnp.int32)
-    arrange = jnp.zeros((block,), jnp.int32).at[recv_gathered].set(counter)
-    home_index = (
-        jnp.zeros((shard,), jnp.int32).at[send_piece].set(jnp.arange(shard, dtype=jnp.int32))
-    )
-    stretch_rows = lax.dynamic_slice_in_dim(arrange, part_index * shard, shard, 0)
-    return (send_piece, recv_gathered, arrange, home_index, stretch_rows)
-
-
-def to_dealt(values, tables):
-    moved = lax.all_to_all(values[tables[0]], "dp", split_axis=0, concat_axis=0, tiled=True)
-    return full_rows(moved)[tables[1]]
-
-
-def to_home(stretch, tables):
-    moved = lax.all_to_all(
-        stretch.astype(jnp.bfloat16), "dp", split_axis=0, concat_axis=0, tiled=True
-    ).astype(stretch.dtype)
-    return moved[tables[3]]
+    own = (me_index * parts + part_index) * shard + jnp.arange(shard, dtype=jnp.int32)
+    spots = jnp.arange(deal_order.shape[0], dtype=jnp.int32)
+    dealt = jnp.sum(jnp.where(deal_order[:, None] == own[None, :], spots[:, None], 0), axis=0)
+    home = jnp.sum((dealt[:, None] < dealt[None, :]).astype(jnp.int32), axis=0)
+    mine = lax.dynamic_slice_in_dim(deal_order, me_index * block, block, 0)
+    anchor = (mine % block) // shard * groups + mine // block
+    key = anchor * block + jnp.arange(block, dtype=jnp.int32)
+    arrival = jnp.sum((key[:, None] < key[None, :]).astype(jnp.int32), axis=0)
+    pair = expert_ids[:, 0] * E + expert_ids[:, 1]
+    hits = arrival[:, None] == jnp.arange(block, dtype=jnp.int32)[None, :]
+    code = jnp.sum(jnp.where(hits, pair[:, None], 0), axis=0)
+    order = jnp.sum(jnp.where(home[:, None] == jnp.arange(shard, dtype=jnp.int32)[None, :],
+                              jnp.arange(shard, dtype=jnp.int32)[:, None], 0), axis=0)
+    counts = jnp.sum((expert_ids.reshape(-1)[:, None] == jnp.arange(E, dtype=jnp.int32)[None, :]).astype(jnp.int32), axis=0)
+    return (home, order, code[None, :], counts)
+
+
+def to_dealt(values, order):
+    moved = lax.all_to_all(values[order], "dp", split_axis=0, concat_axis=0, tiled=True)
+    return full_rows(moved)
+
+
+def to_home(stretch, home):
+    moved = lax.all_to_all(stretch, "dp", split_axis=0, concat_axis=0, tiled=True)
+    return moved[home].astype(jnp.float32)
 
 
 def segment_of(lengths, rows):
@@ -94,13 +83,6 @@
     key_pos = jnp.arange(finish, dtype=jnp.int32)
     same = segment[start:finish][:, None] == segment[:finish][None, :]
     return same & (key_pos[None, :] <= query_pos[:, None])
-
-
-def slot_table(expert_ids):
-    flat = expert_ids.reshape(-1)
-    hits = (flat[:, None] == jnp.arange(E, dtype=jnp.int32)[None, :]).astype(jnp.int32)
-    rank = jnp.sum((jnp.cumsum(hits, axis=0) - hits) * hits, axis=1)
-    return flat * CAP + rank
 
 
 def block_scores(query, key, segment, start, block, heads_kv, share):
@@ -184,63 +166,145 @@
     )
 
 
-def swiglu_both(rows_in, grad_in, gate_w, up_w, down_w):
-    gate_part = jnp.einsum("ecd,edf->ecf", rows_in, gate_w, preferred_element_type=jnp.float32)
-    up_part = jnp.einsum("ecd,edf->ecf", rows_in, up_w, preferred_element_type=jnp.float32)
+def mm(a, b, dims=((1,), (0,))):
+    return lax.dot_general(a, b, (dims, ((), ())), preferred_element_type=jnp.float32)
+
+
+NT = ((1,), (1,))
+TN = ((0,), (0,))
+
+
+def expert_step(width, e, refs):
+    (second, grad, gate_w, up_w, down_w, gate_out, up_out, down_out, rank, gates, dots, mixed, back) = refs
+    rows = second.shape[0]
+    low = jnp.bfloat16
+    place = lax.broadcasted_iota(jnp.int32, (width, rows), 0).astype(jnp.float32)
+    hit = place == rank[pl.ds(e, 1), :]
+    pick = jnp.where(hit, 1.0, 0.0).astype(low)
+    gate = jnp.sum(jnp.where(hit, gates[pl.ds(e, 1), :], 0.0), axis=1, keepdims=True)
+    x = mm(pick, second[...]).astype(low)
+    grad_rows = mm(pick, grad[...])
+    gate_part = mm(x, gate_w[0])
+    up_part = mm(x, up_w[0])
     sigma = jax.nn.sigmoid(gate_part)
-    hidden = (gate_part * sigma * up_part).astype(jnp.bfloat16)
-    each = jnp.einsum("ecf,efd->ecd", hidden, down_w, preferred_element_type=jnp.float32)
-    grad_hidden = jnp.einsum("ecd,efd->ecf", grad_in, down_w, preferred_element_type=jnp.float32)
-    grad_gate = (grad_hidden * up_part * sigma * (1.0 + gate_part * (1.0 - sigma))).astype(
-        jnp.bfloat16
-    )
-    grad_up = (grad_hidden * gate_part * sigma).astype(jnp.bfloat16)
-    gate_grad = jnp.einsum("ecd,ecf->edf", rows_in, grad_gate, preferred_element_type=jnp.float32)
-    up_grad = jnp.einsum("ecd,ecf->edf", rows_in, grad_up, preferred_element_type=jnp.float32)
-    down_grad = jnp.einsum("ecf,ecd->efd", hidden, grad_in, preferred_element_type=jnp.float32)
-    back_slots = jnp.einsum("ecf,edf->ecd", grad_gate, gate_w, preferred_element_type=jnp.float32)
-    back_slots = back_slots + jnp.einsum(
-        "ecf,edf->ecd", grad_up, up_w, preferred_element_type=jnp.float32
-    )
-    return (each, back_slots, gate_grad, up_grad, down_grad)
-
-
-def experts_blocked(second_full, grad_full, owner, slot_gate, gate_w, up_w, down_w):
-    rows = second_full.shape[0]
-    stride = E // 4
-    width = stride * CAP
-    mixed = jnp.zeros((rows, D), jnp.float32)
-    grad_mixed = jnp.zeros((rows, D), jnp.float32)
-    dots, gate_grads, up_grads, down_grads = ([], [], [], [])
-    for part in range(4):
-        lead = part * stride
-        owners = owner[part * width : (part + 1) * width]
-        gates_here = slot_gate[part * width : (part + 1) * width]
-        buffer = second_full[owners].reshape(stride, CAP, D)
-        grad_slots = grad_full[owners].astype(jnp.float32)
-        grad_each = (gates_here[:, None] * grad_slots).astype(jnp.bfloat16).reshape(stride, CAP, D)
-        each, back_slots, gate_grad, up_grad, down_grad = swiglu_both(
-            buffer,
-            grad_each,
-            gate_w[lead : lead + stride],
-            up_w[lead : lead + stride],
-            down_w[lead : lead + stride],
-        )
-        each = each.reshape(width, D)
-        mixed = mixed.at[owners].add(each * gates_here[:, None])
-        grad_mixed = grad_mixed.at[owners].add(back_slots.reshape(width, D))
-        dots.append(jnp.sum(grad_slots * each, axis=1))
-        gate_grads.append(gate_grad)
-        up_grads.append(up_grad)
-        down_grads.append(down_grad)
-    return (
-        mixed,
-        grad_mixed,
-        jnp.concatenate(dots, axis=0),
-        jnp.concatenate(gate_grads, axis=0),
-        jnp.concatenate(up_grads, axis=0),
-        jnp.concatenate(down_grads, axis=0),
-    )
+    hidden = (gate_part * sigma * up_part).astype(low)
+    each = mm(hidden, down_w[0])
+    dot = jnp.sum(grad_rows * each, axis=1, keepdims=True)
+    dots[pl.ds(e, 1), :] = jnp.sum(jnp.where(hit, dot, 0.0), axis=0, keepdims=True)
+    mixed[...] += mm(pick, (each * gate).astype(low), TN)
+    grad_each = (grad_rows * gate).astype(low)
+    grad_hidden = mm(grad_each, down_w[0], NT)
+    grad_gate = (grad_hidden * up_part * sigma * (1.0 + gate_part * (1.0 - sigma))).astype(low)
+    grad_up = (grad_hidden * gate_part * sigma).astype(low)
+    down_out[0] = mm(hidden, grad_each, TN).astype(low)
+    gate_out[0] = mm(x, grad_gate, TN).astype(low)
+    up_out[0] = mm(x, grad_up, TN).astype(low)
+    back_rows = mm(grad_gate, gate_w[0], NT) + mm(grad_up, up_w[0], NT)
+    back[...] += mm(pick, back_rows.astype(low), TN)
+
+
+def expert_kernel(counts, code, router, second, grad, gate_w, up_w, down_w,
+                  mixed_out, back_out, gate_out, up_out, down_out, router_out,
+                  rank, gates, dots, mixed, back):
+    e = pl.program_id(0)
+    rows = second.shape[0]
+    low = jnp.bfloat16
+    expert = lax.broadcasted_iota(jnp.int32, (E, rows), 0)
+    first_id = code[...] // E
+    second_id = code[...] % E
+    picks = [jnp.where(expert == ids, 1.0, 0.0) for ids in (first_id, second_id)]
+
+    @pl.when(e == 0)
+    def _():
+        logits = mm(router[...], second[...], NT)
+        chosen = [jnp.sum(pick * logits, axis=0, keepdims=True) for pick in picks]
+        top = jnp.maximum(chosen[0], chosen[1])
+        raised = [jnp.exp(value - top) for value in chosen]
+        total = raised[0] + raised[1]
+        gates[...] = picks[0] * (raised[0] / total) + picks[1] * (raised[1] / total)
+        hits = picks[0] + picks[1]
+        earlier = lax.broadcasted_iota(jnp.int32, (rows, rows), 0) < lax.broadcasted_iota(
+            jnp.int32, (rows, rows), 1
+        )
+        before = mm(hits.astype(low), jnp.where(earlier, 1.0, 0.0).astype(low))
+        rank[...] = jnp.where(hits > 0.0, before, -1.0)
+        mixed[...] = jnp.zeros_like(mixed)
+        back[...] = jnp.zeros_like(back)
+
+    refs = (second, grad, gate_w, up_w, down_w, gate_out, up_out, down_out, rank, gates, dots, mixed, back)
+    count = counts[e]
+
+    @pl.when(count <= CAP // 2)
+    def _():
+        expert_step(CAP // 2, e, refs)
+
+    @pl.when(count > CAP // 2)
+    def _():
+        expert_step(CAP, e, refs)
+
+    @pl.when(e == E - 1)
+    def _():
+        grad_gates = [jnp.sum(pick * dots[...], axis=0, keepdims=True) for pick in picks]
+        own = [jnp.sum(pick * gates[...], axis=0, keepdims=True) for pick in picks]
+        inner = own[0] * grad_gates[0] + own[1] * grad_gates[1]
+        grad_logits = picks[0] * (own[0] * (grad_gates[0] - inner)) + picks[1] * (
+            own[1] * (grad_gates[1] - inner)
+        )
+        grad_logits = grad_logits.astype(low)
+        router_out[...] = mm(grad_logits, second[...])
+        mixed_out[...] = mixed[...].astype(low)
+        back_out[...] = (back[...] + mm(grad_logits, router[...], TN)).astype(low)
+
+
+def experts(second, grad, code, counts, router, gate_w, up_w, down_w):
+    rows = second.shape[0]
+    hidden = gate_w.shape[2]
+    low = jnp.bfloat16
+    whole = lambda e, *_: (0, 0)
+    by_expert = lambda e, *_: (e, 0, 0)
+    wide = pl.BlockSpec((1, D, hidden), by_expert)
+    tall = pl.BlockSpec((1, hidden, D), by_expert)
+    block = pl.BlockSpec((rows, D), whole)
+    return pl.pallas_call(
+        expert_kernel,
+        grid_spec=pltpu.PrefetchScalarGridSpec(
+            num_scalar_prefetch=1,
+            grid=(E,),
+            in_specs=[
+                pl.BlockSpec((1, rows), whole),
+                pl.BlockSpec((E, D), whole),
+                block,
+                block,
+                wide,
+                wide,
+                tall,
+            ],
+            out_specs=[block, block, wide, wide, tall, pl.BlockSpec((E, D), whole)],
+            scratch_shapes=[
+                pltpu.VMEM((E, rows), jnp.float32),
+                pltpu.VMEM((E, rows), jnp.float32),
+                pltpu.VMEM((E, rows), jnp.float32),
+                pltpu.VMEM((rows, D), jnp.float32),
+                pltpu.VMEM((rows, D), jnp.float32),
+            ],
+        ),
+        out_shape=[
+            jax.ShapeDtypeStruct((rows, D), low),
+            jax.ShapeDtypeStruct((rows, D), low),
+            jax.ShapeDtypeStruct((E, D, hidden), low),
+            jax.ShapeDtypeStruct((E, D, hidden), low),
+            jax.ShapeDtypeStruct((E, hidden, D), low),
+            jax.ShapeDtypeStruct((E, D), jnp.float32),
+        ],
+        compiler_params=pltpu.CompilerParams(
+            dimension_semantics=("arbitrary",), vmem_limit_bytes=58 * 2**20
+        ),
+        cost_estimate=pl.CostEstimate(
+            flops=E * CAP * D * (18 * hidden + 8 * rows),
+            bytes_accessed=12 * E * D * hidden + 8 * rows * D,
+            transcendentals=E * CAP * hidden,
+        ),
+    )(counts, code, router, second, grad, gate_w, up_w, down_w)
 
 
 def body(
@@ -272,7 +336,7 @@
         lax.all_gather(w_up.astype(low_type), "dp", axis=1, tiled=True),
         lax.all_gather(w_down.astype(low_type), "dp", axis=0, tiled=True),
     )
-    tables = deal_tables(deal_order, rows)
+    home, order, code, counts = deal_tables(deal_order, expert_ids, rows)
     segment = segment_of(seq_lengths[0], rows)
     scale_one, normed_one = norm_apply(tokens, attn_gain)
     first_full = full_rows(normed_one)
@@ -281,35 +345,15 @@
     value = jnp.dot(first_full, value_w, preferred_element_type=jnp.float32).astype(low_type)
     mix, totals = attend_forward(query, key, value, segment)
     mix = mix.astype(low_type)
-    middle = tokens + row_share(jnp.dot(mix, out_w, preferred_element_type=jnp.float32))
+    middle = tokens + row_share(jnp.dot(mix, out_w, preferred_element_type=jnp.float32).astype(low_type)).astype(jnp.float32)
     scale_two, normed_two = norm_apply(middle, moe_gain)
-    second_full = to_dealt(normed_two, tables)
-    grad_full = to_dealt(out_grad.astype(low_type), tables)
-    logits = jnp.dot(second_full, router_w, preferred_element_type=jnp.float32)
-    picker = (expert_ids[:, :, None] == jnp.arange(E, dtype=jnp.int32)[None, None, :]).astype(
-        jnp.float32
-    )
-    gates = jax.nn.softmax(jnp.sum(picker * logits[:, None, :], axis=2), axis=1)
-    slots = slot_table(expert_ids)
-    owner = (
-        jnp.zeros((E * CAP,), jnp.int32).at[slots].set(jnp.arange(2 * rows, dtype=jnp.int32) // 2)
-    )
-    slot_gate = jnp.zeros((E * CAP,), jnp.float32).at[slots].set(gates.reshape(-1))
-    mixed, grad_mixed, dots, grad_gate_all, grad_up_all, grad_down_all = experts_blocked(
-        second_full, grad_full, owner, slot_gate, gate_w, up_w, down_w
-    )
-    block_out = middle + to_home(row_share(mixed[tables[2]]), tables)
-    grad_gates = lax.psum(dots[slots].reshape(rows, 2), "mp")
-    grad_chosen = gates * (grad_gates - jnp.sum(gates * grad_gates, axis=1, keepdims=True))
-    grad_logits = jnp.sum(picker * grad_chosen[:, :, None], axis=1).astype(low_type)
-    grad_router = jnp.einsum(
-        "td,te->de", second_full, grad_logits, preferred_element_type=jnp.float32
-    )
-    grad_stretch = row_share(grad_mixed[tables[2]])
-    grad_stretch = grad_stretch + jnp.einsum(
-        "te,de->td", grad_logits[tables[4]], router_w, preferred_element_type=jnp.float32
-    )
-    grad_normed_two = to_home(grad_stretch, tables)
+    second_full = to_dealt(normed_two, order)
+    grad_full = to_dealt(out_grad.astype(low_type), order)
+    mixed, back, grad_gate_all, grad_up_all, grad_down_all, grad_router = experts(
+        second_full, grad_full, code, counts, router_w.T, gate_w, up_w, down_w
+    )
+    grad_normed_two = to_home(row_share(back), home)
+    block_out = middle + to_home(row_share(mixed), home)
     grad_middle_norm, grad_moe_gain = norm_back(middle, moe_gain, scale_two, grad_normed_two)
     grad_middle = out_grad + grad_middle_norm
     grad_attn_full = full_rows(grad_middle.astype(low_type))
@@ -333,11 +377,15 @@
         "td,th->dh", first_full, grad_value, preferred_element_type=jnp.float32
     )
     grad_tokens_norm, grad_attn_gain = norm_back(
-        tokens, attn_gain, scale_one, row_share(grad_first)
+        tokens, attn_gain, scale_one, row_share(grad_first.astype(low_type)).astype(jnp.float32)
     )
     tokens_grad = grad_middle + grad_tokens_norm
-    attn_gain_sum, moe_gain_sum = lax.psum((grad_attn_gain, grad_moe_gain), ("dp", "mp"))
-    query_sum, key_sum, value_sum, out_sum, router_sum, gate_sum, up_sum, down_sum = (
+    attn_gain_sum, moe_gain_sum, router_total = lax.psum(
+        (grad_attn_gain, grad_moe_gain, grad_router), ("dp", "mp")
+    )
+    width = w_router.shape[0]
+    router_sum = lax.dynamic_slice_in_dim(router_total, lax.axis_index("dp") * width, width, 1).T
+    query_sum, key_sum, value_sum, out_sum, gate_sum, up_sum, down_sum = (
         lax.psum_scatter(
             grad_query_w.astype(jnp.bfloat16), "dp", scatter_dimension=0, tiled=True
         ).astype(jnp.float32),
@@ -349,9 +397,6 @@
         ).astype(jnp.float32),
         lax.psum_scatter(
             grad_out_w.astype(jnp.bfloat16), "dp", scatter_dimension=1, tiled=True
-        ).astype(jnp.float32),
-        lax.psum_scatter(
-            grad_router.astype(jnp.bfloat16), "dp", scatter_dimension=0, tiled=True
         ).astype(jnp.float32),
         lax.psum_scatter(
             grad_gate_all.astype(jnp.bfloat16), "dp", scatter_dimension=1, tiled=True

time: 1750 us -> 1500 us (0.86)
  other arithmetic: 255 us -> 72.9 us
  local copies, waits for them, and re-layouts: 185 us -> 27.3 us
  waiting for transfers between devices: 958 us -> 1100 us
  matrix products: 200 us -> 69 us
  Pallas kernels: 0 us -> 94.5 us
    scatter-add x8 -> x0, other arithmetic: 134 us -> none  [the longest x4 67.2 us: experts_blocked(): grad_mixed = grad_mixed.at[owners].add(back_slots.reshape(width, D))]
    dot_general x40 -> x1, matrix products: 137 us -> 4.78 us  [body(): jnp.dot(mix, out_w, preferred_element_type=jnp.float32).astype(low_type)]
    psum x0 -> x1, waiting for transfers between devices: none -> 112 us  [body(): lax.psum((grad_attn_gain, grad_moe_gain, grad_router), ('dp', 'mp'))]
    reduce_scatter x4, waiting for transfers between devices: 268 us -> 158 us  [row_share(): lax.psum_scatter(partial_value, 'mp', scatter_dimension=0, tiled=True)]
    gather x18 -> x4, local copies, waits for them, and re-layouts: 104 us -> 7.75 us  [the longest x2 4.82 us: to_home(): return moved[home].astype(jnp.float32)]
    pallas_call x0 -> x1, Pallas kernels: none -> 94.5 us  [experts(): pl.pallas_call(expert_kernel, grid_spec=pltpu.PrefetchScalarGridSpec(num_...]
    all_gather x4, waiting for transfers between devices: 118 us -> 186 us  [full_rows(): return lax.all_gather(values, 'mp', axis=0, tiled=True)]
    reduce_scatter x1, waiting for transfers between devices: 94.4 us -> 49.8 us  [body(): lax.psum_scatter(grad_down_all.astype(jnp.bfloat16), 'dp', scatter_dimens...]
  transfers between devices with their start and end apart: 23 -> 23, of which waited for: 18 -> 21; matrix products, arithmetic and copies ran while one was open for 26% -> 9% of each run, Pallas kernels for 0% -> 0%
where the time goes in v1:
time: 1500 us; the launch traced here: 1490 us
  waiting for transfers between devices  1100 us (73%)
  blocking collectives  102 us (7%)
  Pallas kernels  94.5 us (6%)
  other arithmetic  72.9 us (5%)
  matrix products  69 us (5%)
  local copies, waits for them, and re-layouts  27.3 us (2%)
  between operations  15.7 us (1%)
    all_gather x4, waiting for transfers between devices, full_rows(): return lax.all_gather(values, 'mp', axis=0, tiled=True)  186 us
    reduce_scatter x4, waiting for transfers between devices, row_share(): lax.psum_scatter(partial_value, 'mp', scatter_dimension=0, tiled=True)  158 us
    psum x1, waiting for transfers between devices, body(): lax.psum((grad_attn_gain, grad_moe_gain, grad_router), ('dp', 'mp'))  112 us
    pallas_call x1, Pallas kernels, experts(): pl.pallas_call(expert_kernel, grid_spec=pltpu.PrefetchScalarGridSpec(num_...  94.5 us
    reduce_scatter x1, waiting for transfers between devices, body(): lax.psum_scatter(grad_gate_all.astype(jnp.bfloat16), 'dp', scatter_dimens...  92.5 us
    reduce_scatter x1, waiting for transfers between devices, body(): lax.psum_scatter(grad_up_all.astype(jnp.bfloat16), 'dp', scatter_dimensio...  92.3 us
    all_gather x1, waiting for transfers between devices, body(): lax.all_gather(w_up.astype(low_type), 'dp', axis=1, tiled=True)  74.6 us
    all_gather x1, waiting for transfers between devices, body(): lax.all_gather(w_down.astype(low_type), 'dp', axis=0, tiled=True)  74.6 us
  transfers between devices with their start and end apart: 23, of which 21 were waited for; matrix products, arithmetic and copies ran while one was open for 9% of the time, Pallas kernels for 0%

profile of v1, /device:TPU:0, one launch (start us, length us, event | category | flops | bytes accessed | tf_op | source)
XLA Modules:
  0.0 1493.1 jit_solution(9773788368608810213)
XLA Ops:
  10.1 2.5 multiply_convert_fusion.1
  15.4 12.1 all_gather.37
  27.5 9.5 all_gather.38
  38.2 40.7 %all-gather.11.cloned.1.call-done = bf16[1024,1536]{1,0:T(8,128)(2,1)} async-done(((bf16[256,1536]{1,0:T(8,128)(2,1)}), bf16[1024,1536]{1,0:T(8,128)(2,1)}) %all-gather.11.cloned.1.call-update) | async-done | bytes 3145744 | tf_op jit(solution)/shard_map/all_gather | solution.py:20
  79.0 3.2 convolution_convert_fusion.7
  85.4 18.7 %all-gather.13.cloned.1.call-done = bf16[1536,384]{1,0:T(8,128)(2,1)} async-done(((bf16[192,384]{1,0:T(8,128)(2,1)}), bf16[1536,384]{1,0:T(8,128)(2,1)}) %all-gather.13.cloned.1.call-update) | async-done | bytes 1179664 | tf_op jit(solution)/shard_map/all_gather | solution.py:330
  104.1 2.7 convolution_convert_fusion.6
  112.1 2.2 fusion.75
  116.1 2.9 copy-done
  119.0 2.6 fusion.36
  121.6 9.2 all-gather.15.cloned.1.call-done
  130.8 4.8 convolution_convert_fusion
  137.1 3.7 select_reduce_fusion
  143.6 15.7 %all_to_all.48 = bf16[8,32,1536]{2,1,0:T(8,128)(2,1)} all-to-all(bf16[8,32,1536]{2,1,0:T(8,128)(2,1)S(1)} %bitcast.184), channel_id=1, replica_groups=mesh['dp'=8,'mp'=4] {'dp'}, dimensions={0} | all-to-all | bytes 1572864 | tf_op jit(solution)/shard_map/all_to_all | solution.py:66
  159.4 36.6 %reduce-scatter.12.cloned.1.call-done = bf16[256,1536]{1,0:T(8,128)(2,1)} async-done(((bf16[1024,1536]{1,0:T(8,128)(2,1)}), bf16[256,1536]{1,0:T(8,128)(2,1)}) %reduce-scatter.12.cloned.1.call-update) | async-done | bytes 786448 | tf_op jit(solution)/shard_map/reduce_scatter | solution.py:24
  201.3 16.1 %all_to_all.49 = bf16[8,32,1536]{2,1,0:T(8,128)(2,1)} all-to-all(bf16[8,32,1536]{2,1,0:T(8,128)(2,1)S(1)} %bitcast.183), channel_id=1, replica_groups=mesh['dp'=8,'mp'=4] {'dp'}, dimensions={0} | all-to-all | bytes 1572864 | tf_op jit(solution)/shard_map/all_to_all | solution.py:66
  217.5 3.2 convert_element_type.162
  220.8 3.2 convert_element_type.163
  224.2 3.2 convert_element_type.164
  227.5 8.3 all-gather
  240.2 20.8 %all-gather.19.cloned.1.call-done.grad = bf16[1024,1536]{1,0:T(8,128)(2,1)} async-done(((bf16[256,1536]{1,0:T(8,128)(2,1)}), bf16[1024,1536]{1,0:T(8,128)(2,1)}) %all-gather.19.cloned.1.call-update) | async-done | bytes 3145744 | tf_op jit(solution)/shard_map/all_gather | solution.py:20
  261.0 63.6 %all-gather.17.cloned.1.call-done.second = bf16[1024,1536]{1,0:T(8,128)(2,1)} async-done(((bf16[256,1536]{1,0:T(8,128)(2,1)}), bf16[1024,1536]{1,0:T(8,128)(2,1)}) %all-gather.17.cloned.1.call-update) | async-done | bytes 3145744 | tf_op jit(solution)/shard_map/all_gather | solution.py:20
  324.6 73.3 %all-gather.21.cloned.1.call-done.gate_w = bf16[16,1536,256]{2,1,0:T(8,128)(2,1)} async-done(((bf16[16,192,256]{2,1,0:T(8,128)(2,1)}), bf16[16,1536,256]{2,1,0:T(8,128)(2,1)}) %all-gather.21.cloned.1.call-update) | async-done | bytes 12582928 | tf_op jit(solution)/shard_map/all_gather | solution.py:335
  397.9 74.6 %all-gather.23.cloned.1.call-done.up_w = bf16[16,1536,256]{2,1,0:T(8,128)(2,1)} async-done(((bf16[16,192,256]{2,1,0:T(8,128)(2,1)}), bf16[16,1536,256]{2,1,0:T(8,128)(2,1)}) %all-gather.23.cloned.1.call-update) | async-done | bytes 12582928 | tf_op jit(solution)/shard_map/all_gather | solution.py:336
  472.5 74.6 %all-gather.25.cloned.1.call-done.down_w = bf16[16,256,1536]{2,1,0:T(8,128)(2,1)} async-done(((bf16[2,256,1536]{2,1,0:T(8,128)(2,1)}), bf16[16,256,1536]{2,1,0:T(8,128)(2,1)}) %all-gather.25.cloned.1.call-update) | async-done | bytes 12582928 | tf_op jit(solution)/shard_map/all_gather | solution.py:337
  547.1 94.5 %shard_map.248 = (bf16[1024,1536]{1,0:T(8,128)(2,1)}, bf16[1024,1536]{1,0:T(8,128)(2,1)}, bf16[16,1536,256]{2,1,0:T(8,128)(2,1)}, bf16[16,1536,256]{2,1,0:T(8,12...) custom-call(s32[16]{0:T(128)} %convert_reduce_fusion.2.counts, s32[1,1024]{1,0:T(1,128)} %bitcast.202, ...), custom_call_target="tpu_custom_call" | custom-call | flops 80530636800 | bytes 88080384 | tf_op jit(solution)/shard_map/pallas_call | solution.py:268
  641.7 60.4 %reduce-scatter.16.cloned.1.call-done = bf16[256,1536]{1,0:T(8,128)(2,1)} async-done(((bf16[1024,1536]{1,0:T(8,128)(2,1)}), bf16[256,1536]{1,0:T(8,128)(2,1)}) %reduce-scatter.16.cloned.1.call-update) | async-done | bytes 786448 | tf_op jit(solution)/shard_map/reduce_scatter | solution.py:24
  702.1 3.7 all-to-all-start.3
  706.4 11.9 all-to-all-done.3
  718.4 2.4 gather_fusion.3
  720.8 2.4 fusion.30
  726.6 60.5 %all-gather.27.cloned.1.call-done = bf16[1024,1536]{1,0:T(8,128)(2,1)} async-done(((bf16[256,1536]{1,0:T(8,128)(2,1)}), bf16[1024,1536]{1,0:T(8,128)(2,1)}) %all-gather.27.cloned.1.call-update) | async-done | bytes 3145744 | tf_op jit(solution)/shard_map/all_gather | solution.py:20
  787.1 3.8 convolution_convert_fusion.5
  790.9 3.9 fusion.50
  794.8 6.8 fusion.7
  801.6 6.0 fusion
  807.6 2.1 fusion.46
  809.7 4.7 fusion.9
  816.1 1.8 fusion.54
  818.0 1.8 convolution_convert_fusion.3
  819.9 9.9 fusion.2
  829.9 2.0 fusion.49
  835.9 5.0 convolution_convert_fusion.1
  841.2 2.5 fusion.34
  843.8 4.2 fusion.35
  848.7 2.9 convolution_convert_fusion.2
  853.2 1.8 fusion.56
  855.1 2.7 add_convert_fusion
  859.9 3.7 all-to-all-start.2
  863.7 111.8 %all-reduce.5.cloned.1.call-done = f32[16,1536]{1,0:T(8,128)} async-done(((f32[16,1536]{1,0:T(8,128)}), f32[16,1536]{1,0:T(8,128)}) %all-reduce.5.cloned.1.call-update) | async-done | bytes 98320 | tf_op jit(solution)/shard_map/psum | solution.py:383
  976.9 2.4 gather_fusion.2
  979.3 33.8 %reduce-scatter.24.cloned.1.call-done = bf16[192,128]{1,0:T(8,128)(2,1)} async-done(((bf16[1536,128]{1,0:T(8,128)(2,1)}), bf16[192,128]{1,0:T(8,128)(2,1)}) %reduce-scatter.24.cloned.1.call-update) | async-done | bytes 49168 | tf_op jit(solution)/shard_map/reduce_scatter | solution.py:395
  1014.6 35.3 %reduce-scatter.22.cloned.1.call-done = bf16[192,128]{1,0:T(8,128)(2,1)} async-done(((bf16[1536,128]{1,0:T(8,128)(2,1)}), bf16[192,128]{1,0:T(8,128)(2,1)}) %reduce-scatter.22.cloned.1.call-update) | async-done | bytes 49168 | tf_op jit(solution)/shard_map/reduce_scatter | solution.py:392
  1051.3 39.0 %reduce-scatter.26.cloned.1.call-done = bf16[384,192]{0,1:T(8,128)(2,1)} async-done(((bf16[384,1536]{0,1:T(8,128)(2,1)}), bf16[384,192]{0,1:T(8,128)(2,1)}) %reduce-scatter.26.cloned.1.call-update) | async-done | bytes 147472 | tf_op jit(solution)/shard_map/reduce_scatter | solution.py:398
  1092.0 39.2 %reduce-scatter.20.cloned.1.call-done = bf16[192,384]{1,0:T(8,128)(2,1)} async-done(((bf16[1536,384]{1,0:T(8,128)(2,1)}), bf16[192,384]{1,0:T(8,128)(2,1)}) %reduce-scatter.20.cloned.1.call-update) | async-done | bytes 147472 | tf_op jit(solution)/shard_map/reduce_scatter | solution.py:389
  1132.8 61.3 %reduce-scatter.18.cloned.1.call-done = bf16[256,1536]{1,0:T(8,128)(2,1)} async-done(((bf16[1024,1536]{1,0:T(8,128)(2,1)}), bf16[256,1536]{1,0:T(8,128)(2,1)}) %reduce-scatter.18.cloned.1.call-update) | async-done | bytes 786448 | tf_op jit(solution)/shard_map/reduce_scatter | solution.py:24
  1195.7 40.8 %all-reduce.2 = (f32[1536]{0:T(1024)}, f32[1536]{0:T(1024)}) all-reduce(f32[1536]{0:T(1024)S(1)} %get-tuple-element.90, f32[1536]{0:T(1024)S(1)} %copy-done.55), channel_id=1, replica_groups=mesh['dp'=8,'mp'=4] {'dp','mp'}, use_global_device_ids=true, to_apply=%region_23.24 | all-reduce | flops 3072 | bytes 24576 | tf_op jit(solution)/shard_map/psum | solution.py:383
  1236.6 4.3 fusion.24
  1240.9 49.8 %reduce-scatter.32.cloned.1.call-done = bf16[2,256,1536]{2,1,0:T(8,128)(2,1)} async-done(((bf16[16,256,1536]{2,1,0:T(8,128)(2,1)}), bf16[2,256,1536]{2,1,0:T(8,128)(2,1)}) %reduce-scatter.32.cloned.1.call-update) | async-done | bytes 1572880 | tf_op jit(solution)/shard_map/reduce_scatter | solution.py:407
  1290.7 3.5 convert_element_type.189
  1294.2 92.3 %reduce-scatter.30.cloned.1.call-done = bf16[16,192,256]{2,1,0:T(8,128)(2,1)} async-done(((bf16[16,1536,256]{2,1,0:T(8,128)(2,1)}), bf16[16,192,256]{2,1,0:T(8,128)(2,1)}) %reduce-scatter.30.cloned.1.call-update) | async-done | bytes 1572880 | tf_op jit(solution)/shard_map/reduce_scatter | solution.py:404
  1386.5 3.4 convert_element_type.188
  1389.9 92.5 %reduce-scatter.28.cloned.1.call-done = bf16[16,192,256]{2,1,0:T(8,128)(2,1)} async-done(((bf16[16,1536,256]{2,1,0:T(8,128)(2,1)}), bf16[16,192,256]{2,1,0:T(8,128)(2,1)}) %reduce-scatter.28.cloned.1.call-update) | async-done | bytes 1572880 | tf_op jit(solution)/shard_map/reduce_scatter | solution.py:401
  1482.4 3.4 convert_element_type.187
  (258 shorter events, 55.0 us)
Async XLA Ops:
  7.2 5.5 copy-start.38
  7.2 6.2 copy-start.39
  7.2 7.0 copy-start.70
  7.2 7.3 copy-start.46
  7.2 7.3 copy-start.47
  7.2 71.7 %all-gather.11.cloned.1.call-start = ((), (), s32[]{:S(2)}) async-start(), calls=%async_computation.15 | async-start | bytes 3932160 | tf_op jit(solution)/shard_map/all_gather | solution.py:20
  12.6 91.6 %all-gather.13.cloned.1.call-start = ((), (), s32[]{:S(2)}) async-start(), calls=%async_computation.16 | async-start | bytes 1327104 | tf_op jit(solution)/shard_map/all_gather | solution.py:330
  13.4 117.4 %all-gather.15.cloned.1.call-start = ((), (), s32[]{:S(2)}) async-start(), calls=%async_computation.17 | async-start | bytes 1327104 | tf_op jit(solution)/shard_map/all_gather | solution.py:333
  14.1 181.9 %reduce-scatter.12.cloned.1.call-start = ((), (), s32[]{:S(2)}) async-start(), calls=%async_computation.18 | async-start | bytes 3932160 | tf_op jit(solution)/shard_map/reduce_scatter | solution.py:24
  37.0 47.1 %copy-start.17 = (bf16[1536,128]{1,0:T(8,128)(2,1)}, bf16[1536,128]{1,0:T(8,128)(2,1)S(1)}, u32[]{:S(2)}) copy-start(bf16[1536,128]{1,0:T(8,128)(2,1)S(1)} %all_gather.38) | copy-start | bytes 1179652
  78.9 3.9 copy-start.3
  79.0 3.9 copy-start.21
  85.4 21.5 %copy-start.26 = (pred[512,512]{0,1:T(8,128)(4,1)S(1)}, pred[512,512]{0,1:T(8,128)(4,1)}, u32[]{:S(2)}) copy-start(pred[512,512]{0,1:T(8,128)(4,1)} %fusion.55) | copy-start | bytes 786436
  85.4 21.5 %copy-start.33 = (bf16[512,128]{0,1:T(8,128)(2,1)S(1)}, bf16[512,128]{0,1:T(8,128)(2,1)}, u32[]{:S(2)}) copy-start(bf16[512,128]{0,1:T(8,128)(2,1)} %slice.137) | copy-start | bytes 393220
  106.9 5.1 copy-start.15
  112.0 18.8 %copy-start.71 = (bf16[2,64,3,512]{3,1,2,0:T(8,128)(2,1)}, bf16[2,64,3,512]{3,1,2,0:T(8,128)(2,1)S(1)}, u32[]{:S(2)}) copy-start(bf16[2,64,3,512]{3,1,2,0:T(8,128)(2,1)S(1)} %fusion.33) | copy-start | bytes 1179652
  114.3 4.7 copy-start
  114.3 4.7 copy-start.41
  114.3 4.7 copy-start.28
  121.6 9.2 copy-start.72
  135.6 125.4 %all-gather.19.cloned.1.call-start = ((), (), s32[]{:S(2)}) async-start(), calls=%async_computation.20 | async-start | bytes 3932160 | tf_op jit(solution)/shard_map/all_gather | solution.py:20
  142.1 53.9 %copy-start.2 = (f32[256,1536]{1,0:T(8,128)S(1)}, f32[256,1536]{1,0:T(8,128)}, u32[]{:S(2)}) copy-start(f32[256,1536]{1,0:T(8,128)} %param.27) | copy-start | bytes 4718596
  159.3 39.2 %copy-start.43 = (f32[1536]{0:T(1024)S(1)}, f32[1536]{0:T(1024)}, u32[]{:S(2)}) copy-start(f32[1536]{0:T(1024)} %param.33) | copy-start | bytes 18436
  159.3 165.3 %all-gather.17.cloned.1.call-start = ((), (), s32[]{:S(2)}) async-start(), calls=%async_computation.19 | async-start | bytes 3932160 | tf_op jit(solution)/shard_map/all_gather | solution.py:20
  217.5 180.4 %all-gather.21.cloned.1.call-start = ((), (), s32[]{:S(2)}) async-start(), calls=%async_computation.21 | async-start | bytes 14155776 | tf_op jit(solution)/shard_map/all_gather | solution.py:335
  220.8 251.7 %all-gather.23.cloned.1.call-start = ((), (), s32[]{:S(2)}) async-start(), calls=%async_computation.22 | async-start | bytes 14155776 | tf_op jit(solution)/shard_map/all_gather | solution.py:336
  224.1 12.5 copy-start.54
  224.1 323.0 %all-gather.25.cloned.1.call-start = ((), (), s32[]{:S(2)}) async-start(), calls=%async_computation.23 | async-start | bytes 14155776 | tf_op jit(solution)/shard_map/all_gather | solution.py:337
  227.4 474.7 %reduce-scatter.16.cloned.1.call-start = ((), (), s32[]{:S(2)}) async-start(), calls=%async_computation.25 | async-start | bytes 3932160 | tf_op jit(solution)/shard_map/reduce_scatter | solution.py:24
  641.6 64.2 %copy-start.67 = (s32[256]{0:T(256)S(1)}, s32[256]{0:T(256)}, u32[]{:S(2)}) copy-start(s32[256]{0:T(256)} %copy-done.66) | copy-start | bytes 3076
  702.1 16.3 %all-to-all-start.3 = ((bf16[8,32,1536]{2,1,0:T(8,128)(2,1)}), bf16[8,32,1536]{2,1,0:T(8,128)(2,1)S(1)}, u32[]{:S(2)}, u32[]{:S(2)}) async-start(bf16[8,32,1536]{2,1,0:T(8,128)(2,1)} %bitcast.196), calls=%async_computation.6 | async-start | bytes 1572864 | tf_op jit(solution)/shard_map/all_to_all | solution.py:71
  705.8 81.3 %all-gather.27.cloned.1.call-start = ((), (), s32[]{:S(2)}) async-start(), calls=%async_computation.26 | async-start | bytes 3932160 | tf_op jit(solution)/shard_map/all_gather | solution.py:20
  725.2 134.7 %reduce-scatter.14.cloned.1.call-start = ((), (), s32[]{:S(2)}) async-start(), calls=%async_computation.24 | async-start | bytes 3932160 | tf_op jit(solution)/shard_map/reduce_scatter | solution.py:24
  725.8 249.7 %all-reduce.5.cloned.1.call-start = ((), (), s32[]{:S(2)}) async-start(), calls=%async_computation.32 | async-start | bytes 196608 | tf_op jit(solution)/shard_map/psum | solution.py:383
  726.5 286.6 %reduce-scatter.24.cloned.1.call-start = ((), (), s32[]{:S(2)}) async-start(), calls=%async_computation.30 | async-start | bytes 442368 | tf_op jit(solution)/shard_map/reduce_scatter | solution.py:395
  787.1 14.5 slice-start
  787.1 14.5 slice-start.1
  790.9 3.9 copy-start.40
  794.8 6.8 slice-start.2
  794.8 14.9 slice-start.3
  801.6 8.1 slice-start.4
  809.7 6.4 copy-start.20
  819.8 230.0 %reduce-scatter.22.cloned.1.call-start = ((), (), s32[]{:S(2)}) async-start(), calls=%async_computation.29 | async-start | bytes 442368 | tf_op jit(solution)/shard_map/reduce_scatter | solution.py:392
  819.9 10.0 copy-start.16
  819.9 10.0 copy-start.36
  829.9 4.2 copy-start.5
  835.9 5.3 copy-start.34
  835.9 254.5 %reduce-scatter.26.cloned.1.call-start = ((), (), s32[]{:S(2)}) async-start(), calls=%async_computation.31 | async-start | bytes 1327104 | tf_op jit(solution)/shard_map/reduce_scatter | solution.py:398
  840.9 290.2 %reduce-scatter.20.cloned.1.call-start = ((), (), s32[]{:S(2)}) async-start(), calls=%async_computation.28 | async-start | bytes 1327104 | tf_op jit(solution)/shard_map/reduce_scatter | solution.py:389
  843.8 4.2 copy-start.29
  843.8 5.0 copy-start.6
  851.6 342.5 %reduce-scatter.18.cloned.1.call-start = ((), (), s32[]{:S(2)}) async-start(), calls=%async_computation.27 | async-start | bytes 3932160 | tf_op jit(solution)/shard_map/reduce_scatter | solution.py:24
  857.8 432.9 %reduce-scatter.32.cloned.1.call-start = ((), (), s32[]{:S(2)}) async-start(), calls=%async_computation.35 | async-start | bytes 14155776 | tf_op jit(solution)/shard_map/reduce_scatter | solution.py:407
  858.6 527.9 %reduce-scatter.30.cloned.1.call-start = ((), (), s32[]{:S(2)}) async-start(), calls=%async_computation.34 | async-start | bytes 14155776 | tf_op jit(solution)/shard_map/reduce_scatter | solution.py:404
  859.2 623.3 %reduce-scatter.28.cloned.1.call-start = ((), (), s32[]{:S(2)}) async-start(), calls=%async_computation.33 | async-start | bytes 14155776 | tf_op jit(solution)/shard_map/reduce_scatter | solution.py:401
  859.9 117.0 %all-to-all-start.2 = ((bf16[8,32,1536]{2,1,0:T(8,128)(2,1)}), bf16[8,32,1536]{2,1,0:T(8,128)(2,1)S(1)}, u32[]{:S(2)}, u32[]{:S(2)}) async-start(bf16[8,32,1536]{2,1,0:T(8,128)(2,1)} %bitcast.195), calls=%async_computation.4 | async-start | bytes 1572864 | tf_op jit(solution)/shard_map/all_to_all | solution.py:71
  976.9 217.3 %copy-start.48 = (f32[1536]{0:T(1024)S(1)}, f32[1536]{0:T(1024)}, u32[]{:S(2)}) copy-start(f32[1536]{0:T(1024)} %param.28) | copy-start | bytes 18436
  976.9 217.3 %copy-start.60 = (f32[256]{0:T(256)S(1)}, f32[256]{0:T(256)}, u32[]{:S(2)}) copy-start(f32[256]{0:T(256)} %copy-done.59) | copy-start | bytes 3076
  979.3 216.4 %copy-start.55 = (f32[1536]{0:T(1024)S(1)}, f32[1536]{0:T(1024)}, u32[]{:S(2)}) copy-start(f32[1536]{0:T(1024)} %get-tuple-element.88) | copy-start | bytes 18436
  979.3 257.2 %copy-start.69 = (f32[256]{0:T(256)S(1)}, f32[256]{0:T(256)}, u32[]{:S(2)}) copy-start(f32[256]{0:T(256)} %copy-done.68) | copy-start | bytes 3076
  979.3 257.2 %copy-start.13 = (bf16[256,1536]{1,0:T(8,128)(2,1)S(1)}, bf16[256,1536]{1,0:T(8,128)(2,1)}, u32[]{:S(2)}) copy-start(bf16[256,1536]{1,0:T(8,128)(2,1)} %gather_fusion.3) | copy-start | bytes 2359300
  979.3 257.2 %copy-start.45 = (f32[1536]{0:T(1024)S(1)}, f32[1536]{0:T(1024)}, u32[]{:S(2)}) copy-start(f32[1536]{0:T(1024)} %param.33) | copy-start | bytes 18436
  979.3 257.2 %copy-start.58 = (f32[256]{0:T(256)S(1)}, f32[256]{0:T(256)}, u32[]{:S(2)}) copy-start(f32[256]{0:T(256)} %copy-done.56) | copy-start | bytes 3076
  979.3 257.2 %copy-start.63 = (f32[256]{0:T(256)S(1)}, f32[256]{0:T(256)}, u32[]{:S(2)}) copy-start(f32[256]{0:T(256)} %copy-done.62) | copy-start | bytes 3076
  (37 other events, 66.2 us)
Sparse Core Ops, SparseCore 0:
  12.7 66.1 all-gather.10
  81.4 22.6 all-gather.12
  106.6 24.1 all-gather.14
  135.7 60.2 reduce-scatter.11
  197.4 63.5 all-gather.18
  262.4 62.1 all-gather.16
  327.1 70.7 all-gather.20
  400.3 72.1 all-gather.22
  475.0 72.1 all-gather.24
  641.8 60.2 reduce-scatter.15
  725.3 61.7 all-gather.26
  789.8 58.8 reduce-scatter.13
  854.9 120.5 all-reduce.4
  978.4 34.6 reduce-scatter.23
  1016.0 33.8 reduce-scatter.21
  1053.5 36.7 reduce-scatter.25
  1094.3 36.7 reduce-scatter.19
  1133.9 60.2 reduce-scatter.17
  1197.6 93.0 reduce-scatter.31
  1294.1 92.3 reduce-scatter.29
  1390.0 92.3 reduce-scatter.27

commit v2 on v1

--- a/solution.py
+++ b/solution.py
@@ -11,6 +11,7 @@
 HD = 64
 E = 16
 CAP = 256
+MESH = pl.DeviceIdType.MESH
 
 
 EPS = 1e-05
@@ -56,15 +57,8 @@
     pair = expert_ids[:, 0] * E + expert_ids[:, 1]
     hits = arrival[:, None] == jnp.arange(block, dtype=jnp.int32)[None, :]
     code = jnp.sum(jnp.where(hits, pair[:, None], 0), axis=0)
-    order = jnp.sum(jnp.where(home[:, None] == jnp.arange(shard, dtype=jnp.int32)[None, :],
-                              jnp.arange(shard, dtype=jnp.int32)[:, None], 0), axis=0)
     counts = jnp.sum((expert_ids.reshape(-1)[:, None] == jnp.arange(E, dtype=jnp.int32)[None, :]).astype(jnp.int32), axis=0)
-    return (home, order, code[None, :], counts)
-
-
-def to_dealt(values, order):
-    moved = lax.all_to_all(values[order], "dp", split_axis=0, concat_axis=0, tiled=True)
-    return full_rows(moved)
+    return (home, code[None, :], counts)
 
 
 def to_home(stretch, home):
@@ -95,26 +89,16 @@
     return (query_rows, key_rows, jnp.where(visible(segment, start, finish), scores, -1e30))
 
 
-def attend_forward(query, key, value, segment):
+def attend_totals(query, key, segment):
     rows = query.shape[0]
     heads_kv = key.shape[1] // HD
     share = query.shape[1] // key.shape[1]
     block = min(512, rows)
-    outputs, totals = ([], [])
+    totals = []
     for start in range(0, rows, block):
-        finish = start + block
-        query_rows, key_rows, masked = block_scores(
-            query, key, segment, start, block, heads_kv, share
-        )
-        value_rows = value[:finish].reshape(finish, heads_kv, HD)
-        highest = jnp.max(masked, axis=-1, keepdims=True)
-        raised = jnp.exp(masked - highest)
-        total = jnp.sum(raised, axis=-1, keepdims=True)
-        probs = (raised / total).astype(jnp.bfloat16)
-        mixed = jnp.einsum("gsqt,tgd->qgsd", probs, value_rows, preferred_element_type=jnp.float32)
-        outputs.append(mixed.reshape(block, -1))
-        totals.append(highest + jnp.log(total))
-    return (jnp.concatenate(outputs, axis=0), totals)
+        _, _, masked = block_scores(query, key, segment, start, block, heads_kv, share)
+        totals.append(jax.nn.logsumexp(masked, axis=-1, keepdims=True))
+    return totals
 
 
 def attend_back(query, key, value, segment, grad_mix, totals):
@@ -307,6 +291,446 @@
     )(counts, code, router, second, grad, gate_w, up_w, down_w)
 
 
+class CubeGather:
+    def __init__(self, groups, chunks, block, place, sems):
+        self.bits = groups.bit_length() - 2
+        self.chunks, self.block, self.place = chunks, block, place
+        self.out_sem, self.in_sem, self.pair_out, self.pair_in, self.own_sem = sems
+        self.me = lax.axis_index("dp")
+        self.waits = []
+
+    def flip(self, index, mask):
+        for bit in range(self.bits + 1):
+            if mask >> bit & 1:
+                index = index + (1 << bit) * (1 - 2 * ((index // (1 << bit)) % 2))
+        return index
+
+    def send(self, chunk, have, bit, source):
+        slot = have * self.bits + bit
+        copy = pltpu.make_async_remote_copy(
+            src_ref=source,
+            dst_ref=self.place(chunk, self.flip(self.me, have << 1)),
+            send_sem=self.out_sem.at[chunk, slot],
+            recv_sem=self.in_sem.at[chunk, have ^ (1 << bit)],
+            device_id={"dp": self.flip(self.me, 2 << bit)},
+            device_id_type=MESH,
+        )
+        copy.start()
+        self.waits.append(copy.wait_send)
+
+    def pair(self, chunk, have, source):
+        copy = pltpu.make_async_remote_copy(
+            src_ref=source,
+            dst_ref=self.place(chunk, self.flip(self.me, have << 1)),
+            send_sem=self.pair_out.at[chunk, have],
+            recv_sem=self.pair_in.at[chunk, have],
+            device_id={"dp": self.flip(self.me, 1)},
+            device_id_type=MESH,
+        )
+        copy.start()
+        self.waits.append(copy.wait_send)
+
+    def arrived(self, chunk, have, sem):
+        ref = self.place(chunk, self.flip(self.me, have))
+        pltpu.make_async_copy(ref, ref, sem).wait()
+
+    def begin(self):
+        for chunk in range(self.chunks):
+            for step in range(self.bits):
+                self.send(chunk, 0, (chunk + step) % self.bits, self.block(chunk))
+        for chunk in range(self.chunks):
+            self.pair(chunk, 0, self.block(chunk))
+            copy = pltpu.make_async_copy(self.block(chunk), self.place(chunk, self.me), self.own_sem.at[chunk])
+            copy.start()
+            self.waits.append(copy.wait)
+
+    def events(self):
+        found = []
+        for have in range(1, 1 << self.bits):
+            for chunk in range(self.chunks):
+                order = [(chunk + step) % self.bits for step in range(self.bits)]
+                last = max(step for step, bit in enumerate(order) if have >> bit & 1)
+                found.append((bin(have).count("1"), chunk, have, order[last + 1 :]))
+
+        def event(chunk, have, later):
+            self.arrived(chunk, have << 1, self.in_sem.at[chunk, have])
+            source = self.place(chunk, self.flip(self.me, have << 1))
+            for bit in later:
+                self.send(chunk, have, bit, source)
+            self.pair(chunk, have, source)
+
+        return [functools.partial(event, *item[1:]) for item in sorted(found)]
+
+    def finish(self):
+        for chunk in range(self.chunks):
+            for have in range(1 << self.bits):
+                self.arrived(chunk, (have << 1) + 1, self.pair_in.at[chunk, have])
+        for wait in self.waits:
+            wait()
+
+
+def cube_sems(groups, chunks):
+    bits = groups.bit_length() - 2
+    dma = pltpu.SemaphoreType.DMA
+    return [
+        dma((chunks, bits << bits)),
+        dma((chunks, 1 << bits)),
+        dma((chunks, 1 << bits)),
+        dma((chunks, 1 << bits)),
+        dma((chunks,)),
+    ]
+
+
+class LineGather:
+    def __init__(self, parts, chunks, held, out_sem, in_sem):
+        self.parts, self.chunks, self.held = parts, chunks, held
+        self.out_sem, self.in_sem = out_sem, in_sem
+        self.me = lax.axis_index("mp")
+        self.rows = held.shape[1] // chunks
+
+    def copy(self, origin, chunk, way):
+        piece = self.held.at[origin, pl.ds(chunk * self.rows, self.rows)]
+        return pltpu.make_async_remote_copy(
+            src_ref=piece,
+            dst_ref=piece,
+            send_sem=self.out_sem.at[way, origin, chunk],
+            recv_sem=self.in_sem.at[origin, chunk],
+            device_id={"mp": self.me + 2 * way - 1},
+            device_id_type=MESH,
+        )
+
+    def on_way(self, way, do):
+        pl.when(self.me > 0 if way == 0 else self.me < self.parts - 1)(do)
+
+    def begin(self, chunk):
+        for way in (0, 1):
+            self.on_way(way, lambda way=way: self.copy(self.me, chunk, way).start())
+
+    def step(self, distance, way, chunk):
+        origin = self.me + distance * (1 - 2 * way)
+
+        @pl.when((origin >= 0) & (origin < self.parts))
+        def _():
+            self.copy(origin, chunk, way).wait_recv()
+            self.on_way(way, lambda: self.copy(origin, chunk, way).start())
+
+    def from_side(self, distance, way, do):
+        origin = self.me + distance * (1 - 2 * way)
+        pl.when((origin >= 0) & (origin < self.parts))(lambda: do(origin))
+
+    def finish(self):
+        for way in (0, 1):
+            for distance in range(self.parts):
+                origin = self.me + distance * (1 - 2 * way)
+                here = (origin >= 0) & (origin < self.parts)
+                there = (self.me > 0) if way == 0 else (self.me < self.parts - 1)
+
+                @pl.when(here & there)
+                def _():
+                    for chunk in range(self.chunks):
+                        self.copy(origin, chunk, way).wait_send()
+
+
+class LineSum:
+    def __init__(self, parts, chunks, held, come, out_sem, in_sem):
+        self.parts, self.chunks, self.held, self.come = parts, chunks, held, come
+        self.out_sem, self.in_sem = out_sem, in_sem
+        self.me = lax.axis_index("mp")
+        self.rows = held.shape[1] // chunks
+
+    def copy(self, target, chunk):
+        way = (target > self.me).astype(jnp.int32)
+        span = pl.ds(chunk * self.rows, self.rows)
+        return pltpu.make_async_remote_copy(
+            src_ref=self.held.at[target, span],
+            dst_ref=self.come.at[way, target, span],
+            send_sem=self.out_sem.at[target, chunk],
+            recv_sem=self.in_sem.at[way, target, chunk],
+            device_id={"mp": self.me + 2 * way - 1},
+            device_id_type=MESH,
+        )
+
+    def come_in(self, way, target, chunk):
+        piece = self.come.at[way, target, pl.ds(chunk * self.rows, self.rows)]
+        pltpu.make_async_copy(piece, piece, self.in_sem.at[way, target, chunk]).wait()
+
+    def begin(self, target):
+        end = ((target < self.me) & (self.me == self.parts - 1)) | ((target > self.me) & (self.me == 0))
+
+        @pl.when(end)
+        def _():
+            for chunk in range(self.chunks):
+                self.copy(target, chunk).start()
+
+    def relay(self, target, chunk):
+        between = ((target < self.me) & (self.me < self.parts - 1)) | ((target > self.me) & (self.me > 0))
+
+        @pl.when(between)
+        def _():
+            way = (target > self.me).astype(jnp.int32)
+            span = pl.ds(chunk * self.rows, self.rows)
+            self.come_in(way, target, chunk)
+            self.held[target, span, :] = self.held[target, span, :] + self.come[way, target, span, :]
+            self.copy(target, chunk).start()
+
+    def total(self, chunk, out):
+        span = pl.ds(chunk * self.rows, self.rows)
+        out[span, :] = self.held[self.me, span, :].astype(jnp.float32)
+        for way, there in ((0, self.me < self.parts - 1), (1, self.me > 0)):
+
+            @pl.when(there)
+            def _():
+                self.come_in(way, self.me, chunk)
+                out[span, :] = out[span, :] + self.come[way, self.me, span, :].astype(jnp.float32)
+
+    def finish(self):
+        for target in range(self.parts):
+
+            @pl.when(self.me != target)
+            def _():
+                for chunk in range(self.chunks):
+                    self.copy(target, chunk).wait_send()
+
+
+class Exchange:
+    def __init__(self, groups, source, held, out_sem, in_sem):
+        self.groups, self.source, self.held = groups, source, held
+        self.out_sem, self.in_sem = out_sem, in_sem
+        self.me = lax.axis_index("dp")
+        self.rows = source.shape[0] // groups
+
+    def copy(self, turn):
+        peer = lax.rem(self.me + turn, self.groups)
+        return pltpu.make_async_remote_copy(
+            src_ref=self.source.at[pl.ds(peer * self.rows, self.rows)],
+            dst_ref=self.held.at[pl.ds(self.me * self.rows, self.rows)],
+            send_sem=self.out_sem.at[turn],
+            recv_sem=self.in_sem.at[turn],
+            device_id={"dp": peer},
+            device_id_type=MESH,
+        )
+
+    def begin(self):
+        for turn in range(1, self.groups):
+            self.copy(turn).start()
+        span = pl.ds(pl.multiple_of(self.me * self.rows, self.rows), self.rows)
+        self.held[span, :] = self.source[span, :]
+
+    def arrive(self):
+        for turn in range(1, self.groups):
+            self.copy(turn).wait_recv()
+
+    def finish(self):
+        for turn in range(1, self.groups):
+            self.copy(turn).wait_send()
+
+
+def row_type(rows):
+    return jnp.bfloat16 if rows % 16 == 0 else jnp.float32
+
+
+def greet(groups, parts):
+    barrier = pltpu.get_barrier_semaphore()
+    me, part = lax.axis_index("dp"), lax.axis_index("mp")
+    for turn in range(1, groups):
+        pl.semaphore_signal(
+            barrier, inc=1, device_id={"dp": lax.rem(me + turn, groups)}, device_id_type=MESH
+        )
+    for step, there in ((-1, part > 0), (1, part < parts - 1)):
+
+        @pl.when(there)
+        def _():
+            pl.semaphore_signal(barrier, inc=1, device_id={"mp": part + step}, device_id_type=MESH)
+
+    sides = (part > 0).astype(jnp.int32) + (part < parts - 1).astype(jnp.int32)
+    pl.semaphore_wait(barrier, groups - 1 + sides)
+
+
+def scale_of(values):
+    return lax.rsqrt(jnp.mean(values * values, axis=1, keepdims=True) + EPS)
+
+
+def sorting(home, rows):
+    place = lax.broadcasted_iota(jnp.int32, (rows, rows), 0)
+    return jnp.where(place == home, 1.0, 0.0).astype(jnp.bfloat16)
+
+
+def bias_of(seg_row, seg_col, start, low, stop):
+    span = stop - start
+    query = lax.broadcasted_iota(jnp.int32, (span, stop - low), 0) + start
+    key = lax.broadcasted_iota(jnp.int32, (span, stop - low), 1) + low
+    same = seg_col[start:stop, :] == seg_row[:, low:stop]
+    return jnp.where(same & (key <= query), 0.0, -1e30)
+
+
+def forward_kernel(groups, parts, heads, heads_kv, home, seg_row, seg_col, attn_gain, moe_gain, tokens, out_grad, wpack,
+                   middle, first_out, qkv_out, mix_out, weights_out, second_out, grad_out,
+                   first, second, grad, weights, qkv, mix, part, come, bias, sorted_second, sorted_grad, dealt_second, dealt_grad,
+                   gather_sems, line_out, line_in, sum_out, sum_in, deal_out, deal_in, save_sem):
+    low = jnp.bfloat16
+    shard, width = tokens.shape
+    me, place = lax.axis_index("dp"), lax.axis_index("mp")
+    share = heads // heads_kv
+    block = wpack.shape[0]
+    cut = block // 2
+    saves = []
+
+    def save(number, source, target):
+        copy = pltpu.make_async_copy(source, target, save_sem.at[number])
+        copy.start()
+        saves.append(copy)
+
+    greet(groups, parts)
+    gather = CubeGather(
+        groups,
+        2,
+        lambda chunk: wpack.at[pl.ds(chunk * cut, cut)],
+        lambda chunk, owner: weights.at[pl.ds(owner * block + chunk * cut, cut)],
+        gather_sems,
+    )
+    gather.begin()
+    values = tokens[...]
+    first[place] = (values * scale_of(values) * attn_gain[...]).astype(low)
+    lines = [LineGather(parts, 2, held, line_out.at[n], line_in.at[n]) for n, held in enumerate((first, grad, second))]
+    for chunk in range(2):
+        lines[0].begin(chunk)
+    sort = sorting(home[...], shard)
+    sorted_grad[...] = mm(sort, out_grad[...].astype(low)).astype(sorted_grad.dtype)
+    for event in gather.events():
+        event()
+    deal_grad = Exchange(groups, sorted_grad, dealt_grad, deal_out.at[0], deal_in.at[0])
+    deal_grad.begin()
+    gather.finish()
+    save(0, weights, weights_out)
+
+    def project(origin):
+        result = mm(first[origin], weights[:, : (heads + 2 * heads_kv) * HD])
+        span = pl.ds(pl.multiple_of(origin * shard, shard), shard)
+        for head in range(heads + 2 * heads_kv):
+            qkv[head, span, :] = result[:, head * HD : (head + 1) * HD].astype(low)
+
+    project(place)
+    for distance in range(1, parts):
+        for chunk in range(2):
+            for way in (0, 1):
+                lines[0].step(distance, way, chunk)
+        for way in (0, 1):
+            lines[0].from_side(distance, way, project)
+    deal_grad.arrive()
+    grad[place] = dealt_grad[...].astype(low)
+    for chunk in range(2):
+        lines[1].begin(chunk)
+    save(1, first, first_out)
+    save(2, qkv, qkv_out)
+
+    sums = LineSum(parts, 2, part, come, sum_out, sum_in)
+    order = sorted(range(parts), key=lambda t: (-abs(2 * t - parts + 1), -t))
+    reach = -(-512 // shard)
+    for number, target in enumerate(order):
+        start, stop = target * shard, (target + 1) * shard
+        bottom = max(0, target - reach) * shard
+        bias[:, : stop - bottom] = bias_of(seg_row, seg_col, start, bottom, stop)
+
+        def attend(head, _):
+            group = head // share
+            keys = qkv[heads + group, bottom:stop, :]
+            scores = mm(qkv[head, start:stop, :], keys, NT) * HD**-0.5 + bias[:, : stop - bottom]
+            raised = jnp.exp(scores - jnp.max(scores, axis=1, keepdims=True))
+            probs = (raised * (1.0 / jnp.sum(raised, axis=1, keepdims=True))).astype(low)
+            mix[head, start:stop, :] = mm(probs, qkv[heads + heads_kv + group, bottom:stop, :]).astype(low)
+            return 0
+
+        lax.fori_loop(0, heads, attend, 0)
+        flat = jnp.concatenate([mix[head, start:stop, :] for head in range(heads)], axis=1)
+        part[target] = mm(flat, weights[:, (heads + 2 * heads_kv) * HD :], NT).astype(low)
+        sums.begin(target)
+        if number < parts - 1:
+            for chunk in range(2):
+                for way in (0, 1):
+                    lines[1].step(number + 1, way, chunk)
+    save(3, mix, mix_out)
+    for target in order:
+        for chunk in range(2):
+            sums.relay(target, chunk)
+    for chunk in range(2):
+        sums.total(chunk, middle)
+    values = tokens[...] + middle[...]
+    middle[...] = values
+    normed = (values * scale_of(values) * moe_gain[...]).astype(low)
+    sorted_second[...] = mm(sort, normed).astype(sorted_second.dtype)
+    deal = Exchange(groups, sorted_second, dealt_second, deal_out.at[1], deal_in.at[1])
+    deal.begin()
+    save(4, grad, grad_out)
+    deal.arrive()
+    second[place] = dealt_second[...].astype(low)
+    for chunk in range(2):
+        lines[2].begin(chunk)
+    for distance in range(1, parts):
+        for chunk in range(2):
+            for way in (0, 1):
+                lines[2].step(distance, way, chunk)
+    save(5, second, second_out)
+    for line in lines:
+        line.finish()
+    sums.finish()
+    deal_grad.finish()
+    deal.finish()
+    for copy in saves:
+        copy.wait()
+
+
+def forward(groups, parts, home, seg, attn_gain, moe_gain, tokens, out_grad, wpack, heads, heads_kv):
+    shard, width = tokens.shape
+    rows = shard * parts
+    low = jnp.bfloat16
+    slots = heads + 2 * heads_kv
+    columns = wpack.shape[1]
+    vmem = pl.BlockSpec(memory_space=pltpu.VMEM)
+    hbm = pl.BlockSpec(memory_space=pl.ANY)
+    dma = pltpu.SemaphoreType.DMA
+    held = lambda: pltpu.VMEM((parts, shard, width), low)
+    return pl.pallas_call(
+        functools.partial(forward_kernel, groups, parts, heads, heads_kv),
+        in_specs=[vmem] * 7 + [hbm],
+        out_specs=[vmem] + [hbm] * 6,
+        out_shape=[
+            jax.ShapeDtypeStruct((shard, width), jnp.float32),
+            jax.ShapeDtypeStruct((parts, shard, width), low),
+            jax.ShapeDtypeStruct((slots, rows, HD), low),
+            jax.ShapeDtypeStruct((heads, rows, HD), low),
+            jax.ShapeDtypeStruct((width, columns), low),
+            jax.ShapeDtypeStruct((parts, shard, width), low),
+            jax.ShapeDtypeStruct((parts, shard, width), low),
+        ],
+        scratch_shapes=[
+            held(),
+            held(),
+            held(),
+            pltpu.VMEM((width, columns), low),
+            pltpu.VMEM((slots, rows, HD), low),
+            pltpu.VMEM((heads, rows, HD), low),
+            held(),
+            pltpu.VMEM((2, parts, shard, width), low),
+            pltpu.VMEM((shard, shard * (1 - (-512 // shard))), jnp.float32),
+            *[pltpu.VMEM((shard, width), row_type(shard // groups))] * 4,
+            cube_sems(groups, 2),
+            dma((3, 2, parts, 2)),
+            dma((3, parts, 2)),
+            dma((parts, 2)),
+            dma((2, parts, 2)),
+            dma((2, groups)),
+            dma((2, groups)),
+            dma((6,)),
+        ],
+        compiler_params=pltpu.CompilerParams(
+            collective_id=0, has_side_effects=True, vmem_limit_bytes=56 * 2**20
+        ),
+        cost_estimate=pl.CostEstimate(
+            flops=12 * rows * width * columns, bytes_accessed=60 * 2**20, transcendentals=rows * rows * heads
+        ),
+    )(home, seg[None, :], seg[:, None], attn_gain[None, :], moe_gain[None, :], tokens, out_grad, wpack)
+
+
 def body(
     tokens,
     attn_gain,
@@ -324,36 +748,42 @@
     expert_ids,
     out_grad,
 ):
-    rows = tokens.shape[0] * lax.axis_size("mp")
+    groups, parts = lax.axis_size("dp"), lax.axis_size("mp")
+    rows = tokens.shape[0] * parts
     low_type = jnp.bfloat16
-    query_w, key_w, value_w, out_w, router_w, gate_w, up_w, down_w = (
-        lax.all_gather(w_query.astype(low_type), "dp", axis=0, tiled=True),
-        lax.all_gather(w_key.astype(low_type), "dp", axis=0, tiled=True),
-        lax.all_gather(w_value.astype(low_type), "dp", axis=0, tiled=True),
-        lax.all_gather(w_out.astype(low_type), "dp", axis=1, tiled=True),
+    heads, heads_kv = w_query.shape[1] // HD, w_key.shape[1] // HD
+    wpack = jnp.concatenate([w_query, w_key, w_value, w_out.T], axis=1).astype(low_type)
+    router_w, gate_w, up_w, down_w = (
         lax.all_gather(w_router.astype(low_type), "dp", axis=0, tiled=True),
         lax.all_gather(w_gate.astype(low_type), "dp", axis=1, tiled=True),
         lax.all_gather(w_up.astype(low_type), "dp", axis=1, tiled=True),
         lax.all_gather(w_down.astype(low_type), "dp", axis=0, tiled=True),
     )
-    home, order, code, counts = deal_tables(deal_order, expert_ids, rows)
+    home, code, counts = deal_tables(deal_order, expert_ids, rows)
     segment = segment_of(seq_lengths[0], rows)
-    scale_one, normed_one = norm_apply(tokens, attn_gain)
-    first_full = full_rows(normed_one)
-    query = jnp.dot(first_full, query_w, preferred_element_type=jnp.float32).astype(low_type)
-    key = jnp.dot(first_full, key_w, preferred_element_type=jnp.float32).astype(low_type)
-    value = jnp.dot(first_full, value_w, preferred_element_type=jnp.float32).astype(low_type)
-    mix, totals = attend_forward(query, key, value, segment)
-    mix = mix.astype(low_type)
-    middle = tokens + row_share(jnp.dot(mix, out_w, preferred_element_type=jnp.float32).astype(low_type)).astype(jnp.float32)
-    scale_two, normed_two = norm_apply(middle, moe_gain)
-    second_full = to_dealt(normed_two, order)
-    grad_full = to_dealt(out_grad.astype(low_type), order)
+    middle, first_full, qkv, mix, weights, second_full, grad_full = forward(
+        groups, parts, home[None, :], segment, attn_gain, moe_gain, tokens, out_grad, wpack, heads, heads_kv
+    )
+    second_full, grad_full = second_full.reshape(rows, D), grad_full.reshape(rows, D)
     mixed, back, grad_gate_all, grad_up_all, grad_down_all, grad_router = experts(
         second_full, grad_full, code, counts, router_w.T, gate_w, up_w, down_w
     )
     grad_normed_two = to_home(row_share(back), home)
     block_out = middle + to_home(row_share(mixed), home)
+    columns = heads * HD
+    first_full = first_full.reshape(rows, D)
+    query_w, key_w, value_w, out_w = (
+        weights[:, :columns],
+        weights[:, columns : columns + heads_kv * HD],
+        weights[:, columns + heads_kv * HD : columns + 2 * heads_kv * HD],
+        weights[:, columns + 2 * heads_kv * HD :].T,
+    )
+    flat = lambda items: jnp.transpose(items, (1, 0, 2)).reshape(rows, -1)
+    query, key, value = flat(qkv[:heads]), flat(qkv[heads : heads + heads_kv]), flat(qkv[heads + heads_kv :])
+    mix = flat(mix)
+    totals = attend_totals(query, key, segment)
+    scale_one = lax.rsqrt(jnp.mean(tokens * tokens, axis=1) + EPS)
+    scale_two = lax.rsqrt(jnp.mean(middle * middle, axis=1) + EPS)
     grad_middle_norm, grad_moe_gain = norm_back(middle, moe_gain, scale_two, grad_normed_two)
     grad_middle = out_grad + grad_middle_norm
     grad_attn_full = full_rows(grad_middle.astype(low_type))

time: 1500 us -> 1220 us (0.81)
  waiting for transfers between devices: 1100 us -> 682 us
  Pallas kernels: 94.5 us -> 321 us
  blocking collectives: 102 us -> 51.4 us
  matrix products: 69 us -> 51.6 us
    pallas_call x0 -> x1, Pallas kernels: none -> 228 us  [forward(): pl.pallas_call(functools.partial(forward_kernel, groups, parts, heads, he...]
    all_gather x4 -> x1, waiting for transfers between devices: 186 us -> 49.7 us  [full_rows(): return lax.all_gather(values, 'mp', axis=0, tiled=True)]
    all_gather x1, waiting for transfers between devices: 74.6 us -> 0.02 us  [body(): lax.all_gather(w_up.astype(low_type), 'dp', axis=1, tiled=True)]
    all_gather x1, waiting for transfers between devices: 74.6 us -> 0.02 us  [body(): lax.all_gather(w_down.astype(low_type), 'dp', axis=0, tiled=True)]
    all_gather x1, waiting for transfers between devices: 73.3 us -> 0.02 us  [body(): lax.all_gather(w_gate.astype(low_type), 'dp', axis=1, tiled=True)]
    reduce_scatter x1, waiting for transfers between devices: 92.5 us -> 49.8 us  [body(): lax.psum_scatter(grad_gate_all.astype(jnp.bfloat16), 'dp', scatter_dimens...]
    reduce_scatter x1, waiting for transfers between devices: 49.8 us -> 92.4 us  [body(): lax.psum_scatter(grad_down_all.astype(jnp.bfloat16), 'dp', scatter_dimens...]
    reduce_scatter x4 -> x3, waiting for transfers between devices: 158 us -> 124 us  [row_share(): lax.psum_scatter(partial_value, 'mp', scatter_dimension=0, tiled=True)]
  transfers between devices with their start and end apart: 23 -> 17, of which waited for: 21 -> 12; matrix products, arithmetic and copies ran while one was open for 9% -> 9% of each run, Pallas kernels for 0% -> 19%
where the time goes in v2:
time: 1220 us; the launch traced here: 1210 us
  waiting for transfers between devices  682 us (56%)
  Pallas kernels  321 us (26%)
  other arithmetic  60.3 us (5%)
  matrix products  51.6 us (4%)
  blocking collectives  51.4 us (4%)
  local copies, waits for them, and re-layouts  19.5 us (2%)
  between operations  14.9 us (1%)
    pallas_call x1, Pallas kernels, forward(): pl.pallas_call(functools.partial(forward_kernel, groups, parts, heads, he...  228 us
    reduce_scatter x3, waiting for transfers between devices, row_share(): lax.psum_scatter(partial_value, 'mp', scatter_dimension=0, tiled=True)  124 us
    psum x1, waiting for transfers between devices, body(): lax.psum((grad_attn_gain, grad_moe_gain, grad_router), ('dp', 'mp'))  112 us
    pallas_call x1, Pallas kernels, experts(): pl.pallas_call(expert_kernel, grid_spec=pltpu.PrefetchScalarGridSpec(num_...  92.5 us
    reduce_scatter x1, waiting for transfers between devices, body(): lax.psum_scatter(grad_up_all.astype(jnp.bfloat16), 'dp', scatter_dimensio...  92.4 us
    reduce_scatter x1, waiting for transfers between devices, body(): lax.psum_scatter(grad_down_all.astype(jnp.bfloat16), 'dp', scatter_dimens...  92.4 us
    reduce_scatter x1, waiting for transfers between devices, body(): lax.psum_scatter(grad_gate_all.astype(jnp.bfloat16), 'dp', scatter_dimens...  49.8 us
    all_gather x1, waiting for transfers between devices, full_rows(): return lax.all_gather(values, 'mp', axis=0, tiled=True)  49.7 us
  transfers between devices with their start and end apart: 17, of which 12 were waited for; matrix products, arithmetic and copies ran while one was open for 9% of the time, Pallas kernels for 19%

profile of v2, /device:TPU:0, one launch (start us, length us, event | category | flops | bytes accessed | tf_op | source)
XLA Modules:
  0.0 1209.3 jit_solution(17535181202195508972)
XLA Ops:
  7.2 3.4 convert_element_type.110
  10.7 1.3 convert_element_type.108
  12.2 3.3 convert_element_type.109
  15.9 1.0 copy.84.seg_col
  18.7 10.7 all-gather
  30.9 3.7 select_reduce_fusion
  36.6 1.3 select_reduce_fusion.1
  37.8 228.2 %shard_map.248 = (f32[256,1536]{1,0:T(8,128)}, bf16[4,256,1536]{2,1,0:T(8,128)(2,1)}, bf16[10,1024,64]{2,1,0:T(8,128)(2,1)}, bf16[6,1024,64]{2,1,0:T(8,128)(2,1)...) custom-call(s32[1,256]{1,0:T(1,128)} %bitcast.226, ...), custom_call_target="tpu_custom_call" | custom-call | flops 19327352832 | bytes 62914560 | tf_op jit(solution)/shard_map/pallas_call | solution.py:692
  266.1 92.5 %shard_map.249 = (bf16[1024,1536]{1,0:T(8,128)(2,1)}, bf16[1024,1536]{1,0:T(8,128)(2,1)}, bf16[16,1536,256]{2,1,0:T(8,128)(2,1)}, bf16[16,1536,256]{2,1,0:T(8,12...) custom-call(s32[16]{0:T(128)} %convert_reduce_fusion.2.counts, s32[1,1024]{1,0:T(1,128)} %bitcast.225, ...), custom_call_target="tpu_custom_call" | custom-call | flops 80530636800 | bytes 88080384 | tf_op jit(solution)/shard_map/pallas_call | solution.py:252
  358.6 62.4 %reduce-scatter.13.cloned.1.call-done = bf16[256,1536]{1,0:T(8,128)(2,1)} async-done(((bf16[1024,1536]{1,0:T(8,128)(2,1)}), bf16[256,1536]{1,0:T(8,128)(2,1)}) %reduce-scatter.13.cloned.1.call-update) | async-done | bytes 786448 | tf_op jit(solution)/shard_map/reduce_scatter | solution.py:25
  421.0 3.6 all-to-all-start.1
  424.9 12.3 %all-to-all-done.1 = bf16[8,32,1536]{2,1,0:T(8,128)(2,1)S(1)} async-done(((bf16[8,32,1536]{2,1,0:T(8,128)(2,1)}), bf16[8,32,1536]{2,1,0:T(8,128)(2,1)S(1)}, u32[]{:S(2)}, u32[]{:S(2)}) %all-to-all-start.1) | async-done | bytes 786464 | tf_op jit(solution)/shard_map/all_to_all | solution.py:65
  437.2 1.3 gather_fusion.1
  439.1 1.1 copy-done.17
  440.2 1.3 fusion.84
  442.4 0.9 copy-done.16
  443.3 0.9 slice_bitcast_fusion.2
  444.9 1.2 fusion.12
  446.6 2.3 fusion.4
  449.0 1.3 exponential_reduce_fusion.1
  450.4 2.6 exponential_reduce_fusion
  453.7 49.7 %all-gather.12.cloned.1.call-done = bf16[1024,1536]{1,0:T(8,128)(2,1)} async-done(((bf16[256,1536]{1,0:T(8,128)(2,1)}), bf16[1024,1536]{1,0:T(8,128)(2,1)}) %all-gather.12.cloned.1.call-update) | async-done | bytes 3145744 | tf_op jit(solution)/shard_map/all_gather | solution.py:21
  503.4 3.8 convolution_convert_fusion.4
  507.5 1.6 fusion.49
  509.9 1.7 slice-done.2
  511.7 6.4 fusion
  518.1 3.3 fusion.42
  521.4 4.4 fusion.5
  525.8 4.7 fusion.7
  530.6 1.8 fusion.53
  532.4 1.8 convolution_convert_fusion.2
  534.7 10.2 fusion.2
  545.0 2.6 copy-done.3
  547.6 2.0 fusion.45
  549.7 1.8 convolution_convert_fusion.3
  551.5 5.0 fusion.32
  556.6 1.8 fusion.31
  559.2 2.9 convolution_convert_fusion.1
  562.8 4.7 convolution_convert_fusion
  567.8 2.2 fusion.64
  570.0 1.8 fusion.46
  571.9 2.7 add_convert_fusion
  576.6 3.6 all-to-all-start
  580.3 111.5 %all-reduce.5.cloned.1.call-done = f32[16,1536]{1,0:T(8,128)} async-done(((f32[16,1536]{1,0:T(8,128)}), f32[16,1536]{1,0:T(8,128)}) %all-reduce.5.cloned.1.call-update) | async-done | bytes 98320 | tf_op jit(solution)/shard_map/psum | solution.py:813
  691.8 1.4 dynamic-slice_bitcast_fusion
  693.3 2.1 gather_fusion
  695.4 34.2 %reduce-scatter.21.cloned.1.call-done = bf16[192,128]{1,0:T(8,128)(2,1)} async-done(((bf16[1536,128]{1,0:T(8,128)(2,1)}), bf16[192,128]{1,0:T(8,128)(2,1)}) %reduce-scatter.21.cloned.1.call-update) | async-done | bytes 49168 | tf_op jit(solution)/shard_map/reduce_scatter | solution.py:825
  729.6 1.4 convert_element_type.130
  731.1 35.5 %reduce-scatter.19.cloned.1.call-done = bf16[192,128]{1,0:T(8,128)(2,1)} async-done(((bf16[1536,128]{1,0:T(8,128)(2,1)}), bf16[192,128]{1,0:T(8,128)(2,1)}) %reduce-scatter.19.cloned.1.call-update) | async-done | bytes 49168 | tf_op jit(solution)/shard_map/reduce_scatter | solution.py:822
  766.6 1.4 convert_element_type.128
  768.0 39.0 %reduce-scatter.17.cloned.1.call-done = bf16[192,384]{1,0:T(8,128)(2,1)} async-done(((bf16[1536,384]{1,0:T(8,128)(2,1)}), bf16[192,384]{1,0:T(8,128)(2,1)}) %reduce-scatter.17.cloned.1.call-update) | async-done | bytes 147472 | tf_op jit(solution)/shard_map/reduce_scatter | solution.py:819
  807.0 1.6 convert_element_type.126
  808.7 39.3 %reduce-scatter.23.cloned.1.call-done = bf16[384,192]{0,1:T(8,128)(2,1)} async-done(((bf16[384,1536]{0,1:T(8,128)(2,1)}), bf16[384,192]{0,1:T(8,128)(2,1)}) %reduce-scatter.23.cloned.1.call-update) | async-done | bytes 147472 | tf_op jit(solution)/shard_map/reduce_scatter | solution.py:828
  848.0 1.6 convert_element_type.132
  849.6 61.3 %reduce-scatter.15.cloned.1.call-done = bf16[256,1536]{1,0:T(8,128)(2,1)} async-done(((bf16[1024,1536]{1,0:T(8,128)(2,1)}), bf16[256,1536]{1,0:T(8,128)(2,1)}) %reduce-scatter.15.cloned.1.call-update) | async-done | bytes 786448 | tf_op jit(solution)/shard_map/reduce_scatter | solution.py:25
  911.0 1.6 fusion.30
  912.6 40.7 %all-reduce.2 = (f32[1536]{0:T(1024)}, f32[1536]{0:T(1024)}) all-reduce(f32[1536]{0:T(1024)S(1)} %get-tuple-element.104, f32[1536]{0:T(1024)S(1)} %get-tuple-element.102), channel_id=1, replica_groups=mesh['dp'=8,'mp'=4] {'dp','mp'}, use_global_device_ids=true, to_apply=%region_21.22 | all-reduce | flops 3072 | bytes 24576 | tf_op jit(solution)/shard_map/psum | solution.py:813
  953.3 4.4 fusion.22
  957.7 49.8 %reduce-scatter.25.cloned.1.call-done = bf16[16,192,256]{2,1,0:T(8,128)(2,1)} async-done(((bf16[16,1536,256]{2,1,0:T(8,128)(2,1)}), bf16[16,192,256]{2,1,0:T(8,128)(2,1)}) %reduce-scatter.25.cloned.1.call-update) | async-done | bytes 1572880 | tf_op jit(solution)/shard_map/reduce_scatter | solution.py:831
  1007.6 3.4 convert_element_type.133
  1011.0 92.4 %reduce-scatter.27.cloned.1.call-done = bf16[16,192,256]{2,1,0:T(8,128)(2,1)} async-done(((bf16[16,1536,256]{2,1,0:T(8,128)(2,1)}), bf16[16,192,256]{2,1,0:T(8,128)(2,1)}) %reduce-scatter.27.cloned.1.call-update) | async-done | bytes 1572880 | tf_op jit(solution)/shard_map/reduce_scatter | solution.py:834
  1103.4 3.4 convert_element_type.134
  1106.8 92.4 %reduce-scatter.29.cloned.1.call-done = bf16[2,256,1536]{2,1,0:T(8,128)(2,1)} async-done(((bf16[16,256,1536]{2,1,0:T(8,128)(2,1)}), bf16[2,256,1536]{2,1,0:T(8,128)(2,1)}) %reduce-scatter.29.cloned.1.call-update) | async-done | bytes 1572880 | tf_op jit(solution)/shard_map/reduce_scatter | solution.py:837
  1199.1 3.5 convert_element_type.135
  (166 shorter events, 15.1 us)
Async XLA Ops:
  7.2 3.5 copy-start.18
  7.2 258.8 %all-gather.10.cloned.1.call-start = ((), (), s32[]{:S(2)}) async-start(), calls=%async_computation.14 | async-start | bytes 14155776 | tf_op jit(solution)/shard_map/all_gather | solution.py:760
  10.6 255.4 %all-gather.6.cloned.1.call-start = ((), (), s32[]{:S(2)}) async-start(), calls=%async_computation.12 | async-start | bytes 14155776 | tf_op jit(solution)/shard_map/all_gather | solution.py:758
  12.0 3.6 copy-start.43
  12.1 4.9 copy-start.30
  12.1 4.9 copy-start.33
  12.1 4.9 copy-start.34
  12.1 4.9 copy-start.35
  12.1 5.5 copy-start.32
  12.1 6.1 copy-start.40
  12.1 254.0 %all-gather.8.cloned.1.call-start = ((), (), s32[]{:S(2)}) async-start(), calls=%async_computation.13 | async-start | bytes 14155776 | tf_op jit(solution)/shard_map/all_gather | solution.py:759
  15.5 3.2 copy-start.41
  15.5 14.7 %copy-start.39 = (s32[8192]{0:T(1024)S(1)}, s32[8192]{0:T(1024)}, u32[]{:S(2)}) copy-start(s32[8192]{0:T(1024)} %param.39) | copy-start | bytes 98308
  15.5 19.7 %copy-start.31 = (f32[384,192]{0,1:T(8,128)S(1)}, f32[384,192]{0,1:T(8,128)}, u32[]{:S(2)}) copy-start(f32[384,192]{0,1:T(8,128)} %param.32) | copy-start | bytes 884740
  15.5 405.5 %reduce-scatter.13.cloned.1.call-start = ((), (), s32[]{:S(2)}) async-start(), calls=%async_computation.16 | async-start | bytes 3932160 | tf_op jit(solution)/shard_map/reduce_scatter | solution.py:25
  15.9 22.0 %copy-start.37 = (s32[1024]{0:T(1024)}, s32[1024]{0:T(1024)S(1)}, u32[]{:S(2)}) copy-start(s32[1024]{0:T(1024)S(1)} %convert_reduce_fusion.3) | copy-start | bytes 12292
  358.6 66.1 %copy-start.42 = (s32[256]{0:T(256)S(1)}, s32[256]{0:T(256)}, u32[]{:S(2)}) copy-start(s32[256]{0:T(256)} %convert_reduce_fusion.1) | copy-start | bytes 3076
  358.6 66.1 %copy-start.5 = (f32[256,1536]{1,0:T(8,128)S(1)}, f32[256,1536]{1,0:T(8,128)}, u32[]{:S(2)}) copy-start(f32[256,1536]{1,0:T(8,128)} %get-tuple-element.89) | copy-start | bytes 4718596
  421.0 16.2 %all-to-all-start.1 = ((bf16[8,32,1536]{2,1,0:T(8,128)(2,1)}), bf16[8,32,1536]{2,1,0:T(8,128)(2,1)S(1)}, u32[]{:S(2)}, u32[]{:S(2)}) async-start(bf16[8,32,1536]{2,1,0:T(8,128)(2,1)} %bitcast.219), calls=%async_computation.3 | async-start | bytes 1572864 | tf_op jit(solution)/shard_map/all_to_all | solution.py:65
  424.6 78.8 %all-gather.12.cloned.1.call-start = ((), (), s32[]{:S(2)}) async-start(), calls=%async_computation.17 | async-start | bytes 3932160 | tf_op jit(solution)/shard_map/all_gather | solution.py:21
  438.5 3.0 copy-start.11
  438.5 1.7 copy-start.17
  441.5 0.7 copy-start.38
  441.5 1.8 copy-start.16
  441.5 135.0 %reduce-scatter.11.cloned.1.call-start = ((), (), s32[]{:S(2)}) async-start(), calls=%async_computation.15 | async-start | bytes 3932160 | tf_op jit(solution)/shard_map/reduce_scatter | solution.py:25
  442.1 249.7 %all-reduce.5.cloned.1.call-start = ((), (), s32[]{:S(2)}) async-start(), calls=%async_computation.23 | async-start | bytes 196608 | tf_op jit(solution)/shard_map/psum | solution.py:813
  444.1 0.8 copy-start.19
  444.3 1.8 copy-start.14
  444.4 2.3 copy-start.12
  446.1 2.9 copy-start.1
  446.6 71.5 %copy-start.4 = (pred[512,1024]{0,1:T(8,128)(4,1)}, pred[512,1024]{0,1:T(8,128)(4,1)S(1)}, u32[]{:S(2)}) copy-start(pred[512,1024]{0,1:T(8,128)(4,1)S(1)} %fusion.16) | copy-start | bytes 1572868
  449.0 4.5 copy-start
  453.5 276.2 %reduce-scatter.21.cloned.1.call-start = ((), (), s32[]{:S(2)}) async-start(), calls=%async_computation.21 | async-start | bytes 442368 | tf_op jit(solution)/shard_map/reduce_scatter | solution.py:825
  503.4 4.1 copy-start.2
  503.4 5.7 slice-start
  503.4 6.5 slice-start.1
  507.5 4.1 slice-start.2
  518.1 3.3 copy-start.26
  521.4 11.0 copy-start.27
  525.8 4.7 copy-start.15
  530.6 1.9 copy-start.7
  534.2 232.3 %reduce-scatter.19.cloned.1.call-start = ((), (), s32[]{:S(2)}) async-start(), calls=%async_computation.20 | async-start | bytes 442368 | tf_op jit(solution)/shard_map/reduce_scatter | solution.py:822
  534.7 12.9 %copy-start.13 = (bf16[512,6,64]{2,0,1:T(8,128)(2,1)S(1)}, bf16[512,6,64]{2,0,1:T(8,128)(2,1)}, u32[]{:S(2)}) copy-start(bf16[512,6,64]{2,0,1:T(8,128)(2,1)} %copy-done.12) | copy-start | bytes 1179652
  534.7 12.9 %copy-start.29 = (f32[512,2,64]{0,2,1:T(8,128)S(1)}, f32[512,2,64]{0,2,1:T(8,128)}, u32[]{:S(2)}) copy-start(f32[512,2,64]{0,2,1:T(8,128)} %fusion.53) | copy-start | bytes 786436
  545.0 2.7 copy-start.3
  547.6 2.0 copy-start.8
  556.5 250.5 %reduce-scatter.17.cloned.1.call-start = ((), (), s32[]{:S(2)}) async-start(), calls=%async_computation.19 | async-start | bytes 1327104 | tf_op jit(solution)/shard_map/reduce_scatter | solution.py:819
  556.6 2.6 copy-start.9
  556.6 2.6 copy-start.20
  558.4 0.8 copy-start.22
  559.2 2.9 copy-start.24
  562.1 285.9 %reduce-scatter.23.cloned.1.call-start = ((), (), s32[]{:S(2)}) async-start(), calls=%async_computation.22 | async-start | bytes 1327104 | tf_op jit(solution)/shard_map/reduce_scatter | solution.py:828
  567.6 2.4 copy-start.21
  567.6 2.4 copy-start.23
  567.6 343.4 %reduce-scatter.15.cloned.1.call-start = ((), (), s32[]{:S(2)}) async-start(), calls=%async_computation.18 | async-start | bytes 3932160 | tf_op jit(solution)/shard_map/reduce_scatter | solution.py:25
  567.8 2.2 copy-start.25
  570.0 1.9 copy-start.28
  574.6 432.9 %reduce-scatter.25.cloned.1.call-start = ((), (), s32[]{:S(2)}) async-start(), calls=%async_computation.24 | async-start | bytes 14155776 | tf_op jit(solution)/shard_map/reduce_scatter | solution.py:831
  575.4 528.0 %reduce-scatter.27.cloned.1.call-start = ((), (), s32[]{:S(2)}) async-start(), calls=%async_computation.25 | async-start | bytes 14155776 | tf_op jit(solution)/shard_map/reduce_scatter | solution.py:834
  576.0 623.2 %reduce-scatter.29.cloned.1.call-start = ((), (), s32[]{:S(2)}) async-start(), calls=%async_computation.26 | async-start | bytes 14155776 | tf_op jit(solution)/shard_map/reduce_scatter | solution.py:837
  576.0 4.1 copy-start.10
  576.6 116.7 %all-to-all-start = ((bf16[8,32,1536]{2,1,0:T(8,128)(2,1)}), bf16[8,32,1536]{2,1,0:T(8,128)(2,1)S(1)}, u32[]{:S(2)}, u32[]{:S(2)}) async-start(bf16[8,32,1536]{2,1,0:T(8,128)(2,1)} %bitcast.218), calls=%async_computation.1 | async-start | bytes 1572864 | tf_op jit(solution)/shard_map/all_to_all | solution.py:65
  693.3 217.7 %copy-start.36 = (f32[1536]{0:T(1024)S(1)}, f32[1536]{0:T(1024)}, u32[]{:S(2)}) copy-start(f32[1536]{0:T(1024)} %param.28) | copy-start | bytes 18436
  695.4 257.9 %copy-start.6 = (f32[256,1536]{1,0:T(8,128)S(1)}, f32[256,1536]{1,0:T(8,128)}, u32[]{:S(2)}) copy-start(f32[256,1536]{1,0:T(8,128)} %get-tuple-element.89) | copy-start | bytes 4718596
Sparse Core Ops, SparseCore 0:
  10.7 90.4 all-gather.9
  103.7 72.3 all-gather.5
  178.6 80.0 all-gather.7
  358.8 62.2 reduce-scatter.12
  441.7 61.7 all-gather.11
  506.2 58.8 reduce-scatter.10
  571.3 120.5 all-reduce.4
  694.9 34.6 reduce-scatter.20
  732.7 33.8 reduce-scatter.18
  770.2 36.7 reduce-scatter.16
  811.2 36.7 reduce-scatter.22
  850.7 60.2 reduce-scatter.14
  914.5 93.0 reduce-scatter.24
  1010.9 92.3 reduce-scatter.26
  1106.7 92.3 reduce-scatter.28

commit v3 on v2

--- a/solution.py
+++ b/solution.py
@@ -15,29 +15,6 @@
 
 
 EPS = 1e-05
-
-
-def full_rows(values):
-    return lax.all_gather(values, "mp", axis=0, tiled=True)
-
-
-def row_share(partial_value):
-    return lax.psum_scatter(partial_value, "mp", scatter_dimension=0, tiled=True)
-
-
-def norm_apply(values, gain):
-    energy = jnp.mean(values * values, axis=1)
-    scale = lax.rsqrt(energy + EPS)
-    normed = values * scale[:, None] * gain[None, :]
-    return (scale, normed.astype(jnp.bfloat16))
-
-
-def norm_back(values, gain, scale, grad_normed):
-    weighted = grad_normed * gain[None, :]
-    inner = jnp.mean(weighted * values, axis=1)
-    grad_in = scale[:, None] * weighted - values * (scale * scale * scale * inner)[:, None]
-    gain_grad = jnp.sum(grad_normed * values * scale[:, None], axis=0)
-    return (grad_in, gain_grad)
 
 
 def deal_tables(deal_order, expert_ids, block):
@@ -61,93 +38,10 @@
     return (home, code[None, :], counts)
 
 
-def to_home(stretch, home):
-    moved = lax.all_to_all(stretch, "dp", split_axis=0, concat_axis=0, tiled=True)
-    return moved[home].astype(jnp.float32)
-
-
 def segment_of(lengths, rows):
     ends = jnp.cumsum(lengths)
     places = jnp.arange(rows, dtype=jnp.int32)
     return jnp.sum((places[:, None] >= ends[None, :]).astype(jnp.int32), axis=1)
-
-
-def visible(segment, start, finish):
-    query_pos = jnp.arange(start, finish, dtype=jnp.int32)
-    key_pos = jnp.arange(finish, dtype=jnp.int32)
-    same = segment[start:finish][:, None] == segment[:finish][None, :]
-    return same & (key_pos[None, :] <= query_pos[:, None])
-
-
-def block_scores(query, key, segment, start, block, heads_kv, share):
-    finish = start + block
-    query_rows = query[start:finish].reshape(block, heads_kv, share, HD)
-    key_rows = key[:finish].reshape(finish, heads_kv, HD)
-    scores = jnp.einsum(
-        "qgsd,tgd->gsqt", query_rows, key_rows, preferred_element_type=jnp.float32
-    ) * HD ** (-0.5)
-    return (query_rows, key_rows, jnp.where(visible(segment, start, finish), scores, -1e30))
-
-
-def attend_totals(query, key, segment):
-    rows = query.shape[0]
-    heads_kv = key.shape[1] // HD
-    share = query.shape[1] // key.shape[1]
-    block = min(512, rows)
-    totals = []
-    for start in range(0, rows, block):
-        _, _, masked = block_scores(query, key, segment, start, block, heads_kv, share)
-        totals.append(jax.nn.logsumexp(masked, axis=-1, keepdims=True))
-    return totals
-
-
-def attend_back(query, key, value, segment, grad_mix, totals):
-    rows = query.shape[0]
-    heads_kv = key.shape[1] // HD
-    share = query.shape[1] // key.shape[1]
-    block = min(512, rows)
-    scale = HD ** (-0.5)
-    grad_query = []
-    grad_key = jnp.zeros((rows, heads_kv, HD), jnp.float32)
-    grad_value = jnp.zeros((rows, heads_kv, HD), jnp.float32)
-    for number, start in enumerate(range(0, rows, block)):
-        finish = start + block
-        query_rows, key_rows, masked = block_scores(
-            query, key, segment, start, block, heads_kv, share
-        )
-        value_rows = value[:finish].reshape(finish, heads_kv, HD)
-        probs = jnp.exp(masked - totals[number])
-        grad_rows = grad_mix[start:finish].reshape(block, heads_kv, share, HD)
-        grad_probs = jnp.einsum(
-            "qgsd,tgd->gsqt", grad_rows, value_rows, preferred_element_type=jnp.float32
-        )
-        inner = jnp.sum(probs * grad_probs, axis=-1, keepdims=True)
-        grad_scores = (probs * (grad_probs - inner)).astype(jnp.bfloat16)
-        piece = (
-            jnp.einsum("gsqt,tgd->qgsd", grad_scores, key_rows, preferred_element_type=jnp.float32)
-            * scale
-        )
-        grad_query.append(piece.reshape(block, -1))
-        grad_key = grad_key.at[:finish].add(
-            jnp.einsum(
-                "gsqt,qgsd->tgd", grad_scores, query_rows, preferred_element_type=jnp.float32
-            )
-            * scale
-        )
-        grad_value = grad_value.at[:finish].add(
-            jnp.einsum(
-                "gsqt,qgsd->tgd",
-                probs.astype(jnp.bfloat16),
-                grad_rows,
-                preferred_element_type=jnp.float32,
-            )
-        )
-    grad_query = jnp.concatenate(grad_query, axis=0).astype(jnp.bfloat16)
-    return (
-        grad_query,
-        grad_key.reshape(rows, -1).astype(jnp.bfloat16),
-        grad_value.reshape(rows, -1).astype(jnp.bfloat16),
-    )
 
 
 def mm(a, b, dims=((1,), (0,))):
@@ -180,7 +74,16 @@
     grad_hidden = mm(grad_each, down_w[0], NT)
     grad_gate = (grad_hidden * up_part * sigma * (1.0 + gate_part * (1.0 - sigma))).astype(low)
     grad_up = (grad_hidden * gate_part * sigma).astype(low)
-    down_out[0] = mm(hidden, grad_each, TN).astype(low)
+    down_grad = mm(hidden, grad_each, TN).astype(low)
+    high, wide = down_grad.shape
+    subs, span = down_out.shape[2], high // 4 // down_out.shape[2]
+    for chunk in range(4):
+        for sub in range(subs):
+            row = (chunk * subs + sub) * span
+            for column in range(wide // high):
+                down_out[0, chunk, sub, column * span : (column + 1) * span, :] = down_grad[
+                    row : row + span, column * high : (column + 1) * high
+                ]
     gate_out[0] = mm(x, grad_gate, TN).astype(low)
     up_out[0] = mm(x, grad_up, TN).astype(low)
     back_rows = mm(grad_gate, gate_w[0], NT) + mm(grad_up, up_w[0], NT)
@@ -235,12 +138,16 @@
             own[1] * (grad_gates[1] - inner)
         )
         grad_logits = grad_logits.astype(low)
-        router_out[...] = mm(grad_logits, second[...])
+        router_grad = mm(grad_logits, second[...])
+        for owner in range(router_out.shape[0]):
+            span = router_out.shape[2]
+            router_out[owner] = router_grad[:, owner * span : (owner + 1) * span]
         mixed_out[...] = mixed[...].astype(low)
         back_out[...] = (back[...] + mm(grad_logits, router[...], TN)).astype(low)
 
 
-def experts(second, grad, code, counts, router, gate_w, up_w, down_w):
+def experts(groups, second, grad, code, counts, router, gate_w, up_w, down_w):
+    per = E // groups
     rows = second.shape[0]
     hidden = gate_w.shape[2]
     low = jnp.bfloat16
@@ -263,7 +170,14 @@
                 wide,
                 tall,
             ],
-            out_specs=[block, block, wide, wide, tall, pl.BlockSpec((E, D), whole)],
+            out_specs=[
+                block,
+                block,
+                wide,
+                wide,
+                pl.BlockSpec((1, 4, 4 // per, D // groups, hidden), lambda e, *_: (e // per, 0, e % per, 0, 0)),
+                pl.BlockSpec((groups, E, D // groups), lambda e, *_: (0, 0, 0)),
+            ],
             scratch_shapes=[
                 pltpu.VMEM((E, rows), jnp.float32),
                 pltpu.VMEM((E, rows), jnp.float32),
@@ -277,8 +191,8 @@
             jax.ShapeDtypeStruct((rows, D), low),
             jax.ShapeDtypeStruct((E, D, hidden), low),
             jax.ShapeDtypeStruct((E, D, hidden), low),
-            jax.ShapeDtypeStruct((E, hidden, D), low),
-            jax.ShapeDtypeStruct((E, D), jnp.float32),
+            jax.ShapeDtypeStruct((groups, 4, 4, D // groups, hidden), low),
+            jax.ShapeDtypeStruct((groups, E, D // groups), jnp.float32),
         ],
         compiler_params=pltpu.CompilerParams(
             dimension_semantics=("arbitrary",), vmem_limit_bytes=58 * 2**20
@@ -438,21 +352,29 @@
         self.me = lax.axis_index("mp")
         self.rows = held.shape[1] // chunks
 
+    def slot(self, way, target, device):
+        return target + (self.parts - target) * ((target == device) & (way == 0)).astype(jnp.int32)
+
     def copy(self, target, chunk):
         way = (target > self.me).astype(jnp.int32)
+        slot = self.slot(way, target, self.me + 2 * way - 1)
         span = pl.ds(chunk * self.rows, self.rows)
         return pltpu.make_async_remote_copy(
             src_ref=self.held.at[target, span],
-            dst_ref=self.come.at[way, target, span],
+            dst_ref=self.come.at[slot, span],
             send_sem=self.out_sem.at[target, chunk],
-            recv_sem=self.in_sem.at[way, target, chunk],
+            recv_sem=self.in_sem.at[slot, chunk],
             device_id={"mp": self.me + 2 * way - 1},
             device_id_type=MESH,
         )
 
-    def come_in(self, way, target, chunk):
-        piece = self.come.at[way, target, pl.ds(chunk * self.rows, self.rows)]
-        pltpu.make_async_copy(piece, piece, self.in_sem.at[way, target, chunk]).wait()
+    def come_in(self, slot, chunk):
+        piece = self.come.at[slot, pl.ds(chunk * self.rows, self.rows)]
+        pltpu.make_async_copy(piece, piece, self.in_sem.at[slot, chunk]).wait()
+
+    def turned(self, target):
+        right = (2 * self.me >= self.parts).astype(jnp.int32)
+        return target + right * (self.parts - 1 - 2 * target)
 
     def begin(self, target):
         end = ((target < self.me) & (self.me == self.parts - 1)) | ((target > self.me) & (self.me == 0))
@@ -467,21 +389,20 @@
 
         @pl.when(between)
         def _():
-            way = (target > self.me).astype(jnp.int32)
             span = pl.ds(chunk * self.rows, self.rows)
-            self.come_in(way, target, chunk)
-            self.held[target, span, :] = self.held[target, span, :] + self.come[way, target, span, :]
+            self.come_in(target, chunk)
+            self.held[target, span, :] = self.held[target, span, :] + self.come[target, span, :]
             self.copy(target, chunk).start()
 
     def total(self, chunk, out):
         span = pl.ds(chunk * self.rows, self.rows)
         out[span, :] = self.held[self.me, span, :].astype(jnp.float32)
-        for way, there in ((0, self.me < self.parts - 1), (1, self.me > 0)):
+        for slot, there in ((self.parts, self.me < self.parts - 1), (self.me, self.me > 0)):
 
             @pl.when(there)
             def _():
-                self.come_in(way, self.me, chunk)
-                out[span, :] = out[span, :] + self.come[way, self.me, span, :].astype(jnp.float32)
+                self.come_in(slot, chunk)
+                out[span, :] = out[span, :] + self.come[slot, span, :].astype(jnp.float32)
 
     def finish(self):
         for target in range(self.parts):
@@ -531,19 +452,15 @@
 
 def greet(groups, parts):
     barrier = pltpu.get_barrier_semaphore()
-    me, part = lax.axis_index("dp"), lax.axis_index("mp")
-    for turn in range(1, groups):
-        pl.semaphore_signal(
-            barrier, inc=1, device_id={"dp": lax.rem(me + turn, groups)}, device_id_type=MESH
-        )
-    for step, there in ((-1, part > 0), (1, part < parts - 1)):
-
-        @pl.when(there)
-        def _():
-            pl.semaphore_signal(barrier, inc=1, device_id={"mp": part + step}, device_id_type=MESH)
-
-    sides = (part > 0).astype(jnp.int32) + (part < parts - 1).astype(jnp.int32)
-    pl.semaphore_wait(barrier, groups - 1 + sides)
+    for axis, size in (("dp", groups), ("mp", parts)):
+        for turn in range(1, size):
+            peer = lax.rem(lax.axis_index(axis) + turn, size)
+            pl.semaphore_signal(barrier, inc=1, device_id={axis: peer}, device_id_type=MESH)
+    pl.semaphore_wait(barrier, groups + parts - 2)
+
+
+def far_first(parts):
+    return sorted(range(parts), key=lambda t: (-abs(2 * t - parts + 1), -t))
 
 
 def scale_of(values):
@@ -624,7 +541,7 @@
     save(2, qkv, qkv_out)
 
     sums = LineSum(parts, 2, part, come, sum_out, sum_in)
-    order = sorted(range(parts), key=lambda t: (-abs(2 * t - parts + 1), -t))
+    order = far_first(parts)
     reach = -(-512 // shard)
     for number, target in enumerate(order):
         start, stop = target * shard, (target + 1) * shard
@@ -651,7 +568,7 @@
     save(3, mix, mix_out)
     for target in order:
         for chunk in range(2):
-            sums.relay(target, chunk)
+            sums.relay(sums.turned(target), chunk)
     for chunk in range(2):
         sums.total(chunk, middle)
     values = tokens[...] + middle[...]
@@ -710,14 +627,14 @@
             pltpu.VMEM((slots, rows, HD), low),
             pltpu.VMEM((heads, rows, HD), low),
             held(),
-            pltpu.VMEM((2, parts, shard, width), low),
+            pltpu.VMEM((parts + 1, shard, width), low),
             pltpu.VMEM((shard, shard * (1 - (-512 // shard))), jnp.float32),
             *[pltpu.VMEM((shard, width), row_type(shard // groups))] * 4,
             cube_sems(groups, 2),
             dma((3, 2, parts, 2)),
             dma((3, parts, 2)),
             dma((parts, 2)),
-            dma((2, parts, 2)),
+            dma((parts + 1, 2)),
             dma((2, groups)),
             dma((2, groups)),
             dma((6,)),
@@ -729,6 +646,480 @@
             flops=12 * rows * width * columns, bytes_accessed=60 * 2**20, transcendentals=rows * rows * heads
         ),
     )(home, seg[None, :], seg[:, None], attn_gain[None, :], moe_gain[None, :], tokens, out_grad, wpack)
+
+
+class CubeSum:
+    def __init__(self, groups, chunks, own, pair_held, step_held, sems):
+        self.bits = groups.bit_length() - 2
+        self.chunks, self.own, self.pair_held, self.step_held = chunks, own, pair_held, step_held
+        self.out_sem, self.in_sem, self.pair_out, self.pair_in = sems
+        self.me = lax.axis_index("dp")
+        self.waits = []
+
+    def flip(self, index, mask):
+        for bit in range(self.bits + 1):
+            if mask >> bit & 1:
+                index = index + (1 << bit) * (1 - 2 * ((index // (1 << bit)) % 2))
+        return index
+
+    def step_of(self, chunk, want):
+        for step in range(self.bits):
+            bit = (chunk + step) % self.bits
+            if want >> bit & 1:
+                return step, bit
+        return self.bits, None
+
+    def pair(self, chunk):
+        for want in range(1 << self.bits):
+            copy = pltpu.make_async_remote_copy(
+                src_ref=self.own(chunk, self.flip(self.me, 2 * want + 1)),
+                dst_ref=self.pair_held(chunk, want),
+                send_sem=self.pair_out.at[chunk, want],
+                recv_sem=self.pair_in.at[chunk, want],
+                device_id={"dp": self.flip(self.me, 1)},
+                device_id_type=MESH,
+            )
+            copy.start()
+            self.waits.append(copy.wait_send)
+
+    def send(self, chunk, want, source):
+        step, bit = self.step_of(chunk, want)
+        rest = want ^ (1 << bit)
+        copy = pltpu.make_async_remote_copy(
+            src_ref=source,
+            dst_ref=self.step_held(chunk, step, rest),
+            send_sem=self.out_sem.at[chunk, want],
+            recv_sem=self.in_sem.at[chunk, step, rest],
+            device_id={"dp": self.flip(self.me, 2 << bit)},
+            device_id_type=MESH,
+        )
+        copy.start()
+        return copy.wait_send
+
+    def terms(self, chunk, want):
+        found = [self.own(chunk, self.flip(self.me, 2 * want)), self.pair_held(chunk, want)]
+        pltpu.make_async_copy(found[1], found[1], self.pair_in.at[chunk, want]).wait()
+        for step in range(self.step_of(chunk, want)[0]):
+            held = self.step_held(chunk, step, want)
+            pltpu.make_async_copy(held, held, self.in_sem.at[chunk, step, want]).wait()
+            found.append(held)
+        return found
+
+    def items(self, lag):
+        found = []
+        for chunk in range(self.chunks):
+            for want in range(1 << self.bits):
+                step = self.step_of(chunk, want)[0]
+                found.append((chunk + lag * step, step, chunk, want))
+        return [item[2:] for item in sorted(found)]
+
+    def finish(self):
+        for wait in self.waits:
+            wait()
+
+
+def sum_sems(groups, chunks):
+    bits = groups.bit_length() - 2
+    dma = pltpu.SemaphoreType.DMA
+    return [
+        dma((chunks, 1 << bits)),
+        dma((chunks, bits, 1 << bits)),
+        dma((chunks, 1 << bits)),
+        dma((chunks, 1 << bits)),
+    ]
+
+
+class Stream:
+    def __init__(self, cube, lag, terms, sums, totals, out, load_sem, save_sem):
+        self.cube, self.terms, self.sums, self.totals, self.out = cube, terms, sums, totals, out
+        self.load_sem, self.save_sem = load_sem, save_sem
+        self.list = cube.items(lag)
+        self.at, self.sent, self.saved, self.loads = 0, [], [], None
+
+    def tick(self, times=1):
+        for _ in range(times):
+            if self.at <= len(self.list):
+                loads = self.fetch(self.at) if self.at < len(self.list) else None
+                if self.loads is not None:
+                    self.add(self.at - 1)
+                self.loads = loads
+                self.at += 1
+
+    def fetch(self, number):
+        slot = number % 2
+        loads = []
+        for term, ref in enumerate(self.cube.terms(*self.list[number])):
+            copy = pltpu.make_async_copy(ref, self.terms.at[slot, term], self.load_sem.at[slot, term])
+            copy.start()
+            loads.append(copy)
+        return loads
+
+    def add(self, number):
+        slot = number % 2
+        chunk, want = self.list[number]
+        for copy in self.loads:
+            copy.wait()
+        count = len(self.loads)
+        if want:
+            place = len(self.sent) % self.sums.shape[0]
+            if len(self.sent) >= self.sums.shape[0]:
+                self.sent[len(self.sent) - self.sums.shape[0]]()
+            target = self.sums.at[place]
+        else:
+            place = len(self.saved) % self.totals.shape[0]
+            if len(self.saved) >= self.totals.shape[0]:
+                self.saved[len(self.saved) - self.totals.shape[0]]()
+            target = self.totals.at[place]
+
+        def row(index, _):
+            total = self.terms[slot, 0, index].astype(jnp.float32)
+            for term in range(1, count):
+                total = total + self.terms[slot, term, index].astype(jnp.float32)
+            target[index] = total.astype(target.dtype)
+            return 0
+
+        lax.fori_loop(0, target.shape[0], row, 0)
+        if want:
+            self.sent.append(self.cube.send(chunk, want, target))
+        else:
+            copy = pltpu.make_async_copy(target, self.out(chunk), self.save_sem.at[place])
+            copy.start()
+            self.saved.append(copy.wait)
+
+    def finish(self):
+        self.tick(len(self.list) + 1 - self.at)
+        for wait in self.sent[-self.sums.shape[0] :] + self.saved[-self.totals.shape[0] :]:
+            wait()
+
+
+class Share:
+    def __init__(self, axis, size, held, out_sem, in_sem, source):
+        self.axis, self.size, self.held = axis, size, held
+        self.out_sem, self.in_sem, self.source = out_sem, in_sem, source
+        self.me = lax.axis_index(axis)
+
+    def copy(self, turn):
+        peer = lax.rem(self.me + turn, self.size)
+        return pltpu.make_async_remote_copy(
+            src_ref=self.source(peer),
+            dst_ref=self.held.at[self.me],
+            send_sem=self.out_sem.at[turn],
+            recv_sem=self.in_sem.at[turn],
+            device_id={self.axis: peer},
+            device_id_type=MESH,
+        )
+
+    def begin(self):
+        for turn in range(1, self.size):
+            self.copy(turn).start()
+        self.held[self.me] = self.source(self.me)[...]
+
+    def total(self):
+        for turn in range(1, self.size):
+            self.copy(turn).wait()
+        total = self.held[0]
+        for index in range(1, self.size):
+            total = total + self.held[index]
+        return total
+
+
+def backward_kernel(groups, parts, heads, heads_kv, home, seg_row, seg_col, attn_gain, moe_gain, tokens, out_grad, middle,
+                    router_part, back_in, mixed_in, first_in, qkv_in, mix_in, weights_in, gate_in, up_in, down_in,
+                    block_out, tokens_grad, gains_out, router_out, pack_out, gate_out, up_out, down_out, pair_held, step_held,
+                    held, come, mixed, mixed_come, grad, qkv, mix, weights, grad_mix, grad_query, grad_key, grad_value,
+                    flat, bias, pack, pack_pair, pack_step, stage, land_back, land_mixed, terms, sums, totals,
+                    router_all, router_line, gains, gains_line, gains_all,
+                    load_sem, cube_sems, pack_sems, term_sem, save_sem, line_out, line_in, sum_out, sum_in, deal_out, deal_in,
+                    share_out, share_in):
+    low = jnp.bfloat16
+    shard, width = tokens.shape
+    me, place = lax.axis_index("dp"), lax.axis_index("mp")
+    share = heads // heads_kv
+    slots = heads + 2 * heads_kv
+    bits = groups.bit_length() - 2
+    arrays = ((back_in, held), (weights_in, weights), (mix_in, mix), (qkv_in, qkv), (mixed_in, mixed))
+    loads = []
+    for number, (source, target) in enumerate(arrays):
+        loads.append(pltpu.make_async_copy(source, target, load_sem.at[number]))
+        loads[-1].start()
+    greet(groups, parts)
+
+    gains[...] = jnp.zeros_like(gains)
+    count = gate_in.shape[0] // 4
+    owner_rows = width // groups
+
+    def own(chunk, owner):
+        if chunk < 2 * count:
+            ref = (gate_in, up_in)[chunk // count]
+            return ref.at[pl.ds(chunk % count * 4, 4), pl.ds(owner * owner_rows, owner_rows)]
+        return down_in.at[owner, chunk - 2 * count]
+
+    places = {}
+
+    def step_place(chunk, step, want):
+        return step_held.at[chunk, places.setdefault((chunk, step, want), len([k for k in places if k[0] == chunk]))]
+
+    cube = CubeSum(groups, 3 * count, own, lambda chunk, want: pair_held.at[chunk, want], step_place, cube_sems)
+    out = lambda chunk: (gate_out, up_out, down_out)[chunk // count].at[chunk % count]
+    stream = Stream(cube, 3, terms, sums, totals, out, term_sem, save_sem)
+
+    back = LineSum(parts, 2, held, come, sum_out.at[0], sum_in.at[0])
+    loads[0].wait()
+    order = far_first(parts)
+    for target in order:
+        back.begin(back.turned(target))
+    for chunk in range(3 * count):
+        cube.pair(chunk)
+    routers = Share("dp", groups, router_all, share_out.at[0], share_in.at[0], lambda peer: router_part.at[peer])
+    routers.begin()
+    stream.tick(3)
+    for target in order:
+        for chunk in range(2):
+            back.relay(back.turned(target), chunk)
+            stream.tick(2 if target != order[-1] else 0)
+    for chunk in range(2):
+        back.total(chunk, block_out)
+    stage[...] = block_out[...].astype(stage.dtype)
+    deal = Exchange(groups, stage, land_back, deal_out.at[0], deal_in.at[0])
+    deal.begin()
+    back.finish()
+    loads[4].wait()
+    extra = LineSum(parts, 2, mixed, mixed_come, sum_out.at[1], sum_in.at[1])
+    for target in order:
+        extra.begin(extra.turned(target))
+    router_line[place] = routers.total()
+    router_sums = Share("mp", parts, router_line, share_out.at[1], share_in.at[1], lambda peer: router_line.at[place])
+    for turn in range(1, parts):
+        router_sums.copy(turn).start()
+    sort = sorting(home[...], shard)
+    values = middle[...]
+    scale = scale_of(values)
+    deal.arrive()
+    grad_second = mm(sort, land_back[...].astype(low), TN)
+    weighted = grad_second * moe_gain[...]
+    inner = jnp.mean(weighted * values, axis=1, keepdims=True)
+    gains[0:1, :] = jnp.sum(grad_second * values * scale, axis=0, keepdims=True)
+    grad_middle = out_grad[...] + (scale * weighted - values * (scale * scale * scale * inner))
+    tokens_grad[...] = grad_middle
+    grad[place] = grad_middle.astype(low)
+    line = LineGather(parts, 2, grad, line_out, line_in)
+    for chunk in range(2):
+        line.begin(chunk)
+    loads[1].wait()
+    loads[2].wait()
+
+    def mix_back(origin):
+        result = mm(grad[origin], weights[:, slots * HD :])
+        span = pl.ds(pl.multiple_of(origin * shard, shard), shard)
+        for head in range(heads):
+            grad_mix[head, span, :] = result[:, head * HD : (head + 1) * HD].astype(low)
+
+    mix_back(place)
+    stream.tick(2)
+    for distance in range(1, parts):
+        for chunk in range(2):
+            for way in (0, 1):
+                line.step(distance, way, chunk)
+            extra.relay(extra.turned(order[distance - 1]), chunk)
+            stream.tick(3)
+        for way in (0, 1):
+            line.from_side(distance, way, mix_back)
+    for chunk in range(2):
+        extra.relay(extra.turned(order[parts - 1]), chunk)
+    mix_flat = jnp.concatenate([mix[head] for head in range(heads)], axis=1)
+    pack[:, slots * HD :] = mm(grad[...].reshape(parts * shard, width), mix_flat, TN).astype(low)
+    deal.finish()
+    for chunk in range(2):
+        extra.total(chunk, block_out)
+    stage[...] = block_out[...].astype(stage.dtype)
+    deal_mixed = Exchange(groups, stage, land_mixed, deal_out.at[1], deal_in.at[1])
+    deal_mixed.begin()
+    loads[3].wait()
+    extra.finish()
+    first_load = pltpu.make_async_copy(first_in, mixed, load_sem.at[5])
+    first_load.start()
+    stream.tick(2)
+
+    first_sum = LineSum(parts, 2, held, come, sum_out.at[2], sum_in.at[2])
+    grad_key[...] = jnp.zeros_like(grad_key)
+    grad_value[...] = jnp.zeros_like(grad_value)
+    reach = -(-512 // shard)
+    for target in reversed(range(parts)):
+        start, stop = target * shard, (target + 1) * shard
+        bottom = max(0, target - reach) * shard
+        bias[:, : stop - bottom] = bias_of(seg_row, seg_col, start, bottom, stop)
+
+        def attend(head, _):
+            group = head // share
+            query = qkv[head, start:stop, :]
+            keys = qkv[heads + group, bottom:stop, :]
+            scores = mm(query, keys, NT) * HD**-0.5 + bias[:, : stop - bottom]
+            raised = jnp.exp(scores - jnp.max(scores, axis=1, keepdims=True))
+            probs = raised * (1.0 / jnp.sum(raised, axis=1, keepdims=True))
+            grad_rows = grad_mix[head, start:stop, :]
+            grad_probs = mm(grad_rows, qkv[heads + heads_kv + group, bottom:stop, :], NT)
+            inner = jnp.sum(probs * grad_probs, axis=1, keepdims=True)
+            grad_scores = (probs * (grad_probs - inner)).astype(low)
+            grad_query[head, start:stop, :] = (mm(grad_scores, keys) * HD**-0.5).astype(low)
+            grad_key[group, bottom:stop, :] += mm(grad_scores, query, TN)
+            grad_value[group, bottom:stop, :] += mm(probs.astype(low), grad_rows, TN)
+            return 0
+
+        lax.fori_loop(0, heads, attend, 0)
+        pieces = [grad_query[head, start:stop, :] for head in range(heads)]
+        pieces += [(grad_key[group, start:stop, :] * HD**-0.5).astype(low) for group in range(heads_kv)]
+        pieces += [grad_value[group, start:stop, :].astype(low) for group in range(heads_kv)]
+        flat[start:stop, :] = jnp.concatenate(pieces, axis=1)
+        held[target] = mm(flat[start:stop, :], weights[:, : slots * HD], NT).astype(low)
+        first_sum.begin(target)
+        stream.tick(2)
+    first_load.wait()
+    pack[:, : slots * HD] = mm(mixed[...].reshape(parts * shard, width), flat[...], TN).astype(low)
+    cut = owner_rows // 2
+    pack_places = {}
+
+    def pack_place(chunk, step, want):
+        return pack_step.at[chunk, pack_places.setdefault((chunk, step, want), len([k for k in pack_places if k[0] == chunk]))]
+
+    pack_cube = CubeSum(
+        groups,
+        2,
+        lambda chunk, owner: pack.at[pl.ds(owner * owner_rows + chunk * cut, cut)],
+        lambda chunk, want: pack_pair.at[chunk, want],
+        pack_place,
+        pack_sems,
+    )
+    for chunk in range(2):
+        pack_cube.pair(chunk)
+    for target in reversed(range(parts)):
+        for chunk in range(2):
+            first_sum.relay(target, chunk)
+        stream.tick(2)
+    pack_sent = []
+    for chunk, want in pack_cube.items(1):
+        refs = pack_cube.terms(chunk, want)
+        total = refs[0][...].astype(jnp.float32)
+        for ref in refs[1:]:
+            total = total + ref[...].astype(jnp.float32)
+        if want:
+            refs[0][...] = total.astype(low)
+            pack_sent.append(pack_cube.send(chunk, want, refs[0]))
+        else:
+            pack_out[chunk * cut : (chunk + 1) * cut, :] = total
+    for chunk in range(2):
+        first_sum.total(chunk, block_out)
+    grad_first = block_out[...]
+    values = tokens[...]
+    scale = scale_of(values)
+    weighted = grad_first * attn_gain[...]
+    inner = jnp.mean(weighted * values, axis=1, keepdims=True)
+    gains[1:2, :] = jnp.sum(grad_first * values * scale, axis=0, keepdims=True)
+    gains_lines = Share("mp", parts, gains_line, share_out.at[2], share_in.at[2], lambda peer: gains)
+    gains_lines.begin()
+    tokens_grad[...] += scale * weighted - values * (scale * scale * scale * inner)
+    deal_mixed.arrive()
+    block_out[...] = middle[...] + mm(sort, land_mixed[...].astype(low), TN)
+    router_out[...] = router_sums.total()
+    gains[...] = gains_lines.total()
+    gains_rest = Share("dp", groups, gains_all, share_out.at[3], share_in.at[3], lambda peer: gains)
+    gains_rest.begin()
+    stream.finish()
+    gains_out[...] = gains_rest.total()
+    line.finish()
+    first_sum.finish()
+    deal_mixed.finish()
+    cube.finish()
+    pack_cube.finish()
+    for wait in pack_sent:
+        wait()
+
+
+def backward(groups, parts, heads, heads_kv, home, seg, attn_gain, moe_gain, tokens, out_grad, middle, router_part,
+             back, mixed, first, qkv, mix, weights, gate_grad, up_grad, down_grad):
+    shard, width = tokens.shape
+    rows = shard * parts
+    low = jnp.bfloat16
+    slots = heads + 2 * heads_kv
+    columns = weights.shape[1]
+    owner_rows, hidden = width // groups, gate_grad.shape[2]
+    bits = groups.bit_length() - 2
+    chunks = 3 * (E // 4)
+    cut = owner_rows // 2
+    vmem = pl.BlockSpec(memory_space=pltpu.VMEM)
+    hbm = pl.BlockSpec(memory_space=pl.ANY)
+    dma = pltpu.SemaphoreType.DMA
+    f32 = lambda *shape: jax.ShapeDtypeStruct(shape, jnp.float32)
+    unit = (4, owner_rows, hidden)
+    held = pltpu.VMEM((parts, shard, width), low)
+    come = pltpu.VMEM((parts + 1, shard, width), low)
+    line = row_type(shard // groups)
+    return pl.pallas_call(
+        functools.partial(backward_kernel, groups, parts, heads, heads_kv),
+        in_specs=[vmem] * 9 + [hbm] * 9,
+        out_specs=[vmem] * 5 + [hbm] * 5,
+        out_shape=[
+            f32(shard, width),
+            f32(shard, width),
+            f32(8, width),
+            f32(E, owner_rows),
+            f32(owner_rows, columns),
+            f32(E // 4, *unit),
+            f32(E // 4, *unit),
+            f32(E // 4, *unit),
+            jax.ShapeDtypeStruct((chunks, 1 << bits, *unit), low),
+            jax.ShapeDtypeStruct((chunks, (1 << bits) - 1, *unit), low),
+        ],
+        scratch_shapes=[
+            held,
+            come,
+            held,
+            come,
+            held,
+            pltpu.VMEM((slots, rows, HD), low),
+            pltpu.VMEM((heads, rows, HD), low),
+            pltpu.VMEM((width, columns), low),
+            pltpu.VMEM((heads, rows, HD), low),
+            pltpu.VMEM((heads, rows, HD), low),
+            pltpu.VMEM((heads_kv, rows, HD), jnp.float32),
+            pltpu.VMEM((heads_kv, rows, HD), jnp.float32),
+            pltpu.VMEM((rows, slots * HD), low),
+            pltpu.VMEM((shard, shard * (1 - (-512 // shard))), jnp.float32),
+            pltpu.VMEM((width, columns), low),
+            pltpu.VMEM((2, 1 << bits, cut, columns), low),
+            pltpu.VMEM((2, (1 << bits) - 1, cut, columns), low),
+            pltpu.VMEM((shard, width), line),
+            pltpu.VMEM((shard, width), line),
+            pltpu.VMEM((shard, width), line),
+            pltpu.VMEM((2, 2 + bits, *unit), low),
+            pltpu.VMEM((4, *unit), low),
+            pltpu.VMEM((2, *unit), jnp.float32),
+            pltpu.VMEM((groups, E, owner_rows), jnp.float32),
+            pltpu.VMEM((parts, E, owner_rows), jnp.float32),
+            pltpu.VMEM((8, width), jnp.float32),
+            pltpu.VMEM((parts, 8, width), jnp.float32),
+            pltpu.VMEM((groups, 8, width), jnp.float32),
+            dma((6,)),
+            sum_sems(groups, chunks),
+            sum_sems(groups, 2),
+            dma((2, 2 + bits)),
+            dma((2,)),
+            dma((2, parts, 2)),
+            dma((parts, 2)),
+            dma((3, parts, 2)),
+            dma((3, parts + 1, 2)),
+            dma((2, groups)),
+            dma((2, groups)),
+            dma((4, max(groups, parts))),
+            dma((4, max(groups, parts))),
+        ],
+        compiler_params=pltpu.CompilerParams(
+            collective_id=1, has_side_effects=True, vmem_limit_bytes=63 * 2**20
+        ),
+        cost_estimate=pl.CostEstimate(
+            flops=24 * rows * width * columns, bytes_accessed=200 * 2**20, transcendentals=rows * rows * heads
+        ),
+    )(home, seg[None, :], seg[:, None], attn_gain[None, :], moe_gain[None, :], tokens, out_grad, middle, router_part,
+      back, mixed, first, qkv, mix, weights, gate_grad, up_grad, down_grad)
 
 
 def body(
@@ -764,93 +1155,58 @@
     middle, first_full, qkv, mix, weights, second_full, grad_full = forward(
         groups, parts, home[None, :], segment, attn_gain, moe_gain, tokens, out_grad, wpack, heads, heads_kv
     )
-    second_full, grad_full = second_full.reshape(rows, D), grad_full.reshape(rows, D)
-    mixed, back, grad_gate_all, grad_up_all, grad_down_all, grad_router = experts(
-        second_full, grad_full, code, counts, router_w.T, gate_w, up_w, down_w
+    mixed, back, gate_grad, up_grad, down_grad, router_part = experts(
+        groups,
+        second_full.reshape(rows, D),
+        grad_full.reshape(rows, D),
+        code,
+        counts,
+        router_w.T,
+        gate_w,
+        up_w,
+        down_w,
     )
-    grad_normed_two = to_home(row_share(back), home)
-    block_out = middle + to_home(row_share(mixed), home)
-    columns = heads * HD
-    first_full = first_full.reshape(rows, D)
-    query_w, key_w, value_w, out_w = (
-        weights[:, :columns],
-        weights[:, columns : columns + heads_kv * HD],
-        weights[:, columns + heads_kv * HD : columns + 2 * heads_kv * HD],
-        weights[:, columns + 2 * heads_kv * HD :].T,
+    block_out, tokens_grad, gains, router_sum, pack_sum, gate_sum, up_sum, down_sum, _, _ = backward(
+        groups,
+        parts,
+        heads,
+        heads_kv,
+        home[None, :],
+        segment,
+        attn_gain,
+        moe_gain,
+        tokens,
+        out_grad,
+        middle,
+        router_part,
+        back.reshape(second_full.shape),
+        mixed.reshape(second_full.shape),
+        first_full,
+        qkv,
+        mix,
+        weights,
+        gate_grad,
+        up_grad,
+        down_grad,
     )
-    flat = lambda items: jnp.transpose(items, (1, 0, 2)).reshape(rows, -1)
-    query, key, value = flat(qkv[:heads]), flat(qkv[heads : heads + heads_kv]), flat(qkv[heads + heads_kv :])
-    mix = flat(mix)
-    totals = attend_totals(query, key, segment)
-    scale_one = lax.rsqrt(jnp.mean(tokens * tokens, axis=1) + EPS)
-    scale_two = lax.rsqrt(jnp.mean(middle * middle, axis=1) + EPS)
-    grad_middle_norm, grad_moe_gain = norm_back(middle, moe_gain, scale_two, grad_normed_two)
-    grad_middle = out_grad + grad_middle_norm
-    grad_attn_full = full_rows(grad_middle.astype(low_type))
-    grad_mix = jnp.einsum(
-        "td,hd->th", grad_attn_full, out_w, preferred_element_type=jnp.float32
-    ).astype(low_type)
-    grad_out_w = jnp.einsum("th,td->hd", mix, grad_attn_full, preferred_element_type=jnp.float32)
-    grad_query, grad_key, grad_value = attend_back(query, key, value, segment, grad_mix, totals)
-    grad_first = jnp.einsum("th,dh->td", grad_query, query_w, preferred_element_type=jnp.float32)
-    grad_first = grad_first + jnp.einsum(
-        "th,dh->td", grad_key, key_w, preferred_element_type=jnp.float32
-    )
-    grad_first = grad_first + jnp.einsum(
-        "th,dh->td", grad_value, value_w, preferred_element_type=jnp.float32
-    )
-    grad_query_w = jnp.einsum(
-        "td,th->dh", first_full, grad_query, preferred_element_type=jnp.float32
-    )
-    grad_key_w = jnp.einsum("td,th->dh", first_full, grad_key, preferred_element_type=jnp.float32)
-    grad_value_w = jnp.einsum(
-        "td,th->dh", first_full, grad_value, preferred_element_type=jnp.float32
-    )
-    grad_tokens_norm, grad_attn_gain = norm_back(
-        tokens, attn_gain, scale_one, row_share(grad_first.astype(low_type)).astype(jnp.float32)
-    )
-    tokens_grad = grad_middle + grad_tokens_norm
-    attn_gain_sum, moe_gain_sum, router_total = lax.psum(
-        (grad_attn_gain, grad_moe_gain, grad_router), ("dp", "mp")
-    )
-    width = w_router.shape[0]
-    router_sum = lax.dynamic_slice_in_dim(router_total, lax.axis_index("dp") * width, width, 1).T
-    query_sum, key_sum, value_sum, out_sum, gate_sum, up_sum, down_sum = (
-        lax.psum_scatter(
-            grad_query_w.astype(jnp.bfloat16), "dp", scatter_dimension=0, tiled=True
-        ).astype(jnp.float32),
-        lax.psum_scatter(
-            grad_key_w.astype(jnp.bfloat16), "dp", scatter_dimension=0, tiled=True
-        ).astype(jnp.float32),
-        lax.psum_scatter(
-            grad_value_w.astype(jnp.bfloat16), "dp", scatter_dimension=0, tiled=True
-        ).astype(jnp.float32),
-        lax.psum_scatter(
-            grad_out_w.astype(jnp.bfloat16), "dp", scatter_dimension=1, tiled=True
-        ).astype(jnp.float32),
-        lax.psum_scatter(
-            grad_gate_all.astype(jnp.bfloat16), "dp", scatter_dimension=1, tiled=True
-        ).astype(jnp.float32),
-        lax.psum_scatter(
-            grad_up_all.astype(jnp.bfloat16), "dp", scatter_dimension=1, tiled=True
-        ).astype(jnp.float32),
-        lax.psum_scatter(
-            grad_down_all.astype(jnp.bfloat16), "dp", scatter_dimension=0, tiled=True
-        ).astype(jnp.float32),
-    )
+    per, hidden = w_down.shape[:2]
+    subs = 4 // per
+    down_sum = down_sum.reshape(4, per, subs, D // hidden, hidden // 4 // subs, hidden)
+    down_sum = jnp.transpose(down_sum, (1, 0, 2, 4, 3, 5))
+    columns, columns_kv = heads * HD, heads_kv * HD
     return (
         block_out,
         tokens_grad,
-        attn_gain_sum,
-        query_sum,
-        key_sum,
-        value_sum,
-        out_sum,
-        moe_gain_sum,
-        router_sum,
-        gate_sum,
-        up_sum,
-        down_sum,
+        gains[1],
+        pack_sum[:, :columns],
+        pack_sum[:, columns : columns + columns_kv],
+        pack_sum[:, columns + columns_kv : columns + 2 * columns_kv],
+        pack_sum[:, columns + 2 * columns_kv :].T,
+        gains[0],
+        router_sum.T,
+        gate_sum.reshape(w_gate.shape),
+        up_sum.reshape(w_up.shape),
+        down_sum.reshape(w_down.shape),
     )
 
 

time: 1220 us -> 700 us (0.57)
  waiting for transfers between devices: 682 us -> 0.11 us
  Pallas kernels: 321 us -> 623 us
  matrix products: 51.6 us -> 0 us
  other arithmetic: 60.3 us -> 16 us
  blocking collectives: 51.4 us -> 10.7 us
    reduce_scatter x10 -> x0, waiting for transfers between devices: 506 us -> none  [the longest x3 124 us: row_share(): lax.psum_scatter(partial_value, 'mp', scatter_dimension=0, tiled=True)]
    pallas_call x0 -> x1, Pallas kernels: none -> 305 us  [backward(): pl.pallas_call(functools.partial(backward_kernel, groups, parts, heads, h...]
    psum x1 -> x0, waiting for transfers between devices: 112 us -> none  [body(): lax.psum((grad_attn_gain, grad_moe_gain, grad_router), ('dp', 'mp'))]
    dot_general x18 -> x0, matrix products: 51.6 us -> none  [the longest x2 10.8 us: attend_back(): jnp.einsum('qgsd,tgd->gsqt', grad_rows, value_rows, preferred_element_typ...]
    all_gather x1 -> x0, waiting for transfers between devices: 49.7 us -> none  [full_rows(): return lax.all_gather(values, 'mp', axis=0, tiled=True)]
    psum x1 -> x0, blocking collectives: 40.7 us -> none  [body(): lax.psum((grad_attn_gain, grad_moe_gain, grad_router), ('dp', 'mp'))]
    convert_element_type x10 -> x0, other arithmetic: 32.7 us -> none  [the longest x7 16.5 us: body(): query_sum, key_sum, value_sum, out_sum, gate_sum, up_sum, down_sum = (lax...]
    all_to_all x2 -> x0, waiting for transfers between devices: 12.3 us -> none  [to_home(): lax.all_to_all(stretch, 'dp', split_axis=0, concat_axis=0, tiled=True)]
  transfers between devices with their start and end apart: 17 -> 3, of which waited for: 12 -> 0; matrix products, arithmetic and copies ran while one was open for 9% -> 2% of each run, Pallas kernels for 19% -> 32%
where the time goes in v3:
time: 700 us; the launch traced here: 692 us
  Pallas kernels  623 us (89%)
  local copies, waits for them, and re-layouts  28.2 us (4%)
  other arithmetic  16 us (2%)
  between operations  14.5 us (2%)
  blocking collectives  10.7 us (2%)
    pallas_call x1, Pallas kernels, backward(): pl.pallas_call(functools.partial(backward_kernel, groups, parts, heads, h...  305 us
    pallas_call x1, Pallas kernels, forward(): pl.pallas_call(functools.partial(forward_kernel, groups, parts, heads, he...  222 us
    pallas_call x1, Pallas kernels, experts(): pl.pallas_call(expert_kernel, grid_spec=pltpu.PrefetchScalarGridSpec(num_...  94.7 us
  transfers between devices with their start and end apart: 3, of which 0 were waited for; matrix products, arithmetic and copies ran while one was open for 2% of the time, Pallas kernels for 32%

profile of v3, /device:TPU:0, one launch (start us, length us, event | category | flops | bytes accessed | tf_op | source)
XLA Modules:
  0.0 692.2 jit_solution(9351930775316605512)
XLA Ops:
  7.2 0.0 copy-start
  7.2 0.0 all-gather.5.cloned.1.call-start
  7.2 3.4 convert_element_type.30
  10.6 0.0 all-gather.5.cloned.1.call-update
  10.6 0.0 all-gather.7.cloned.1.call-start
  10.7 0.0 copy-done
  10.7 1.3 convert_element_type.31
  12.0 0.0 all-gather.7.cloned.1.call-update
  12.1 0.0 copy-start.16
  12.1 0.0 copy-start.14
  12.1 0.0 copy-start.15
  12.1 0.0 copy-start.7
  12.1 0.0 copy-start.8
  12.1 0.0 copy-start.12
  12.1 0.0 copy-start.5
  12.1 0.0 copy-start.10
  12.2 0.0 all-gather.9.cloned.1.call-start
  12.2 3.3 convert_element_type.32
  15.5 0.0 all-gather.9.cloned.1.call-update
  15.6 0.0 copy-done.16
  15.6 0.2 reduce-window.8
  15.8 0.0 copy-done.14
  15.8 0.6 broadcast_in_dim.67.attn_gain
  16.4 0.0 copy-done.15
  16.4 0.6 broadcast_in_dim.68.moe_gain
  17.0 0.0 copy-done.7
  17.0 0.0 copy-done.8
  17.0 0.0 copy-done.12
  17.0 10.7 %all-gather = bf16[8,192,16]{1,2,0:T(8,128)(2,1)S(1)} all-gather(bf16[1,192,16]{1,2,0:T(8,128)(2,1)S(1)} %convert_bitcast_fusion.1), channel_id=1, replica_groups=mesh['dp'=8,'mp'=4] {'dp'}, dimensions={0}, use_global_device_ids=true | all-gather | bytes 55296 | tf_op jit(solution)/shard_map/all_gather | solution.py:1148
  27.7 0.7 reshape.94
  28.5 0.0 copy-done.5
  28.5 0.1 convert_reduce_fusion.3
  28.6 0.0 copy-start.11
  28.6 1.0 copy.42.seg_col
  29.6 0.2 copy.40
  29.9 0.3 eq.46
  30.1 0.0 copy-done.9
  30.2 0.7 convert_reduce_fusion.2.counts
  30.9 3.7 select_reduce_fusion
  34.6 0.7 convert_reduce_fusion.1
  35.3 0.8 pad_maximum_fusion.wpack
  36.1 0.5 convert_reduce_fusion
  36.6 1.3 select_reduce_fusion.1
  37.9 222.4 %shard_map.238 = (f32[256,1536]{1,0:T(8,128)}, bf16[4,256,1536]{2,1,0:T(8,128)(2,1)}, bf16[10,1024,64]{2,1,0:T(8,128)(2,1)}, bf16[6,1024,64]{2,1,0:T(8,128)(2,1)...) custom-call(s32[1,256]{1,0:T(1,128)} %bitcast.38, s32[1,1024]{1,0:T(1,128)} %bitcast.33, ...), custom_call_target="tpu_custom_call" | custom-call | flops 19327352832 | bytes 62914560 | tf_op jit(solution)/shard_map/pallas_call | solution.py:609
  260.3 0.0 all-gather.5.cloned.1.call-done.gate_w
  260.3 0.0 all-gather.7.cloned.1.call-done.up_w
  260.3 0.0 all-gather.9.cloned.1.call-done.down_w
  260.3 94.7 %shard_map.239 = (bf16[1024,1536]{1,0:T(8,128)(2,1)}, bf16[1024,1536]{1,0:T(8,128)(2,1)}, bf16[16,1536,256]{2,1,0:T(8,128)(2,1)}, bf16[16,1536,256]{2,1,0:T(8,12...) custom-call(s32[16]{0:T(128)} %convert_reduce_fusion.2.counts, s32[1,1024]{1,0:T(1,128)} %bitcast.37, ...), custom_call_target="tpu_custom_call" | custom-call | flops 80530636800 | bytes 88080384 | tf_op jit(solution)/shard_map/pallas_call | solution.py:159
  355.1 305.4 %shard_map.240 = (f32[256,1536]{1,0:T(8,128)}, f32[256,1536]{1,0:T(8,128)}, f32[8,1536]{1,0:T(8,128)}, f32[16,192]{1,0:T(8,128)}, f32[192,1024]{1,0:T(8,128)}, /...) custom-call(s32[1,256]{1,0:T(1,128)} %bitcast.39, ...), custom_call_target="tpu_custom_call" | custom-call | flops 38654705664 | bytes 209715200 | tf_op jit(solution)/shard_map/pallas_call | solution.py:1056
  660.5 1.6 fusion.8
  662.2 1.9 slice_bitcast_fusion
  664.1 1.5 slice_reduce_fusion
  665.6 6.1 copy.45
  671.7 5.1 reshape.92
  676.8 0.0 copy-done.4
  676.8 1.1 copy.51
  677.9 0.8 copy-done.3
  678.8 1.1 copy.52
  679.9 0.0 copy-done.13
  679.9 0.6 copy.53
  680.5 0.0 copy-done.2
  680.5 1.7 copy.54
  682.2 1.4 copy-done.1
  683.5 1.7 copy.55
  (19 shorter events, 0.1 us)
Async XLA Ops:
  7.2 3.5 copy-start
  7.2 253.1 %all-gather.5.cloned.1.call-start = ((), (), s32[]{:S(2)}) async-start(), calls=%async_computation | async-start | bytes 14155776 | tf_op jit(solution)/shard_map/all_gather | solution.py:1149
  10.6 249.7 %all-gather.7.cloned.1.call-start = ((), (), s32[]{:S(2)}) async-start(), calls=%async_computation.1 | async-start | bytes 14155776 | tf_op jit(solution)/shard_map/all_gather | solution.py:1150
  12.1 3.5 copy-start.16
  12.1 3.7 copy-start.14
  12.1 4.3 copy-start.15
  12.1 4.9 copy-start.7
  12.1 4.9 copy-start.8
  12.1 4.9 copy-start.12
  12.1 16.3 %copy-start.5 = (f32[192,384]{1,0:T(8,128)S(1)}, f32[192,384]{1,0:T(8,128)}, u32[]{:S(2)}) copy-start(f32[192,384]{1,0:T(8,128)} %param.17) | copy-start | bytes 884740
  12.1 17.5 %copy-start.10 = (s32[1024,2]{0,1:T(2,128)S(1)}, s32[1024,2]{0,1:T(2,128)}, u32[]{:S(2)}) copy-start(s32[1024,2]{0,1:T(2,128)} %param.28) | copy-start | bytes 24580
  12.2 248.2 %all-gather.9.cloned.1.call-start = ((), (), s32[]{:S(2)}) async-start(), calls=%async_computation.2 | async-start | bytes 14155776 | tf_op jit(solution)/shard_map/all_gather | solution.py:1151
  15.5 14.6 %copy-start.9 = (s32[8192]{0:T(1024)S(1)}, s32[8192]{0:T(1024)}, u32[]{:S(2)}) copy-start(s32[8192]{0:T(1024)} %param.27) | copy-start | bytes 98308
  15.5 19.7 %copy-start.6 = (f32[384,192]{0,1:T(8,128)S(1)}, f32[384,192]{0,1:T(8,128)}, u32[]{:S(2)}) copy-start(f32[384,192]{0,1:T(8,128)} %param.20) | copy-start | bytes 884740
  28.6 9.3 %copy-start.11 = (s32[1024]{0:T(1024)}, s32[1024]{0:T(1024)S(1)}, u32[]{:S(2)}) copy-start(s32[1024]{0:T(1024)S(1)} %convert_reduce_fusion.3) | copy-start | bytes 12292
  671.7 5.1 copy-start.4
  676.8 2.0 copy-start.3
  676.8 3.1 copy-start.13
  676.8 3.7 copy-start.2
  680.5 3.0 copy-start.1
Sparse Core Ops, SparseCore 0:
  10.8 92.4 all-gather.4
  105.7 70.3 all-gather.6
  178.6 79.3 all-gather.8

commit v4 on v3

--- a/solution.py
+++ b/solution.py
@@ -11,6 +11,7 @@
 HD = 64
 E = 16
 CAP = 256
+CUTS = 4
 MESH = pl.DeviceIdType.MESH
 
 
@@ -52,98 +53,127 @@
 TN = ((0,), (0,))
 
 
-def expert_step(width, e, refs):
-    (second, grad, gate_w, up_w, down_w, gate_out, up_out, down_out, rank, gates, dots, mixed, back) = refs
-    rows = second.shape[0]
+def expert_step(width, start, count, refs):
+    (x_all, grad_all, gate_all, dots, gate_w, up_w, down_w, gate_out, up_out, down_out) = refs
     low = jnp.bfloat16
-    place = lax.broadcasted_iota(jnp.int32, (width, rows), 0).astype(jnp.float32)
-    hit = place == rank[pl.ds(e, 1), :]
-    pick = jnp.where(hit, 1.0, 0.0).astype(low)
-    gate = jnp.sum(jnp.where(hit, gates[pl.ds(e, 1), :], 0.0), axis=1, keepdims=True)
-    x = mm(pick, second[...]).astype(low)
-    grad_rows = mm(pick, grad[...])
+    span = pl.ds(start, width)
+    valid = lax.broadcasted_iota(jnp.int32, (width, 1), 0) < count
+    gate = jnp.where(valid, gate_all[span, :], 0.0)
+    x = x_all[span, :]
+    grad_rows = grad_all[span, :]
     gate_part = mm(x, gate_w[0])
     up_part = mm(x, up_w[0])
     sigma = jax.nn.sigmoid(gate_part)
     hidden = (gate_part * sigma * up_part).astype(low)
     each = mm(hidden, down_w[0])
-    dot = jnp.sum(grad_rows * each, axis=1, keepdims=True)
-    dots[pl.ds(e, 1), :] = jnp.sum(jnp.where(hit, dot, 0.0), axis=0, keepdims=True)
-    mixed[...] += mm(pick, (each * gate).astype(low), TN)
-    grad_each = (grad_rows * gate).astype(low)
+    grad_rows_wide = grad_rows.astype(jnp.float32)
+    dots[span, :] = jnp.sum(grad_rows_wide * each, axis=1, keepdims=True)
+    grad_each = (grad_rows_wide * gate).astype(low)
+    grad_all[span, :] = jnp.where(valid, (each * gate).astype(low), grad_rows)
     grad_hidden = mm(grad_each, down_w[0], NT)
     grad_gate = (grad_hidden * up_part * sigma * (1.0 + gate_part * (1.0 - sigma))).astype(low)
     grad_up = (grad_hidden * gate_part * sigma).astype(low)
     down_grad = mm(hidden, grad_each, TN).astype(low)
     high, wide = down_grad.shape
-    subs, span = down_out.shape[2], high // 4 // down_out.shape[2]
+    subs, rows = down_out.shape[2], high // 4 // down_out.shape[2]
     for chunk in range(4):
         for sub in range(subs):
-            row = (chunk * subs + sub) * span
+            row = (chunk * subs + sub) * rows
             for column in range(wide // high):
-                down_out[0, chunk, sub, column * span : (column + 1) * span, :] = down_grad[
-                    row : row + span, column * high : (column + 1) * high
+                down_out[0, chunk, sub, column * rows : (column + 1) * rows, :] = down_grad[
+                    row : row + rows, column * high : (column + 1) * high
                 ]
     gate_out[0] = mm(x, grad_gate, TN).astype(low)
     up_out[0] = mm(x, grad_up, TN).astype(low)
     back_rows = mm(grad_gate, gate_w[0], NT) + mm(grad_up, up_w[0], NT)
-    back[...] += mm(pick, back_rows.astype(low), TN)
-
-
-def expert_kernel(counts, code, router, second, grad, gate_w, up_w, down_w,
+    x_all[span, :] = jnp.where(valid, back_rows.astype(low), x)
+
+
+def expert_kernel(counts, starts, code, base, router, second, grad, gate_w, up_w, down_w,
                   mixed_out, back_out, gate_out, up_out, down_out, router_out,
-                  rank, gates, dots, mixed, back):
+                  slot, gates, x_all, grad_all, gate_all, dots):
     e = pl.program_id(0)
     rows = second.shape[0]
     low = jnp.bfloat16
+    tile = CAP
+    tiles = x_all.shape[0] // tile - 1
     expert = lax.broadcasted_iota(jnp.int32, (E, rows), 0)
-    first_id = code[...] // E
-    second_id = code[...] % E
-    picks = [jnp.where(expert == ids, 1.0, 0.0) for ids in (first_id, second_id)]
+    picks = [jnp.where(expert == ids, 1.0, 0.0) for ids in (code[...] // E, code[...] % E)]
+    own = lambda pick, values: jnp.sum(pick * values, axis=0, keepdims=True)
 
     @pl.when(e == 0)
     def _():
         logits = mm(router[...], second[...], NT)
-        chosen = [jnp.sum(pick * logits, axis=0, keepdims=True) for pick in picks]
+        chosen = [own(pick, logits) for pick in picks]
         top = jnp.maximum(chosen[0], chosen[1])
         raised = [jnp.exp(value - top) for value in chosen]
         total = raised[0] + raised[1]
-        gates[...] = picks[0] * (raised[0] / total) + picks[1] * (raised[1] / total)
-        hits = picks[0] + picks[1]
         earlier = lax.broadcasted_iota(jnp.int32, (rows, rows), 0) < lax.broadcasted_iota(
             jnp.int32, (rows, rows), 1
         )
-        before = mm(hits.astype(low), jnp.where(earlier, 1.0, 0.0).astype(low))
-        rank[...] = jnp.where(hits > 0.0, before, -1.0)
-        mixed[...] = jnp.zeros_like(mixed)
-        back[...] = jnp.zeros_like(back)
-
-    refs = (second, grad, gate_w, up_w, down_w, gate_out, up_out, down_out, rank, gates, dots, mixed, back)
+        before = mm((picks[0] + picks[1]).astype(low), jnp.where(earlier, 1.0, 0.0).astype(low)) + base[...]
+        for k in (0, 1):
+            gates[k : k + 1, :] = raised[k] / total
+            slot[k : k + 1, :] = own(picks[k], before)
+
+        def pick_tile(number, _):
+            span = pl.ds(pl.multiple_of(number * tile, tile), tile)
+            place = (lax.broadcasted_iota(jnp.int32, (tile, rows), 0) + number * tile).astype(jnp.float32)
+            hits = [place == slot[k : k + 1, :] for k in (0, 1)]
+            pick = jnp.where(hits[0] | hits[1], 1.0, 0.0).astype(low)
+            scaled = jnp.where(hits[0], gates[0:1, :], 0.0) + jnp.where(hits[1], gates[1:2, :], 0.0)
+            gate_all[span, :] = jnp.sum(scaled, axis=1, keepdims=True)
+            x_all[span, :] = mm(pick, second[...]).astype(low)
+            grad_all[span, :] = mm(pick, grad[...]).astype(low)
+            return 0
+
+        lax.fori_loop(0, tiles, pick_tile, 0)
+        x_all[tiles * tile :, :] = jnp.zeros((tile, D), low)
+        grad_all[tiles * tile :, :] = jnp.zeros((tile, D), low)
+        gate_all[tiles * tile :, :] = jnp.zeros((tile, 1), jnp.float32)
+
+    refs = (x_all, grad_all, gate_all, dots, gate_w, up_w, down_w, gate_out, up_out, down_out)
     count = counts[e]
-
-    @pl.when(count <= CAP // 2)
-    def _():
-        expert_step(CAP // 2, e, refs)
-
-    @pl.when(count > CAP // 2)
-    def _():
-        expert_step(CAP, e, refs)
+    start = pl.multiple_of(starts[e], 16)
+    widths = (CAP // 2, CAP)
+    for less, width in zip((-1,) + widths, widths):
+
+        @pl.when((count > less) & (count <= width))
+        def _(width=width):
+            expert_step(width, start, count, refs)
 
     @pl.when(e == E - 1)
     def _():
-        grad_gates = [jnp.sum(pick * dots[...], axis=0, keepdims=True) for pick in picks]
-        own = [jnp.sum(pick * gates[...], axis=0, keepdims=True) for pick in picks]
-        inner = own[0] * grad_gates[0] + own[1] * grad_gates[1]
-        grad_logits = picks[0] * (own[0] * (grad_gates[0] - inner)) + picks[1] * (
-            own[1] * (grad_gates[1] - inner)
+        def dots_tile(number, totals):
+            span = pl.ds(pl.multiple_of(number * tile, tile), tile)
+            place = (lax.broadcasted_iota(jnp.int32, (tile, rows), 0) + number * tile).astype(jnp.float32)
+            return tuple(
+                totals[k] + jnp.sum(jnp.where(place == slot[k : k + 1, :], dots[span, :], 0.0), axis=0, keepdims=True)
+                for k in (0, 1)
+            )
+
+        zero = jnp.zeros((1, rows), jnp.float32)
+        grad_gates = lax.fori_loop(0, tiles, dots_tile, (zero, zero))
+        shares = [gates[k : k + 1, :] for k in (0, 1)]
+        inner = shares[0] * grad_gates[0] + shares[1] * grad_gates[1]
+        grad_logits = picks[0] * (shares[0] * (grad_gates[0] - inner)) + picks[1] * (
+            shares[1] * (grad_gates[1] - inner)
         )
-        grad_logits = grad_logits.astype(low)
-        router_grad = mm(grad_logits, second[...])
+        router_grad = mm(grad_logits.astype(low), second[...])
         for owner in range(router_out.shape[0]):
             span = router_out.shape[2]
             router_out[owner] = router_grad[:, owner * span : (owner + 1) * span]
-        mixed_out[...] = mixed[...].astype(low)
-        back_out[...] = (back[...] + mm(grad_logits, router[...], TN)).astype(low)
+        columns = jnp.transpose(jnp.concatenate([slot[...], grad_logits], axis=0))
+        block = rows // 4
+        place = lax.broadcasted_iota(jnp.int32, (block, tiles * tile), 1).astype(jnp.float32)
+        for number in range(4):
+            part = columns[number * block : (number + 1) * block, :]
+            hit = (place == part[:, 0:1]) | (place == part[:, 1:2])
+            put = jnp.where(hit, 1.0, 0.0).astype(low)
+            span = pl.ds(number * block, block)
+            mixed_out[span, :] = mm(put, grad_all[: tiles * tile, :]).astype(low)
+            routed = mm(part[:, 8:].astype(low), router[...])
+            back_out[span, :] = (mm(put, x_all[: tiles * tile, :]) + routed).astype(low)
 
 
 def experts(groups, second, grad, code, counts, router, gate_w, up_w, down_w):
@@ -151,18 +181,23 @@
     rows = second.shape[0]
     hidden = gate_w.shape[2]
     low = jnp.bfloat16
+    taken = (counts + 15) // 16 * 16
+    starts = jnp.cumsum(taken) - taken
+    packed = -(-(2 * rows + 16 * E) // CAP) * CAP + CAP
     whole = lambda e, *_: (0, 0)
     by_expert = lambda e, *_: (e, 0, 0)
     wide = pl.BlockSpec((1, D, hidden), by_expert)
     tall = pl.BlockSpec((1, hidden, D), by_expert)
-    block = pl.BlockSpec((rows, D), whole)
+    block = pl.BlockSpec((rows, D), whole, pipeline_mode=pl.Buffered(1))
+    out = pl.BlockSpec((rows, D), whole)
     return pl.pallas_call(
         expert_kernel,
         grid_spec=pltpu.PrefetchScalarGridSpec(
-            num_scalar_prefetch=1,
+            num_scalar_prefetch=2,
             grid=(E,),
             in_specs=[
                 pl.BlockSpec((1, rows), whole),
+                pl.BlockSpec((E, 1), whole),
                 pl.BlockSpec((E, D), whole),
                 block,
                 block,
@@ -171,19 +206,20 @@
                 tall,
             ],
             out_specs=[
-                block,
-                block,
+                out,
+                out,
                 wide,
                 wide,
                 pl.BlockSpec((1, 4, 4 // per, D // groups, hidden), lambda e, *_: (e // per, 0, e % per, 0, 0)),
                 pl.BlockSpec((groups, E, D // groups), lambda e, *_: (0, 0, 0)),
             ],
             scratch_shapes=[
-                pltpu.VMEM((E, rows), jnp.float32),
-                pltpu.VMEM((E, rows), jnp.float32),
-                pltpu.VMEM((E, rows), jnp.float32),
-                pltpu.VMEM((rows, D), jnp.float32),
-                pltpu.VMEM((rows, D), jnp.float32),
+                pltpu.VMEM((8, rows), jnp.float32),
+                pltpu.VMEM((8, rows), jnp.float32),
+                pltpu.VMEM((packed, D), low),
+                pltpu.VMEM((packed, D), low),
+                pltpu.VMEM((packed, 1), jnp.float32),
+                pltpu.VMEM((packed, 1), jnp.float32),
             ],
         ),
         out_shape=[
@@ -198,11 +234,11 @@
             dimension_semantics=("arbitrary",), vmem_limit_bytes=58 * 2**20
         ),
         cost_estimate=pl.CostEstimate(
-            flops=E * CAP * D * (18 * hidden + 8 * rows),
+            flops=2 * rows * D * (18 * hidden + 8 * rows),
             bytes_accessed=12 * E * D * hidden + 8 * rows * D,
-            transcendentals=E * CAP * hidden,
+            transcendentals=2 * rows * hidden,
         ),
-    )(counts, code, router, second, grad, gate_w, up_w, down_w)
+    )(counts, starts, code, starts.astype(jnp.float32)[:, None], router, second, grad, gate_w, up_w, down_w)
 
 
 class CubeGather:
@@ -248,15 +284,13 @@
         ref = self.place(chunk, self.flip(self.me, have))
         pltpu.make_async_copy(ref, ref, sem).wait()
 
-    def begin(self):
-        for chunk in range(self.chunks):
-            for step in range(self.bits):
-                self.send(chunk, 0, (chunk + step) % self.bits, self.block(chunk))
-        for chunk in range(self.chunks):
-            self.pair(chunk, 0, self.block(chunk))
-            copy = pltpu.make_async_copy(self.block(chunk), self.place(chunk, self.me), self.own_sem.at[chunk])
-            copy.start()
-            self.waits.append(copy.wait)
+    def begin(self, chunk):
+        for step in range(self.bits):
+            self.send(chunk, 0, (chunk + step) % self.bits, self.block(chunk))
+        self.pair(chunk, 0, self.block(chunk))
+        copy = pltpu.make_async_copy(self.block(chunk), self.place(chunk, self.me), self.own_sem.at[chunk])
+        copy.start()
+        self.waits.append(copy.wait)
 
     def events(self):
         found = []
@@ -481,9 +515,11 @@
 
 
 def forward_kernel(groups, parts, heads, heads_kv, home, seg_row, seg_col, attn_gain, moe_gain, tokens, out_grad, wpack,
-                   middle, first_out, qkv_out, mix_out, weights_out, second_out, grad_out,
+                   gate_in, up_in, down_in,
+                   middle, router_out, first_out, qkv_out, mix_out, weights_out, second_out, grad_out, gate_full, up_full, down_full,
                    first, second, grad, weights, qkv, mix, part, come, bias, sorted_second, sorted_grad, dealt_second, dealt_grad,
-                   gather_sems, line_out, line_in, sum_out, sum_in, deal_out, deal_in, save_sem):
+                   wide_load, tall_load, gate_low, up_low, down_low,
+                   gather_sems, moe_sems, line_out, line_in, sum_out, sum_in, deal_out, deal_in, save_sem, load_sem):
     low = jnp.bfloat16
     shard, width = tokens.shape
     me, place = lax.axis_index("dp"), lax.axis_index("mp")
@@ -505,11 +541,12 @@
         lambda chunk, owner: weights.at[pl.ds(owner * block + chunk * cut, cut)],
         gather_sems,
     )
-    gather.begin()
+    for chunk in range(2):
+        gather.begin(chunk)
     values = tokens[...]
     first[place] = (values * scale_of(values) * attn_gain[...]).astype(low)
-    lines = [LineGather(parts, 2, held, line_out.at[n], line_in.at[n]) for n, held in enumerate((first, grad, second))]
-    for chunk in range(2):
+    lines = [LineGather(parts, CUTS, held, line_out.at[n], line_in.at[n]) for n, held in enumerate((first, grad, second))]
+    for chunk in range(CUTS):
         lines[0].begin(chunk)
     sort = sorting(home[...], shard)
     sorted_grad[...] = mm(sort, out_grad[...].astype(low)).astype(sorted_grad.dtype)
@@ -518,7 +555,48 @@
     deal_grad = Exchange(groups, sorted_grad, dealt_grad, deal_out.at[0], deal_in.at[0])
     deal_grad.begin()
     gather.finish()
-    save(0, weights, weights_out)
+
+    count = gate_in.shape[0] // 4
+    per, hidden, _ = down_in.shape
+    high = hidden // 4
+
+    def place_of(chunk, owner):
+        if chunk < 2 * count:
+            full = (gate_full, up_full)[chunk // count]
+            return full.at[pl.ds(chunk % count * 4, 4), pl.ds(owner * block, block)]
+        return down_full.at[pl.ds(owner * per, per), pl.ds((chunk - 2 * count) * high, high)]
+
+    def block_of(chunk, arrays):
+        if chunk < 2 * count:
+            return arrays[chunk // count].at[pl.ds(chunk % count * 4, 4)]
+        return arrays[2].at[:, pl.ds((chunk - 2 * count) * high, high)]
+
+    moe = CubeGather(groups, 2 * count + 4, lambda chunk: block_of(chunk, (gate_low, up_low, down_low)), place_of, moe_sems)
+
+    def load(chunk):
+        held = (wide_load if chunk < 2 * count else tall_load).at[chunk % 2]
+        copy = pltpu.make_async_copy(block_of(chunk, (gate_in, up_in, down_in)), held, load_sem.at[chunk % 2])
+        copy.start()
+        return copy, held
+
+    loaded = [load(0)]
+    for chunk in range(moe.chunks):
+        if chunk + 1 < moe.chunks:
+            loaded.append(load(chunk + 1))
+        copy, held = loaded[chunk]
+        copy.wait()
+        target = block_of(chunk, (gate_low, up_low, down_low))
+
+        def row(index, _):
+            target[index] = held[index].astype(low)
+            return 0
+
+        lax.fori_loop(0, held.shape[0], row, 0)
+        moe.begin(chunk)
+    events = moe.events()
+    save(0, weights.at[:, : weights_out.shape[1]], weights_out)
+    router = weights[:, weights_out.shape[1] :].astype(jnp.float32)
+    router_out[...] = jnp.transpose(router)[:E, :].astype(low)
 
     def project(origin):
         result = mm(first[origin], weights[:, : (heads + 2 * heads_kv) * HD])
@@ -528,19 +606,20 @@
 
     project(place)
     for distance in range(1, parts):
-        for chunk in range(2):
+        if distance == parts - 1:
+            deal_grad.arrive()
+            grad[place] = dealt_grad[...].astype(low)
+            for chunk in range(CUTS):
+                lines[1].begin(chunk)
+        for chunk in range(CUTS):
             for way in (0, 1):
                 lines[0].step(distance, way, chunk)
         for way in (0, 1):
             lines[0].from_side(distance, way, project)
-    deal_grad.arrive()
-    grad[place] = dealt_grad[...].astype(low)
-    for chunk in range(2):
-        lines[1].begin(chunk)
     save(1, first, first_out)
     save(2, qkv, qkv_out)
 
-    sums = LineSum(parts, 2, part, come, sum_out, sum_in)
+    sums = LineSum(parts, CUTS, part, come, sum_out, sum_in)
     order = far_first(parts)
     reach = -(-512 // shard)
     for number, target in enumerate(order):
@@ -559,34 +638,42 @@
 
         lax.fori_loop(0, heads, attend, 0)
         flat = jnp.concatenate([mix[head, start:stop, :] for head in range(heads)], axis=1)
-        part[target] = mm(flat, weights[:, (heads + 2 * heads_kv) * HD :], NT).astype(low)
+        part[target] = mm(flat, weights[:, (heads + 2 * heads_kv) * HD : weights_out.shape[1]], NT).astype(low)
         sums.begin(target)
-        if number < parts - 1:
-            for chunk in range(2):
+    save(3, mix, mix_out)
+    for number, target in enumerate(order):
+        for chunk in range(CUTS):
+            if number < parts - 1:
                 for way in (0, 1):
                     lines[1].step(number + 1, way, chunk)
-    save(3, mix, mix_out)
-    for target in order:
-        for chunk in range(2):
             sums.relay(sums.turned(target), chunk)
-    for chunk in range(2):
+    for chunk in range(CUTS):
         sums.total(chunk, middle)
     values = tokens[...] + middle[...]
     middle[...] = values
     normed = (values * scale_of(values) * moe_gain[...]).astype(low)
     sorted_second[...] = mm(sort, normed).astype(sorted_second.dtype)
     deal = Exchange(groups, sorted_second, dealt_second, deal_out.at[1], deal_in.at[1])
+    for event in events[:4]:
+        event()
     deal.begin()
     save(4, grad, grad_out)
+    singles = moe.bits * moe.chunks
+    for event in events[4:singles]:
+        event()
     deal.arrive()
     second[place] = dealt_second[...].astype(low)
-    for chunk in range(2):
+    for chunk in range(CUTS):
         lines[2].begin(chunk)
-    for distance in range(1, parts):
-        for chunk in range(2):
-            for way in (0, 1):
-                lines[2].step(distance, way, chunk)
+    rest = events[singles:]
+    turns = (parts - 1) * CUTS
+    for turn in range(turns):
+        for way in (0, 1):
+            lines[2].step(1 + turn // CUTS, way, turn % CUTS)
+        for event in rest[turn * len(rest) // turns : (turn + 1) * len(rest) // turns]:
+            event()
     save(5, second, second_out)
+    moe.finish()
     for line in lines:
         line.finish()
     sums.finish()
@@ -596,28 +683,35 @@
         copy.wait()
 
 
-def forward(groups, parts, home, seg, attn_gain, moe_gain, tokens, out_grad, wpack, heads, heads_kv):
+def forward(groups, parts, home, seg, attn_gain, moe_gain, tokens, out_grad, wpack, w_gate, w_up, w_down, heads, heads_kv):
     shard, width = tokens.shape
     rows = shard * parts
     low = jnp.bfloat16
     slots = heads + 2 * heads_kv
     columns = wpack.shape[1]
+    block, hidden = w_gate.shape[1:]
+    per = w_down.shape[0]
+    chunks = 2 * (E // 4) + 4
     vmem = pl.BlockSpec(memory_space=pltpu.VMEM)
     hbm = pl.BlockSpec(memory_space=pl.ANY)
     dma = pltpu.SemaphoreType.DMA
     held = lambda: pltpu.VMEM((parts, shard, width), low)
     return pl.pallas_call(
         functools.partial(forward_kernel, groups, parts, heads, heads_kv),
-        in_specs=[vmem] * 7 + [hbm],
-        out_specs=[vmem] + [hbm] * 6,
+        in_specs=[vmem] * 7 + [hbm] * 4,
+        out_specs=[vmem] * 2 + [hbm] * 9,
         out_shape=[
             jax.ShapeDtypeStruct((shard, width), jnp.float32),
+            jax.ShapeDtypeStruct((E, width), low),
             jax.ShapeDtypeStruct((parts, shard, width), low),
             jax.ShapeDtypeStruct((slots, rows, HD), low),
             jax.ShapeDtypeStruct((heads, rows, HD), low),
-            jax.ShapeDtypeStruct((width, columns), low),
+            jax.ShapeDtypeStruct((width, columns - 128), low),
             jax.ShapeDtypeStruct((parts, shard, width), low),
             jax.ShapeDtypeStruct((parts, shard, width), low),
+            jax.ShapeDtypeStruct((E, width, hidden), low),
+            jax.ShapeDtypeStruct((E, width, hidden), low),
+            jax.ShapeDtypeStruct((E, hidden, width), low),
         ],
         scratch_shapes=[
             held(),
@@ -630,14 +724,21 @@
             pltpu.VMEM((parts + 1, shard, width), low),
             pltpu.VMEM((shard, shard * (1 - (-512 // shard))), jnp.float32),
             *[pltpu.VMEM((shard, width), row_type(shard // groups))] * 4,
+            pltpu.VMEM((2, 4, block, hidden), jnp.float32),
+            pltpu.VMEM((2, per, hidden // 4, width), jnp.float32),
+            pltpu.VMEM((E, block, hidden), low),
+            pltpu.VMEM((E, block, hidden), low),
+            pltpu.VMEM((per, hidden, width), low),
             cube_sems(groups, 2),
-            dma((3, 2, parts, 2)),
-            dma((3, parts, 2)),
-            dma((parts, 2)),
-            dma((parts + 1, 2)),
+            cube_sems(groups, chunks),
+            dma((3, 2, parts, CUTS)),
+            dma((3, parts, CUTS)),
+            dma((parts, CUTS)),
+            dma((parts + 1, CUTS)),
             dma((2, groups)),
             dma((2, groups)),
             dma((6,)),
+            dma((2,)),
         ],
         compiler_params=pltpu.CompilerParams(
             collective_id=0, has_side_effects=True, vmem_limit_bytes=56 * 2**20
@@ -645,7 +746,8 @@
         cost_estimate=pl.CostEstimate(
             flops=12 * rows * width * columns, bytes_accessed=60 * 2**20, transcendentals=rows * rows * heads
         ),
-    )(home, seg[None, :], seg[:, None], attn_gain[None, :], moe_gain[None, :], tokens, out_grad, wpack)
+    )(home, seg[None, :], seg[:, None], attn_gain[None, :], moe_gain[None, :], tokens, out_grad, wpack,
+      w_gate, w_up, w_down)
 
 
 class CubeSum:
@@ -782,9 +884,9 @@
         if want:
             self.sent.append(self.cube.send(chunk, want, target))
         else:
-            copy = pltpu.make_async_copy(target, self.out(chunk), self.save_sem.at[place])
-            copy.start()
-            self.saved.append(copy.wait)
+            for source, result in self.out(chunk, target):
+                pltpu.make_async_copy(source, result, self.save_sem.at[place]).start()
+            self.saved.append(pltpu.make_async_copy(target, target, self.save_sem.at[place]).wait)
 
     def finish(self):
         self.tick(len(self.list) + 1 - self.at)
@@ -860,10 +962,25 @@
         return step_held.at[chunk, places.setdefault((chunk, step, want), len([k for k in places if k[0] == chunk]))]
 
     cube = CubeSum(groups, 3 * count, own, lambda chunk, want: pair_held.at[chunk, want], step_place, cube_sems)
-    out = lambda chunk: (gate_out, up_out, down_out)[chunk // count].at[chunk % count]
+    per, hidden, _ = down_out.shape
+    subs = 4 // per
+    span = hidden // 4 // subs
+
+    def out(chunk, total):
+        if chunk < 2 * count:
+            return [(total, (gate_out, up_out)[chunk // count].at[pl.ds(chunk % count * 4, 4)])]
+        found = []
+        for index in range(4):
+            row = (chunk - 2 * count) * (hidden // 4) + index % subs * span
+            for column in range(width // hidden):
+                source = total.at[index, pl.ds(column * span, span)]
+                target = down_out.at[index // subs, pl.ds(row, span), pl.ds(column * hidden, hidden)]
+                found.append((source, target))
+        return found
+
     stream = Stream(cube, 3, terms, sums, totals, out, term_sem, save_sem)
 
-    back = LineSum(parts, 2, held, come, sum_out.at[0], sum_in.at[0])
+    back = LineSum(parts, CUTS, held, come, sum_out.at[0], sum_in.at[0])
     loads[0].wait()
     order = far_first(parts)
     for target in order:
@@ -872,21 +989,17 @@
         cube.pair(chunk)
     routers = Share("dp", groups, router_all, share_out.at[0], share_in.at[0], lambda peer: router_part.at[peer])
     routers.begin()
-    stream.tick(3)
+    stream.tick(1)
     for target in order:
-        for chunk in range(2):
+        for chunk in range(CUTS):
             back.relay(back.turned(target), chunk)
-            stream.tick(2 if target != order[-1] else 0)
-    for chunk in range(2):
+            stream.tick(1 if target in order[:2] else 0)
+    for chunk in range(CUTS):
         back.total(chunk, block_out)
     stage[...] = block_out[...].astype(stage.dtype)
     deal = Exchange(groups, stage, land_back, deal_out.at[0], deal_in.at[0])
     deal.begin()
     back.finish()
-    loads[4].wait()
-    extra = LineSum(parts, 2, mixed, mixed_come, sum_out.at[1], sum_in.at[1])
-    for target in order:
-        extra.begin(extra.turned(target))
     router_line[place] = routers.total()
     router_sums = Share("mp", parts, router_line, share_out.at[1], share_in.at[1], lambda peer: router_line.at[place])
     for turn in range(1, parts):
@@ -902,11 +1015,14 @@
     grad_middle = out_grad[...] + (scale * weighted - values * (scale * scale * scale * inner))
     tokens_grad[...] = grad_middle
     grad[place] = grad_middle.astype(low)
-    line = LineGather(parts, 2, grad, line_out, line_in)
-    for chunk in range(2):
+    line = LineGather(parts, CUTS, grad, line_out, line_in)
+    for chunk in range(CUTS):
         line.begin(chunk)
+    loads[4].wait()
+    extra = LineSum(parts, CUTS, mixed, mixed_come, sum_out.at[1], sum_in.at[1])
+    for target in order:
+        extra.begin(extra.turned(target))
     loads[1].wait()
-    loads[2].wait()
 
     def mix_back(origin):
         result = mm(grad[origin], weights[:, slots * HD :])
@@ -917,34 +1033,19 @@
     mix_back(place)
     stream.tick(2)
     for distance in range(1, parts):
-        for chunk in range(2):
+        for chunk in range(CUTS):
             for way in (0, 1):
                 line.step(distance, way, chunk)
-            extra.relay(extra.turned(order[distance - 1]), chunk)
-            stream.tick(3)
+            stream.tick()
         for way in (0, 1):
             line.from_side(distance, way, mix_back)
-    for chunk in range(2):
-        extra.relay(extra.turned(order[parts - 1]), chunk)
-    mix_flat = jnp.concatenate([mix[head] for head in range(heads)], axis=1)
-    pack[:, slots * HD :] = mm(grad[...].reshape(parts * shard, width), mix_flat, TN).astype(low)
-    deal.finish()
-    for chunk in range(2):
-        extra.total(chunk, block_out)
-    stage[...] = block_out[...].astype(stage.dtype)
-    deal_mixed = Exchange(groups, stage, land_mixed, deal_out.at[1], deal_in.at[1])
-    deal_mixed.begin()
     loads[3].wait()
-    extra.finish()
-    first_load = pltpu.make_async_copy(first_in, mixed, load_sem.at[5])
-    first_load.start()
-    stream.tick(2)
-
-    first_sum = LineSum(parts, 2, held, come, sum_out.at[2], sum_in.at[2])
+
+    first_sum = LineSum(parts, CUTS, held, come, sum_out.at[2], sum_in.at[2])
     grad_key[...] = jnp.zeros_like(grad_key)
     grad_value[...] = jnp.zeros_like(grad_value)
     reach = -(-512 // shard)
-    for target in reversed(range(parts)):
+    for number, target in enumerate(reversed(range(parts))):
         start, stop = target * shard, (target + 1) * shard
         bottom = max(0, target - reach) * shard
         bias[:, : stop - bottom] = bias_of(seg_row, seg_col, start, bottom, stop)
@@ -972,7 +1073,26 @@
         flat[start:stop, :] = jnp.concatenate(pieces, axis=1)
         held[target] = mm(flat[start:stop, :], weights[:, : slots * HD], NT).astype(low)
         first_sum.begin(target)
-        stream.tick(2)
+        for chunk in range(CUTS):
+            extra.relay(extra.turned(order[number]), chunk)
+            if number > 0:
+                first_sum.relay(target + 1, chunk)
+            stream.tick(1)
+    loads[2].wait()
+    mix_flat = jnp.concatenate([mix[head] for head in range(heads)], axis=1)
+    pack[:, slots * HD :] = mm(grad[...].reshape(parts * shard, width), mix_flat, TN).astype(low)
+    for chunk in range(CUTS):
+        first_sum.relay(0, chunk)
+        extra.total(chunk, block_out)
+        stream.tick()
+    deal.finish()
+    stage[...] = block_out[...].astype(stage.dtype)
+    deal_mixed = Exchange(groups, stage, land_mixed, deal_out.at[1], deal_in.at[1])
+    deal_mixed.begin()
+    extra.finish()
+    first_load = pltpu.make_async_copy(first_in, mixed, load_sem.at[5])
+    first_load.start()
+    stream.tick(2)
     first_load.wait()
     pack[:, : slots * HD] = mm(mixed[...].reshape(parts * shard, width), flat[...], TN).astype(low)
     cut = owner_rows // 2
@@ -991,12 +1111,11 @@
     )
     for chunk in range(2):
         pack_cube.pair(chunk)
-    for target in reversed(range(parts)):
-        for chunk in range(2):
-            first_sum.relay(target, chunk)
-        stream.tick(2)
+    deal_mixed.arrive()
+    home_rows = mm(sort, land_mixed[...].astype(low), TN)
     pack_sent = []
     for chunk, want in pack_cube.items(1):
+        stream.tick(1)
         refs = pack_cube.terms(chunk, want)
         total = refs[0][...].astype(jnp.float32)
         for ref in refs[1:]:
@@ -1006,7 +1125,7 @@
             pack_sent.append(pack_cube.send(chunk, want, refs[0]))
         else:
             pack_out[chunk * cut : (chunk + 1) * cut, :] = total
-    for chunk in range(2):
+    for chunk in range(CUTS):
         first_sum.total(chunk, block_out)
     grad_first = block_out[...]
     values = tokens[...]
@@ -1017,8 +1136,7 @@
     gains_lines = Share("mp", parts, gains_line, share_out.at[2], share_in.at[2], lambda peer: gains)
     gains_lines.begin()
     tokens_grad[...] += scale * weighted - values * (scale * scale * scale * inner)
-    deal_mixed.arrive()
-    block_out[...] = middle[...] + mm(sort, land_mixed[...].astype(low), TN)
+    block_out[...] = middle[...] + home_rows
     router_out[...] = router_sums.total()
     gains[...] = gains_lines.total()
     gains_rest = Share("dp", groups, gains_all, share_out.at[3], share_in.at[3], lambda peer: gains)
@@ -1063,9 +1181,9 @@
             f32(8, width),
             f32(E, owner_rows),
             f32(owner_rows, columns),
-            f32(E // 4, *unit),
-            f32(E // 4, *unit),
-            f32(E // 4, *unit),
+            f32(E, owner_rows, hidden),
+            f32(E, owner_rows, hidden),
+            f32(E // groups, hidden, width),
             jax.ShapeDtypeStruct((chunks, 1 << bits, *unit), low),
             jax.ShapeDtypeStruct((chunks, (1 << bits) - 1, *unit), low),
         ],
@@ -1103,10 +1221,10 @@
             sum_sems(groups, 2),
             dma((2, 2 + bits)),
             dma((2,)),
-            dma((2, parts, 2)),
-            dma((parts, 2)),
-            dma((3, parts, 2)),
-            dma((3, parts + 1, 2)),
+            dma((2, parts, CUTS)),
+            dma((parts, CUTS)),
+            dma((3, parts, CUTS)),
+            dma((3, parts + 1, CUTS)),
             dma((2, groups)),
             dma((2, groups)),
             dma((4, max(groups, parts))),
@@ -1143,17 +1261,13 @@
     rows = tokens.shape[0] * parts
     low_type = jnp.bfloat16
     heads, heads_kv = w_query.shape[1] // HD, w_key.shape[1] // HD
-    wpack = jnp.concatenate([w_query, w_key, w_value, w_out.T], axis=1).astype(low_type)
-    router_w, gate_w, up_w, down_w = (
-        lax.all_gather(w_router.astype(low_type), "dp", axis=0, tiled=True),
-        lax.all_gather(w_gate.astype(low_type), "dp", axis=1, tiled=True),
-        lax.all_gather(w_up.astype(low_type), "dp", axis=1, tiled=True),
-        lax.all_gather(w_down.astype(low_type), "dp", axis=0, tiled=True),
-    )
+    wpack = jnp.concatenate(
+        [w_query, w_key, w_value, w_out.T, jnp.pad(w_router, ((0, 0), (0, 128 - E)))], axis=1
+    ).astype(low_type)
     home, code, counts = deal_tables(deal_order, expert_ids, rows)
     segment = segment_of(seq_lengths[0], rows)
-    middle, first_full, qkv, mix, weights, second_full, grad_full = forward(
-        groups, parts, home[None, :], segment, attn_gain, moe_gain, tokens, out_grad, wpack, heads, heads_kv
+    middle, router_w, first_full, qkv, mix, weights, second_full, grad_full, gate_w, up_w, down_w = forward(
+        groups, parts, home[None, :], segment, attn_gain, moe_gain, tokens, out_grad, wpack, w_gate, w_up, w_down, heads, heads_kv
     )
     mixed, back, gate_grad, up_grad, down_grad, router_part = experts(
         groups,
@@ -1161,7 +1275,7 @@
         grad_full.reshape(rows, D),
         code,
         counts,
-        router_w.T,
+        router_w,
         gate_w,
         up_w,
         down_w,
@@ -1189,10 +1303,6 @@
         up_grad,
         down_grad,
     )
-    per, hidden = w_down.shape[:2]
-    subs = 4 // per
-    down_sum = down_sum.reshape(4, per, subs, D // hidden, hidden // 4 // subs, hidden)
-    down_sum = jnp.transpose(down_sum, (1, 0, 2, 4, 3, 5))
     columns, columns_kv = heads * HD, heads_kv * HD
     return (
         block_out,
@@ -1204,9 +1314,9 @@
         pack_sum[:, columns + 2 * columns_kv :].T,
         gains[0],
         router_sum.T,
-        gate_sum.reshape(w_gate.shape),
-        up_sum.reshape(w_up.shape),
-        down_sum.reshape(w_down.shape),
+        gate_sum,
+        up_sum,
+        down_sum,
     )
 
 

time: 700 us -> 616 us (0.88)
  Pallas kernels: 623 us -> 569 us
  between operations: 14.5 us -> 1.05 us
  blocking collectives: 10.7 us -> 0 us
    pallas_call x1, Pallas kernels: 305 us -> 266 us  [backward(): pl.pallas_call(functools.partial(backward_kernel, groups, parts, heads, h...]
    reshape x2 -> x0, local copies, waits for them, and re-layouts: 11.2 us -> none  [the longest x1 6.15 us: body(): down_sum.reshape(4, per, subs, D // hidden, hidden // 4 // subs, hidden)]
    all_gather x1 -> x0, blocking collectives: 10.7 us -> none  [body(): lax.all_gather(w_router.astype(low_type), 'dp', axis=0, tiled=True)]
    pallas_call x1, Pallas kernels: 94.7 us -> 84.2 us  [experts(): pl.pallas_call(expert_kernel, grid_spec=pltpu.PrefetchScalarGridSpec(num_...]
    convert_element_type x3 -> x1, other arithmetic: 8.04 us -> 0.72 us  [experts(): starts.astype(jnp.float32)[:, None]]
  transfers between devices with their start and end apart: 3 -> 0, of which waited for: 0 -> 0; matrix products, arithmetic and copies ran while one was open for 2% -> 0% of each run, Pallas kernels for 32% -> 0%
where the time goes in v4:
time: 616 us; the launch traced here: 608 us
  Pallas kernels  569 us (92%)
  local copies, waits for them, and re-layouts  22.4 us (4%)
  other arithmetic  15 us (2%)
    pallas_call x1, Pallas kernels, backward(): pl.pallas_call(functools.partial(backward_kernel, groups, parts, heads, h...  266 us
    pallas_call x1, Pallas kernels, forward(): pl.pallas_call(functools.partial(forward_kernel, groups, parts, heads, he...  219 us
    pallas_call x1, Pallas kernels, experts(): pl.pallas_call(expert_kernel, grid_spec=pltpu.PrefetchScalarGridSpec(num_...  84.2 us
    unnamed x23, local copies, waits for them, and re-layouts  13.2 us

profile of v4, /device:TPU:0, one launch (start us, length us, event | category | flops | bytes accessed | tf_op | source)
XLA Modules:
  0.0 607.9 jit_solution(11312585253707231832)
XLA Ops:
  0.7 0.8 reduce-window.13
  1.5 4.3 select_reduce_fusion
  5.8 0.7 convert_reduce_fusion.1
  6.4 0.1 convert_reduce_fusion.3
  6.5 0.0 copy-start.5
  6.5 0.7 fusion.7
  7.2 0.5 convert_reduce_fusion
  7.7 0.8 slice_add_fusion
  8.5 1.3 select_reduce_fusion.1
  9.8 1.3 broadcast_in_dim.68.attn_gain
  11.1 1.3 broadcast_in_dim.69.moe_gain
  12.4 0.7 convert.22
  13.1 0.1 copy.48
  13.2 1.0 convert_dynamic-update-slice_fusion
  14.2 0.9 convert_dynamic-update-slice_fusion.2
  15.1 0.9 convert_dynamic-update-slice_fusion.1
  16.0 1.0 bitcast_dynamic-update-slice_fusion
  17.0 0.0 copy-start.4
  17.1 1.0 copy.55.seg_col
  18.1 0.9 copy.50
  19.0 0.3 eq.46
  19.3 0.1 convert_reduce_fusion.2.counts
  19.4 0.0 copy-start.7
  19.4 0.1 copy.51
  19.6 0.7 subtract_convert_fusion
  20.3 0.5 multiply_subtract_fusion.starts
  20.8 0.0 copy-done.5
  20.8 0.0 copy-done.4
  20.8 218.7 %shard_map.238 = (f32[256,1536]{1,0:T(8,128)}, bf16[16,1536]{1,0:T(8,128)(2,1)}, bf16[4,256,1536]{2,1,0:T(8,128)(2,1)}, bf16[10,1024,64]{2,1,0:T(8,128)(2,1)}, b...) custom-call(s32[1,256]{1,0:T(1,128)} %bitcast.24, ...), custom_call_target="tpu_custom_call" | custom-call | flops 21743271936 | bytes 62914560 | tf_op jit(solution)/shard_map/pallas_call | solution.py:699
  239.5 0.0 copy-done.7
  239.5 84.2 %shard_map.239 = (bf16[1024,1536]{1,0:T(8,128)(2,1)}, bf16[1024,1536]{1,0:T(8,128)(2,1)}, bf16[16,1536,256]{2,1,0:T(8,128)(2,1)}, bf16[16,1536,256]{2,1,0:T(8,12...) custom-call(s32[16]{0:T(128)} %copy-done.7, s32[16]{0:T(128)} %multiply_subtract_fusion.starts, ...), custom_call_target="tpu_custom_call" | custom-call | flops 40265318400 | bytes 88080384 | tf_op jit(solution)/shard_map/pallas_call | solution.py:193
  323.8 266.5 %shard_map.240 = (f32[256,1536]{1,0:T(8,128)}, f32[256,1536]{1,0:T(8,128)}, f32[8,1536]{1,0:T(8,128)}, f32[16,192]{1,0:T(8,128)}, f32[192,1024]{1,0:T(8,128)}, /...) custom-call(s32[1,256]{1,0:T(1,128)} %bitcast.25, ...), custom_call_target="tpu_custom_call" | custom-call | flops 38654705664 | bytes 209715200 | tf_op jit(solution)/shard_map/pallas_call | solution.py:1174
  590.2 0.0 copy-start.3
  590.2 1.6 slice_reduce_fusion
  591.8 1.6 fusion.11
  593.4 1.9 slice_bitcast_fusion
  595.4 0.0 copy-start.6
  595.4 0.0 copy-start.2
  595.4 2.8 copy.66
  598.2 0.0 copy-done.3
  598.2 1.1 copy.67
  599.3 0.0 copy-done.6
  599.3 0.6 copy.68
  599.9 0.0 copy-done.2
  599.9 0.0 copy-start.1
  599.9 1.7 copy.69
  601.6 1.4 copy-done.1
  602.9 0.0 copy-start
  602.9 1.7 copy.70
  604.6 1.4 copy-done
  606.0 1.7 copy.71
  (5 shorter events, 0.1 us)
Async XLA Ops:
  6.5 14.3 %copy-start.5 = (s32[1024]{0:T(1024)}, s32[1024]{0:T(1024)S(1)}, u32[]{:S(2)}) copy-start(s32[1024]{0:T(1024)S(1)} %convert_reduce_fusion.3) | copy-start | bytes 12292
  17.0 3.8 copy-start.4
  19.4 220.1 %copy-start.7 = (s32[16]{0:T(128)}, s32[16]{0:T(128)S(1)}, u32[]{:S(2)}) copy-start(s32[16]{0:T(128)S(1)} %convert_reduce_fusion.2.counts) | copy-start | bytes 196
  590.2 7.9 %copy-start.3 = (f32[256,1536]{1,0:T(8,128)S(1)}, f32[256,1536]{1,0:T(8,128)}, u32[]{:S(2)}) copy-start(f32[256,1536]{1,0:T(8,128)} %get-tuple-element.83) | copy-start | bytes 4718596
  595.4 4.0 copy-start.6
  595.4 4.6 copy-start.2
  599.9 3.0 copy-start.1
  602.9 3.0 copy-start

commit v5 on v4

--- a/solution.py
+++ b/solution.py
@@ -61,16 +61,16 @@
     gate = jnp.where(valid, gate_all[span, :], 0.0)
     x = x_all[span, :]
     grad_rows = grad_all[span, :]
-    gate_part = mm(x, gate_w[0])
-    up_part = mm(x, up_w[0])
+    gate_part = mm(x, gate_w[...])
+    up_part = mm(x, up_w[...])
     sigma = jax.nn.sigmoid(gate_part)
     hidden = (gate_part * sigma * up_part).astype(low)
-    each = mm(hidden, down_w[0])
+    each = mm(hidden, down_w[...])
     grad_rows_wide = grad_rows.astype(jnp.float32)
     dots[span, :] = jnp.sum(grad_rows_wide * each, axis=1, keepdims=True)
     grad_each = (grad_rows_wide * gate).astype(low)
     grad_all[span, :] = jnp.where(valid, (each * gate).astype(low), grad_rows)
-    grad_hidden = mm(grad_each, down_w[0], NT)
+    grad_hidden = mm(grad_each, down_w[...], NT)
     grad_gate = (grad_hidden * up_part * sigma * (1.0 + gate_part * (1.0 - sigma))).astype(low)
     grad_up = (grad_hidden * gate_part * sigma).astype(low)
     down_grad = mm(hidden, grad_each, TN).astype(low)
@@ -85,14 +85,29 @@
                 ]
     gate_out[0] = mm(x, grad_gate, TN).astype(low)
     up_out[0] = mm(x, grad_up, TN).astype(low)
-    back_rows = mm(grad_gate, gate_w[0], NT) + mm(grad_up, up_w[0], NT)
+    back_rows = mm(grad_gate, gate_w[...], NT) + mm(grad_up, up_w[...], NT)
     x_all[span, :] = jnp.where(valid, back_rows.astype(low), x)
 
 
 def expert_kernel(counts, starts, code, base, router, second, grad, gate_w, up_w, down_w,
                   mixed_out, back_out, gate_out, up_out, down_out, router_out,
-                  slot, gates, x_all, grad_all, gate_all, dots):
+                  slot, gates, x_all, grad_all, gate_all, dots, gate_held, up_held, down_held, load_sem):
     e = pl.program_id(0)
+    depth = gate_held.shape[0]
+
+    def load(expert):
+        place = lax.rem(expert, depth)
+        return [
+            pltpu.make_async_copy(source.at[expert], held.at[place], load_sem.at[place, number])
+            for number, (source, held) in enumerate(((gate_w, gate_held), (up_w, up_held), (down_w, down_held)))
+        ]
+
+    @pl.when(e == 0)
+    def _():
+        for expert in range(depth):
+            for copy in load(expert):
+                copy.start()
+
     rows = second.shape[0]
     low = jnp.bfloat16
     tile = CAP
@@ -132,7 +147,10 @@
         grad_all[tiles * tile :, :] = jnp.zeros((tile, D), low)
         gate_all[tiles * tile :, :] = jnp.zeros((tile, 1), jnp.float32)
 
-    refs = (x_all, grad_all, gate_all, dots, gate_w, up_w, down_w, gate_out, up_out, down_out)
+    held = [ref.at[lax.rem(e, depth)] for ref in (gate_held, up_held, down_held)]
+    refs = (x_all, grad_all, gate_all, dots, *held, gate_out, up_out, down_out)
+    for copy in load(e):
+        copy.wait()
     count = counts[e]
     start = pl.multiple_of(starts[e], 16)
     widths = (CAP // 2, CAP)
@@ -141,6 +159,11 @@
         @pl.when((count > less) & (count <= width))
         def _(width=width):
             expert_step(width, start, count, refs)
+
+    @pl.when(e + depth < E)
+    def _():
+        for copy in load(e + depth):
+            copy.start()
 
     @pl.when(e == E - 1)
     def _():
@@ -187,9 +210,9 @@
     whole = lambda e, *_: (0, 0)
     by_expert = lambda e, *_: (e, 0, 0)
     wide = pl.BlockSpec((1, D, hidden), by_expert)
-    tall = pl.BlockSpec((1, hidden, D), by_expert)
+    depth = 4
     block = pl.BlockSpec((rows, D), whole, pipeline_mode=pl.Buffered(1))
-    out = pl.BlockSpec((rows, D), whole)
+    out = pl.BlockSpec((rows, D), whole, pipeline_mode=pl.Buffered(1))
     return pl.pallas_call(
         expert_kernel,
         grid_spec=pltpu.PrefetchScalarGridSpec(
@@ -201,9 +224,7 @@
                 pl.BlockSpec((E, D), whole),
                 block,
                 block,
-                wide,
-                wide,
-                tall,
+                *[pl.BlockSpec(memory_space=pl.ANY)] * 3,
             ],
             out_specs=[
                 out,
@@ -220,6 +241,10 @@
                 pltpu.VMEM((packed, D), low),
                 pltpu.VMEM((packed, 1), jnp.float32),
                 pltpu.VMEM((packed, 1), jnp.float32),
+                pltpu.VMEM((depth, D, hidden), low),
+                pltpu.VMEM((depth, D, hidden), low),
+                pltpu.VMEM((depth, hidden, D), low),
+                pltpu.SemaphoreType.DMA((depth, 3)),
             ],
         ),
         out_shape=[
@@ -544,16 +569,22 @@
     for chunk in range(2):
         gather.begin(chunk)
     values = tokens[...]
-    first[place] = (values * scale_of(values) * attn_gain[...]).astype(low)
+    first[place] = (values * scale_of(values) * attn_gain[...][None, :]).astype(low)
     lines = [LineGather(parts, CUTS, held, line_out.at[n], line_in.at[n]) for n, held in enumerate((first, grad, second))]
     for chunk in range(CUTS):
         lines[0].begin(chunk)
     sort = sorting(home[...], shard)
     sorted_grad[...] = mm(sort, out_grad[...].astype(low)).astype(sorted_grad.dtype)
-    for event in gather.events():
-        event()
     deal_grad = Exchange(groups, sorted_grad, dealt_grad, deal_out.at[0], deal_in.at[0])
     deal_grad.begin()
+    events = gather.events()
+    for event in events[: 2 * gather.bits]:
+        event()
+    for chunk in range(CUTS):
+        for way in (0, 1):
+            lines[0].step(1, way, chunk)
+    for event in events[2 * gather.bits :]:
+        event()
     gather.finish()
 
     count = gate_in.shape[0] // 4
@@ -580,7 +611,8 @@
         return copy, held
 
     loaded = [load(0)]
-    for chunk in range(moe.chunks):
+
+    def cast(chunk):
         if chunk + 1 < moe.chunks:
             loaded.append(load(chunk + 1))
         copy, held = loaded[chunk]
@@ -593,7 +625,9 @@
 
         lax.fori_loop(0, held.shape[0], row, 0)
         moe.begin(chunk)
+
     events = moe.events()
+    cast(0)
     save(0, weights.at[:, : weights_out.shape[1]], weights_out)
     router = weights[:, weights_out.shape[1] :].astype(jnp.float32)
     router_out[...] = jnp.transpose(router)[:E, :].astype(low)
@@ -604,18 +638,26 @@
         for head in range(heads + 2 * heads_kv):
             qkv[head, span, :] = result[:, head * HD : (head + 1) * HD].astype(low)
 
-    project(place)
-    for distance in range(1, parts):
-        if distance == parts - 1:
+    turns = [(distance, chunk) for distance in range(2, parts) for chunk in range(CUTS)]
+    done = 1
+    for number, (distance, chunk) in enumerate(turns):
+        if distance == parts - 1 and chunk == 0:
             deal_grad.arrive()
             grad[place] = dealt_grad[...].astype(low)
-            for chunk in range(CUTS):
-                lines[1].begin(chunk)
-        for chunk in range(CUTS):
+            for piece in range(CUTS):
+                lines[1].begin(piece)
+        for way in (0, 1):
+            lines[0].step(distance, way, chunk)
+        while done < moe.chunks and done * len(turns) <= (number + 1) * moe.chunks:
+            cast(done)
+            done += 1
+        if number == 0:
+            project(place)
+        if chunk == CUTS - 1:
             for way in (0, 1):
-                lines[0].step(distance, way, chunk)
-        for way in (0, 1):
-            lines[0].from_side(distance, way, project)
+                lines[0].from_side(distance - 1, way, project)
+    for way in (0, 1):
+        lines[0].from_side(parts - 1, way, project)
     save(1, first, first_out)
     save(2, qkv, qkv_out)
 
@@ -651,15 +693,13 @@
         sums.total(chunk, middle)
     values = tokens[...] + middle[...]
     middle[...] = values
-    normed = (values * scale_of(values) * moe_gain[...]).astype(low)
+    normed = (values * scale_of(values) * moe_gain[...][None, :]).astype(low)
     sorted_second[...] = mm(sort, normed).astype(sorted_second.dtype)
     deal = Exchange(groups, sorted_second, dealt_second, deal_out.at[1], deal_in.at[1])
-    for event in events[:4]:
-        event()
     deal.begin()
     save(4, grad, grad_out)
     singles = moe.bits * moe.chunks
-    for event in events[4:singles]:
+    for event in events[:singles]:
         event()
     deal.arrive()
     second[place] = dealt_second[...].astype(low)
@@ -746,7 +786,7 @@
         cost_estimate=pl.CostEstimate(
             flops=12 * rows * width * columns, bytes_accessed=60 * 2**20, transcendentals=rows * rows * heads
         ),
-    )(home, seg[None, :], seg[:, None], attn_gain[None, :], moe_gain[None, :], tokens, out_grad, wpack,
+    )(home, seg[None, :], seg[:, None], attn_gain, moe_gain, tokens, out_grad, wpack,
       w_gate, w_up, w_down)
 
 
@@ -874,6 +914,9 @@
             target = self.totals.at[place]
 
         def row(index, _):
+            if count == 2:
+                target[index] = self.terms[slot, 0, index] + self.terms[slot, 1, index]
+                return 0
             total = self.terms[slot, 0, index].astype(jnp.float32)
             for term in range(1, count):
                 total = total + self.terms[slot, term, index].astype(jnp.float32)
@@ -1000,6 +1043,9 @@
     deal = Exchange(groups, stage, land_back, deal_out.at[0], deal_in.at[0])
     deal.begin()
     back.finish()
+    loads[4].wait()
+    extra = LineSum(parts, CUTS, mixed, mixed_come, sum_out.at[1], sum_in.at[1])
+    extra.begin(extra.turned(order[0]))
     router_line[place] = routers.total()
     router_sums = Share("mp", parts, router_line, share_out.at[1], share_in.at[1], lambda peer: router_line.at[place])
     for turn in range(1, parts):
@@ -1009,7 +1055,7 @@
     scale = scale_of(values)
     deal.arrive()
     grad_second = mm(sort, land_back[...].astype(low), TN)
-    weighted = grad_second * moe_gain[...]
+    weighted = grad_second * moe_gain[...][None, :]
     inner = jnp.mean(weighted * values, axis=1, keepdims=True)
     gains[0:1, :] = jnp.sum(grad_second * values * scale, axis=0, keepdims=True)
     grad_middle = out_grad[...] + (scale * weighted - values * (scale * scale * scale * inner))
@@ -1018,9 +1064,7 @@
     line = LineGather(parts, CUTS, grad, line_out, line_in)
     for chunk in range(CUTS):
         line.begin(chunk)
-    loads[4].wait()
-    extra = LineSum(parts, CUTS, mixed, mixed_come, sum_out.at[1], sum_in.at[1])
-    for target in order:
+    for target in order[1:]:
         extra.begin(extra.turned(target))
     loads[1].wait()
 
@@ -1036,6 +1080,8 @@
         for chunk in range(CUTS):
             for way in (0, 1):
                 line.step(distance, way, chunk)
+            if distance == parts - 1:
+                extra.relay(extra.turned(order[0]), chunk)
             stream.tick()
         for way in (0, 1):
             line.from_side(distance, way, mix_back)
@@ -1074,15 +1120,16 @@
         held[target] = mm(flat[start:stop, :], weights[:, : slots * HD], NT).astype(low)
         first_sum.begin(target)
         for chunk in range(CUTS):
-            extra.relay(extra.turned(order[number]), chunk)
-            if number > 0:
-                first_sum.relay(target + 1, chunk)
+            if number < parts - 1:
+                extra.relay(extra.turned(order[number + 1]), chunk)
             stream.tick(1)
+    for target in reversed(range(parts)):
+        for chunk in range(CUTS):
+            first_sum.relay(target, chunk)
     loads[2].wait()
     mix_flat = jnp.concatenate([mix[head] for head in range(heads)], axis=1)
     pack[:, slots * HD :] = mm(grad[...].reshape(parts * shard, width), mix_flat, TN).astype(low)
     for chunk in range(CUTS):
-        first_sum.relay(0, chunk)
         extra.total(chunk, block_out)
         stream.tick()
     deal.finish()
@@ -1130,7 +1177,7 @@
     grad_first = block_out[...]
     values = tokens[...]
     scale = scale_of(values)
-    weighted = grad_first * attn_gain[...]
+    weighted = grad_first * attn_gain[...][None, :]
     inner = jnp.mean(weighted * values, axis=1, keepdims=True)
     gains[1:2, :] = jnp.sum(grad_first * values * scale, axis=0, keepdims=True)
     gains_lines = Share("mp", parts, gains_line, share_out.at[2], share_in.at[2], lambda peer: gains)
@@ -1236,7 +1283,7 @@
         cost_estimate=pl.CostEstimate(
             flops=24 * rows * width * columns, bytes_accessed=200 * 2**20, transcendentals=rows * rows * heads
         ),
-    )(home, seg[None, :], seg[:, None], attn_gain[None, :], moe_gain[None, :], tokens, out_grad, middle, router_part,
+    )(home, seg[None, :], seg[:, None], attn_gain, moe_gain, tokens, out_grad, middle, router_part,
       back, mixed, first, qkv, mix, weights, gate_grad, up_grad, down_grad)
 
 

time: 616 us -> 595 us (0.966)
  Pallas kernels: 569 us -> 554 us
    pallas_call x1, Pallas kernels: 219 us -> 205 us  [forward(): pl.pallas_call(functools.partial(forward_kernel, groups, parts, heads, he...]
where the time goes in v5:
time: 595 us; the launch traced here: 590 us
  Pallas kernels  554 us (93%)
  local copies, waits for them, and re-layouts  19.8 us (3%)
  other arithmetic  15 us (3%)
    pallas_call x1, Pallas kernels, backward(): pl.pallas_call(functools.partial(backward_kernel, groups, parts, heads, h...  266 us
    pallas_call x1, Pallas kernels, forward(): pl.pallas_call(functools.partial(forward_kernel, groups, parts, heads, he...  205 us
    pallas_call x1, Pallas kernels, experts(): pl.pallas_call(expert_kernel, grid_spec=pltpu.PrefetchScalarGridSpec(num_...  82.2 us
    unnamed x23, local copies, waits for them, and re-layouts  13.2 us

profile of v5, /device:TPU:0, one launch (start us, length us, event | category | flops | bytes accessed | tf_op | source)
XLA Modules:
  0.0 589.5 jit_solution(4016756809602442172)
XLA Ops:
  0.7 0.8 reduce-window.13
  1.5 4.3 select_reduce_fusion
  5.8 0.7 convert_reduce_fusion.1
  6.4 0.1 convert_reduce_fusion.3
  6.5 0.0 copy-start.5
  6.5 0.7 fusion.7
  7.2 0.5 convert_reduce_fusion
  7.7 0.8 slice_add_fusion
  8.5 1.3 select_reduce_fusion.1
  9.8 0.7 convert.22
  10.5 0.1 copy.48
  10.6 1.0 convert_dynamic-update-slice_fusion
  11.6 0.9 convert_dynamic-update-slice_fusion.2
  12.5 0.9 convert_dynamic-update-slice_fusion.1
  13.4 1.0 bitcast_dynamic-update-slice_fusion
  14.5 0.0 copy-start.4
  14.5 1.0 copy.55.seg_col
  15.5 0.9 copy.50
  16.4 0.3 eq.46
  16.7 0.1 convert_reduce_fusion.2.counts
  16.8 0.0 copy-start.7
  16.8 0.1 copy.51
  17.0 0.7 subtract_convert_fusion
  17.7 0.5 multiply_subtract_fusion.starts
  18.2 0.0 copy-done.5
  18.2 0.0 copy-done.4
  18.2 205.3 %shard_map.238 = (f32[256,1536]{1,0:T(8,128)}, bf16[16,1536]{1,0:T(8,128)(2,1)}, bf16[4,256,1536]{2,1,0:T(8,128)(2,1)}, bf16[10,1024,64]{2,1,0:T(8,128)(2,1)}, b...) custom-call(s32[1,256]{1,0:T(1,128)} %bitcast.24, ...), custom_call_target="tpu_custom_call" | custom-call | flops 21743271936 | bytes 62914560 | tf_op jit(solution)/shard_map/pallas_call | solution.py:739
  223.6 0.0 copy-done.7
  223.6 82.2 %shard_map.239 = (bf16[1024,1536]{1,0:T(8,128)(2,1)}, bf16[1024,1536]{1,0:T(8,128)(2,1)}, bf16[16,1536,256]{2,1,0:T(8,128)(2,1)}, bf16[16,1536,256]{2,1,0:T(8,12...) custom-call(s32[16]{0:T(128)} %copy-done.7, s32[16]{0:T(128)} %multiply_subtract_fusion.starts, ...), custom_call_target="tpu_custom_call" | custom-call | flops 40265318400 | bytes 88080384 | tf_op jit(solution)/shard_map/pallas_call | solution.py:216
  305.8 266.1 %shard_map.240 = (f32[256,1536]{1,0:T(8,128)}, f32[256,1536]{1,0:T(8,128)}, f32[8,1536]{1,0:T(8,128)}, f32[16,192]{1,0:T(8,128)}, f32[192,1024]{1,0:T(8,128)}, /...) custom-call(s32[1,256]{1,0:T(1,128)} %bitcast.25, ...), custom_call_target="tpu_custom_call" | custom-call | flops 38654705664 | bytes 209715200 | tf_op jit(solution)/shard_map/pallas_call | solution.py:1221
  571.9 0.0 copy-start.3
  571.9 1.6 slice_reduce_fusion
  573.5 1.6 fusion.11
  575.1 1.9 slice_bitcast_fusion
  577.0 0.0 copy-start.6
  577.0 0.0 copy-start.2
  577.0 2.8 copy.66
  579.8 0.0 copy-done.3
  579.8 1.1 copy.67
  580.9 0.0 copy-done.6
  580.9 0.6 copy.68
  581.5 0.0 copy-done.2
  581.6 0.0 copy-start.1
  581.6 1.7 copy.69
  583.2 1.4 copy-done.1
  584.6 0.0 copy-start
  584.6 1.7 copy.70
  586.2 1.4 copy-done
  587.6 1.7 copy.71
  (5 shorter events, 0.1 us)
Async XLA Ops:
  6.5 11.7 %copy-start.5 = (s32[1024]{0:T(1024)}, s32[1024]{0:T(1024)S(1)}, u32[]{:S(2)}) copy-start(s32[1024]{0:T(1024)S(1)} %convert_reduce_fusion.3) | copy-start | bytes 12292
  14.5 3.8 copy-start.4
  16.8 206.8 %copy-start.7 = (s32[16]{0:T(128)}, s32[16]{0:T(128)S(1)}, u32[]{:S(2)}) copy-start(s32[16]{0:T(128)S(1)} %convert_reduce_fusion.2.counts) | copy-start | bytes 196
  571.9 7.9 %copy-start.3 = (f32[256,1536]{1,0:T(8,128)S(1)}, f32[256,1536]{1,0:T(8,128)}, u32[]{:S(2)}) copy-start(f32[256,1536]{1,0:T(8,128)} %get-tuple-element.83) | copy-start | bytes 4718596
  577.0 4.0 copy-start.6
  577.0 4.6 copy-start.2
  581.6 3.0 copy-start.1
  584.6 3.0 copy-start

commit v6 on v5

--- a/solution.py
+++ b/solution.py
@@ -1126,6 +1126,7 @@
     for target in reversed(range(parts)):
         for chunk in range(CUTS):
             first_sum.relay(target, chunk)
+        stream.tick(2)
     loads[2].wait()
     mix_flat = jnp.concatenate([mix[head] for head in range(heads)], axis=1)
     pack[:, slots * HD :] = mm(grad[...].reshape(parts * shard, width), mix_flat, TN).astype(low)

time: 595 us -> 592 us (level)
  no operation moved by 1% of the time
where the time goes in v6:
time: 592 us; the launch traced here: 585 us
  Pallas kernels  549 us (93%)
  local copies, waits for them, and re-layouts  19.8 us (3%)
  other arithmetic  15 us (3%)
    pallas_call x1, Pallas kernels, backward(): pl.pallas_call(functools.partial(backward_kernel, groups, parts, heads, h...  262 us
    pallas_call x1, Pallas kernels, forward(): pl.pallas_call(functools.partial(forward_kernel, groups, parts, heads, he...  205 us
    pallas_call x1, Pallas kernels, experts(): pl.pallas_call(expert_kernel, grid_spec=pltpu.PrefetchScalarGridSpec(num_...  82.2 us
    unnamed x23, local copies, waits for them, and re-layouts  13.2 us

profile of v6, /device:TPU:0, one launch (start us, length us, event | category | flops | bytes accessed | tf_op | source)
XLA Modules:
  0.0 585.4 jit_solution(14785431966368432066)
XLA Ops:
  0.7 0.8 reduce-window.13
  1.5 4.3 select_reduce_fusion
  5.8 0.7 convert_reduce_fusion.1
  6.4 0.1 convert_reduce_fusion.3
  6.5 0.0 copy-start.5
  6.5 0.7 fusion.7
  7.2 0.5 convert_reduce_fusion
  7.7 0.8 slice_add_fusion
  8.5 1.3 select_reduce_fusion.1
  9.8 0.7 convert.22
  10.5 0.1 copy.48
  10.6 1.0 convert_dynamic-update-slice_fusion
  11.6 0.9 convert_dynamic-update-slice_fusion.2
  12.5 0.9 convert_dynamic-update-slice_fusion.1
  13.4 1.0 bitcast_dynamic-update-slice_fusion
  14.5 0.0 copy-start.4
  14.5 1.0 copy.55.seg_col
  15.5 0.9 copy.50
  16.4 0.3 eq.46
  16.7 0.1 convert_reduce_fusion.2.counts
  16.8 0.0 copy-start.7
  16.8 0.1 copy.51
  17.0 0.7 subtract_convert_fusion
  17.7 0.5 multiply_subtract_fusion.starts
  18.2 0.0 copy-done.5
  18.2 0.0 copy-done.4
  18.2 205.3 %shard_map.238 = (f32[256,1536]{1,0:T(8,128)}, bf16[16,1536]{1,0:T(8,128)(2,1)}, bf16[4,256,1536]{2,1,0:T(8,128)(2,1)}, bf16[10,1024,64]{2,1,0:T(8,128)(2,1)}, b...) custom-call(s32[1,256]{1,0:T(1,128)} %bitcast.24, ...), custom_call_target="tpu_custom_call" | custom-call | flops 21743271936 | bytes 62914560 | tf_op jit(solution)/shard_map/pallas_call | solution.py:739
  223.6 0.0 copy-done.7
  223.6 82.2 %shard_map.239 = (bf16[1024,1536]{1,0:T(8,128)(2,1)}, bf16[1024,1536]{1,0:T(8,128)(2,1)}, bf16[16,1536,256]{2,1,0:T(8,128)(2,1)}, bf16[16,1536,256]{2,1,0:T(8,12...) custom-call(s32[16]{0:T(128)} %copy-done.7, s32[16]{0:T(128)} %multiply_subtract_fusion.starts, ...), custom_call_target="tpu_custom_call" | custom-call | flops 40265318400 | bytes 88080384 | tf_op jit(solution)/shard_map/pallas_call | solution.py:216
  305.7 262.0 %shard_map.240 = (f32[256,1536]{1,0:T(8,128)}, f32[256,1536]{1,0:T(8,128)}, f32[8,1536]{1,0:T(8,128)}, f32[16,192]{1,0:T(8,128)}, f32[192,1024]{1,0:T(8,128)}, /...) custom-call(s32[1,256]{1,0:T(1,128)} %bitcast.25, ...), custom_call_target="tpu_custom_call" | custom-call | flops 38654705664 | bytes 209715200 | tf_op jit(solution)/shard_map/pallas_call | solution.py:1222
  567.7 0.0 copy-start.3
  567.7 1.6 slice_reduce_fusion
  569.3 1.6 fusion.11
  570.9 1.9 slice_bitcast_fusion
  572.8 0.0 copy-start.6
  572.8 0.0 copy-start.2
  572.8 2.8 copy.66
  575.6 0.0 copy-done.3
  575.6 1.1 copy.67
  576.8 0.0 copy-done.6
  576.8 0.6 copy.68
  577.4 0.0 copy-done.2
  577.4 0.0 copy-start.1
  577.4 1.7 copy.69
  579.1 1.4 copy-done.1
  580.4 0.0 copy-start
  580.4 1.7 copy.70
  582.1 1.4 copy-done
  583.4 1.7 copy.71
  (5 shorter events, 0.1 us)
Async XLA Ops:
  6.5 11.7 %copy-start.5 = (s32[1024]{0:T(1024)}, s32[1024]{0:T(1024)S(1)}, u32[]{:S(2)}) copy-start(s32[1024]{0:T(1024)S(1)} %convert_reduce_fusion.3) | copy-start | bytes 12292
  14.5 3.8 copy-start.4
  16.8 206.8 %copy-start.7 = (s32[16]{0:T(128)}, s32[16]{0:T(128)S(1)}, u32[]{:S(2)}) copy-start(s32[16]{0:T(128)S(1)} %convert_reduce_fusion.2.counts) | copy-start | bytes 196
  567.7 7.9 %copy-start.3 = (f32[256,1536]{1,0:T(8,128)S(1)}, f32[256,1536]{1,0:T(8,128)}, u32[]{:S(2)}) copy-start(f32[256,1536]{1,0:T(8,128)} %get-tuple-element.83) | copy-start | bytes 4718596
  572.8 4.0 copy-start.6
  572.8 4.6 copy-start.2
  577.4 3.0 copy-start.1
  580.4 3.0 copy-start
